TPU v7x, 256 devices: a whole 4x4x8 slice. The times are simulated.
256 devices in a mesh: pair: 8 (over z_lo, core), vocab: 32 (over x, y, z_hi).
Axes of the slice: x: 4, y: 4, z: 8 (z_hi: 2, z_lo: 4; z = z_hi * 4 + z_lo), core: 2. Of those that a mesh axis runs over, the one named last changes fastest.
Arguments:
- teacher_logits: bfloat16 [1024, 65536], P('pair', 'vocab'), may hold values from -20 to 260
- student_hidden: bfloat16 [1024, 4096], P('pair', 'vocab'), may hold values from -200 to 200
- head_weight: bfloat16 [4096, 65536], P('pair', 'vocab'), may hold values from -0.4 to 0.4
- head_bias: float32 [65536], P('vocab'), may hold values from -2.5 to 3.2
- pairing: int32 [8], replicated, may hold values from 0 to 7, as said below
- targets: int32 [1024], P('pair'), may hold values from 0 to 65535
Outputs:
- hidden_grad: bfloat16 [4096, 1024], P(('pair', 'vocab'))
- row_loss: float32 [1024], P('pair')
Inputs may be any that keep to these rules, and one draw needn't show every extreme that they name: `pairing`: a permutation of the 8 groups.
All inputs are finite; a program needn't handle non-finite values.
Results may differ from a plain program's by a relative error of at most 0.0034.
Values may be sent and summed in bfloat16 or wider, within the bound.
No kernel may reach another device: no remote copies, remote signals or barrier semaphores. Data moves between devices by JAX's collectives and lax.ppermute only.
A program may use at most 128 MiB of HBM per device.

v0:
```python
import jax
import jax.numpy as jnp
from jax import lax
from jax.sharding import PartitionSpec as P


def split_lse(values):
    row_peak = lax.pmax(jnp.max(values, axis=1), "vocab")
    row_total = lax.psum(jnp.sum(jnp.exp(values - row_peak[:, None]), axis=1), "vocab")
    return row_peak + jnp.log(row_total)


def pick_rows(first_row, carry, pieces):
    row_count = carry[0].shape[0]
    piece_rows = pieces[0].shape[0]
    row_index = first_row + jnp.arange(row_count, dtype=jnp.int32)
    inside = (row_index >= 0) & (row_index < piece_rows)
    safe_index = jnp.clip(row_index, 0, piece_rows - 1)
    return tuple(
        (
            jnp.where(
                inside.reshape((row_count,) + (1,) * (member.ndim - 1)),
                jnp.take(member, safe_index, axis=0),
                kept,
            )
            for member, kept in zip(pieces, carry)
        )
    )


def receive(teacher, teacher_lse, first_row):
    row_count, vocab_cols = teacher.shape
    teacher_prob = jnp.exp(teacher - teacher_lse[:, None])
    empty = (jnp.zeros((row_count, vocab_cols), jnp.float32),)
    (target_prob,) = pick_rows(
        first_row, empty, (lax.all_gather(teacher_prob, "pair", axis=0, tiled=True),)
    )
    log_target = jnp.log(jnp.maximum(target_prob, jnp.finfo(jnp.float32).tiny))
    return (log_target, target_prob)


def per_device(teacher_logits, student_hidden, head_weight, head_bias, pairing, targets):
    row_count, vocab_cols = teacher_logits.shape
    groups = lax.axis_size("pair")
    shards = lax.axis_size("vocab")
    own_group = lax.axis_index("pair")
    source = jnp.sum(jnp.arange(groups, dtype=jnp.int32) * (pairing == own_group).astype(jnp.int32))
    first_row = source * row_count
    teacher = teacher_logits.astype(jnp.float32)
    full_weight = lax.all_gather(head_weight, "pair", axis=0, tiled=True)
    teacher_lse = split_lse(teacher)
    log_target, target_prob = receive(teacher, teacher_lse, first_row)
    weight_block = full_weight
    summed = jnp.dot(
        lax.all_gather(student_hidden, "vocab", axis=1, tiled=True),
        weight_block,
        preferred_element_type=jnp.float32,
    )
    logits = summed + head_bias[None, :]
    student_lse = split_lse(logits)
    log_student = logits - student_lse[:, None]
    student_prob = jnp.exp(log_student)
    local_ids = targets - lax.axis_index("vocab") * vocab_cols
    onehot = local_ids[:, None] == jnp.arange(vocab_cols, dtype=jnp.int32)[None, :]
    diverge_terms = jnp.where(target_prob > 0.0, target_prob * (log_target - log_student), 0.0)
    diverge_part = jnp.sum(diverge_terms, axis=1)
    target_part = jnp.sum(jnp.where(onehot, logits, 0.0), axis=1)
    diverge_sum, target_sum = lax.psum((diverge_part, target_part), "vocab")
    row_loss = diverge_sum + student_lse - target_sum
    grad_logits = (2.0 * student_prob - target_prob - onehot.astype(jnp.float32)).astype(
        jnp.bfloat16
    )
    part_rows = full_weight.shape[0] // (groups * shards)
    share_rows = groups * part_rows
    layered = full_weight.reshape(groups, shards, part_rows, vocab_cols)
    weight_block = layered
    weight_block = jnp.transpose(weight_block, (1, 0, 2, 3)).reshape(
        share_rows * lax.axis_size("vocab"), vocab_cols
    )
    summed_grad = lax.psum_scatter(
        lax.dot_general(
            weight_block, grad_logits, (((1,), (1,)), ((), ())), preferred_element_type=jnp.float32
        ),
        "vocab",
        scatter_dimension=0,
        tiled=True,
    )
    hidden_grad = lax.all_to_all(
        summed_grad.astype(jnp.bfloat16), "pair", split_axis=0, concat_axis=1, tiled=True
    )
    return (hidden_grad, row_loss)


def solution(mesh):
    return jax.shard_map(
        per_device,
        mesh=mesh,
        in_specs=(
            P("pair", "vocab"),
            P("pair", "vocab"),
            P("pair", "vocab"),
            P("vocab"),
            P(),
            P("pair"),
        ),
        out_specs=(P(("pair", "vocab"), None), P("pair")),
        check_vma=False,
    )
```

profile of v0, /device:TPU:32, one launch (start us, length us, event | category | flops | bytes accessed | tf_op | source)
XLA Modules:
  0.0 860.2 jit_solution(13503116486281129379)
XLA Ops:
  7.2 0.0 copy-start
  7.2 0.0 all-gather.4.cloned.1.call-start
  7.2 0.7 all-gather.4.cloned.1.call-update
  7.9 0.0 all-gather.6.cloned.1.call-start
  8.0 0.7 all-gather.6.cloned.1.call-update
  8.7 0.0 all-gather.8.cloned.1.call-start
  8.7 1.2 reduce_max.24
  9.9 86.8 %all-gather.4.cloned.1.call-done = bf16[128,4096]{1,0:T(8,128)(2,1)} async-done(((bf16[128,128]{1,0:T(8,128)(2,1)}), bf16[128,4096]{1,0:T(8,128)(2,1)}) %all-gather.4.cloned.1.call-update) | async-done | bytes 1048592 | tf_op jit(solution)/shard_map/all_gather | solution.py:55
  96.7 167.2 %all-gather.6.cloned.1.call-done = bf16[4096,2048]{1,0:T(8,128)(2,1)} async-done(((bf16[512,2048]{1,0:T(8,128)(2,1)}), bf16[4096,2048]{1,0:T(8,128)(2,1)}) %all-gather.6.cloned.1.call-update) | async-done | bytes 16777232 | tf_op jit(solution)/shard_map/all_gather | solution.py:50
  263.9 8.4 fusion.15
  272.3 120.6 %all-reduce.2 = (f32[128]{0:T(128)S(1)}, f32[128]{0:T(128)S(1)}) all-reduce(bf16[128]{0:T(256)(128)(2,1)S(1)} %reduce_max.24, f32[128]{0:T(128)S(1)} %get-tuple-element.10), channel_id=1, replica_groups=mesh['pair'=8,'vocab'=32] {'vocab'}, use_global_device_ids=true, to_apply=%region_6.7 | all-reduce | flops 256 | bytes 1792 | tf_op jit(solution)/shard_map/pmax | solution.py:8
  393.0 0.5 fusion.1
  393.4 108.4 %all-reduce.1 = (f32[128]{0:T(128)S(1)}, f32[128]{0:T(128)S(1)}) all-reduce(f32[128]{0:T(128)S(1)} %get-tuple-element.12, f32[128]{0:T(128)S(1)} %get-tuple-element.13), channel_id=1, replica_groups=mesh['pair'=8,'vocab'=32] {'vocab'}, use_global_device_ids=true, to_apply=%region_8.9 | all-reduce | flops 256 | bytes 2048 | tf_op jit(solution)/shard_map/psum | solution.py:9
  501.8 1.2 fusion.2
  503.0 0.0 all-gather.8.cloned.1.call-update
  503.1 0.0 reduce-scatter.2.cloned.1.call-start
  503.1 0.0 copy-done.1
  503.1 0.6 fusion.10
  504.5 14.2 %copy.10 = bf16[32,8,16,2048]{3,2,1,0:T(8,128)(2,1)} copy(bf16[32,8,16,2048]{3,2,0,1:T(8,128)(2,1)} %bitcast.18) | data formatting | bytes 33554432 | tf_op jit(solution)/shard_map/transpose | solution.py:77
  518.7 71.8 %all-gather.8.cloned.1.call-done = f32[1024,2048]{1,0:T(8,128)} async-done(((f32[128,2048]{1,0:T(8,128)}), f32[1024,2048]{1,0:T(8,128)}) %all-gather.8.cloned.1.call-update) | async-done | bytes 8388624 | tf_op jit(solution)/shard_map/all_gather | solution.py:36
  590.6 4.8 gather_fusion
  595.4 13.1 %convolution_bitcast_fusion = f32[4096,128]{0,1:T(8,128)} fusion(bf16[4096,2048]{1,0:T(8,128)(2,1)} %bitcast.19, f32[128,2048]{1,0:T(8,128)S(1)} %get-tuple-element.11, f32[128,2048]{1,0:T(8,128)S(1)} %gather_fusion, s32[128]{0:T(128)S(1)} %broadcast_subtract_fusion, f32[128]{0:T(128)S(1)} %log_add_fusion.1, pred[128]{0:T(512)(128)(4,1)S(1)} %get-tuple-element.14, ...), kind=kOutput, calls=%fused_computation.1 | convolution fusion | flops 2149842944 | bytes 20972800 | tf_op jit(solution)/shard_map/dot_general | solution.py:81
  608.5 0.0 reduce-scatter.2.cloned.1.call-update
  608.5 0.7 select_reduce_fusion.1
  609.2 121.0 %all-reduce = (f32[128]{0:T(128)S(1)}, f32[128]{0:T(128)S(1)}) all-reduce(f32[128]{0:T(128)S(1)} %get-tuple-element.3, f32[128]{0:T(128)S(1)} %get-tuple-element.2), channel_id=1, replica_groups=mesh['pair'=8,'vocab'=32] {'vocab'}, use_global_device_ids=true, to_apply=%region_13.14 | all-reduce | flops 256 | bytes 2048 | tf_op jit(solution)/shard_map/psum | solution.py:68
  730.2 113.5 %reduce-scatter.2.cloned.1.call-done = f32[128,128]{0,1:T(8,128)} async-done(((f32[4096,128]{0,1:T(8,128)}), f32[128,128]{0,1:T(8,128)}) %reduce-scatter.2.cloned.1.call-update) | async-done | bytes 65552 | tf_op jit(solution)/shard_map/reduce_scatter | solution.py:80
  843.7 0.8 convert_element_type.16
  844.6 0.7 copy.11
  845.3 3.4 all-to-all-start
  848.7 0.5 add_subtract_fusion
  849.2 3.9 all-to-all-done
  853.1 0.6 copy_bitcast_fusion
  (10 shorter events, 0.1 us)
Async XLA Ops:
  7.2 385.8 %copy-start = (bf16[128,2048]{1,0:T(8,128)(2,1)S(1)}, bf16[128,2048]{1,0:T(8,128)(2,1)}, u32[]{:S(2)}) copy-start(bf16[128,2048]{1,0:T(8,128)(2,1)} %param.6) | copy-start | bytes 1572868
  7.2 496.0 %copy-start.1 = (s32[8]{0:T(128)S(1)}, s32[8]{0:T(128)}, u32[]{:S(2)}) copy-start(s32[8]{0:T(128)} %param.10) | copy-start | bytes 100
  7.2 497.3 %copy-start.2 = (s32[128]{0:T(128)S(1)}, s32[128]{0:T(128)}, u32[]{:S(2)}) copy-start(s32[128]{0:T(128)} %param.11) | copy-start | bytes 1540
  7.2 89.5 %all-gather.4.cloned.1.call-start = ((), (), s32[]{:S(2)}) async-start(), calls=%async_computation.2 | async-start | bytes 1081344 | tf_op jit(solution)/shard_map/all_gather | solution.py:55
  7.9 255.9 %all-gather.6.cloned.1.call-start = ((), (), s32[]{:S(2)}) async-start(), calls=%async_computation.3 | async-start | bytes 18874368 | tf_op jit(solution)/shard_map/all_gather | solution.py:50
  8.7 581.9 %all-gather.8.cloned.1.call-start = ((), (), s32[]{:S(2)}) async-start(), calls=%async_computation.4 | async-start | bytes 9437184 | tf_op jit(solution)/shard_map/all_gather | solution.py:36
  503.1 340.6 %reduce-scatter.2.cloned.1.call-start = ((), (), s32[]{:S(2)}) async-start(), calls=%async_computation.5 | async-start | bytes 2162688 | tf_op jit(solution)/shard_map/reduce_scatter | solution.py:80
  845.3 7.8 all-to-all-start
Sparse Core Ops, SparseCore 0:
  11.2 85.3 all-gather.3
  98.5 165.3 all-gather.5
  503.2 87.3 all-gather.7
  608.6 235.0 reduce-scatter.1
where the time goes:
time: 863 us; the launch traced here: 860 us
  waiting for transfers between devices  445 us (52%)
  blocking collectives  350 us (41%)
  matrix products  21.5 us (2%)
  local copies, waits for them, and re-layouts  20.4 us (2%)
  between operations  14.5 us (2%)
    all_gather x1, waiting for transfers between devices, per_device(): full_weight = lax.all_gather(head_weight, 'pair', axis=0, tiled=True)  167 us
    psum x1, blocking collectives, per_device(): diverge_sum, target_sum = lax.psum((diverge_part, target_part), 'vocab')  121 us
    pmax x1, blocking collectives, split_lse(): row_peak = lax.pmax(jnp.max(values, axis=1), 'vocab')  121 us
    reduce_scatter x1, waiting for transfers between devices, per_device(): lax.psum_scatter(lax.dot_general(weight_block, grad_logits, (((1,), (1,))...  114 us
    psum x1, blocking collectives, split_lse(): lax.psum(jnp.sum(jnp.exp(values - row_peak[:, None]), axis=1), 'vocab')  108 us
    all_gather x1, waiting for transfers between devices, per_device(): lax.all_gather(student_hidden, 'vocab', axis=1, tiled=True)  86.8 us
    all_gather x1, waiting for transfers between devices, receive(): lax.all_gather(teacher_prob, 'pair', axis=0, tiled=True)  71.8 us
  transfers between devices with their start and end apart: 5, of which 5 were waited for; matrix products, arithmetic and copies ran while one was open for 2% of the time, Pallas kernels for 0%

commit v1 on v0

v1 whole, which is shorter than its diff:
```python
import jax
import jax.numpy as jnp
from jax import lax
from jax.experimental import pallas as pl
from jax.experimental.pallas import tpu as pltpu
from jax.sharding import Mesh, PartitionSpec as P

AXES = {"zl": 4, "co": 2, "x": 4, "y": 4, "zh": 2}
VMEM_BYTES = 56 * 1024 * 1024
F32 = jnp.float32
BF16 = jnp.bfloat16


def swap(value, axis, flip):
    return lax.ppermute(value, axis, [(i, i ^ flip) for i in range(AXES[axis])])


def swaps(value, axis):
    return [value] + [swap(value, axis, j) for j in range(1, AXES[axis])]


def add_all(parts):
    if len(parts) == 2:
        return parts[0] + parts[1]
    return (parts[0] + parts[1]) + (parts[2] + parts[3])


def in_order(parts, place):
    low = (place & 1) == 1
    if len(parts) == 2:
        return [jnp.where(low, parts[1], parts[0]), jnp.where(low, parts[0], parts[1])]
    high = (place & 2) == 2
    out = []
    for i in range(4):
        out.append(
            jnp.where(
                high,
                jnp.where(low, parts[i ^ 3], parts[i ^ 2]),
                jnp.where(low, parts[i ^ 1], parts[i]),
            )
        )
    return out


def join_stats(parts):
    peak = parts[0][:2]
    for part in parts[1:]:
        peak = jnp.maximum(peak, part[:2])
    total = add_all([part[2:] * jnp.exp(part[:2] - peak) for part in parts])
    return jnp.concatenate([peak, total], axis=0)


def logits_kernel(pos, *refs):
    own, other = refs[0:4], refs[4:8]
    first, second = refs[8:12], refs[12:16]
    bias, teacher_stat, logits, stat, x_buf, w_buf, sems = refs[16:]
    x, y, z, core = pos[0], pos[1], pos[2], pos[3]
    depth = own[0].shape[0]
    half, block = first[0].shape[1:]
    copies = []

    def copy(src, dst):
        made = pltpu.make_async_copy(src, dst, sems.at[len(copies)])
        made.start()
        copies.append(made)

    for j in range(4):
        for pieces, side in ((own, core), (other, 1 - core)):
            row = pl.multiple_of((2 * (z ^ j) + side) * depth, depth)
            copy(pieces[j], w_buf.at[pl.ds(row, depth), :])
    for j in range(4):
        for k in range(4):
            col = pl.multiple_of(((x ^ j) * 4 + (y ^ k)) * block, block)
            copy(first[j].at[k], x_buf.at[pl.ds(0, half), pl.ds(col, block)])
            copy(second[k].at[j], x_buf.at[pl.ds(half, half), pl.ds(col, block)])
    for made in copies:
        made.wait()
    cols = logits.shape[0]
    step = cols // 2
    for c in range(0, cols, step):
        part = jnp.dot(x_buf[...], w_buf[:, c : c + step], preferred_element_type=F32)
        part = part + bias[:, c : c + step]
        logits[c : c + step, :] = part.T
    values = logits[...]
    peak = jnp.max(values, axis=0, keepdims=True)
    stat[0:1, :] = peak
    stat[1:2, :] = teacher_stat[0:1, :]
    stat[2:3, :] = jnp.sum(jnp.exp(values - peak), axis=0, keepdims=True)
    stat[3:4, :] = teacher_stat[1:2, :]


def grad_kernel(pos, *refs):
    weights, pieces = refs[0:2], refs[2:6]
    first, second = refs[6:10], refs[10:14]
    w_buf, g_buf, sems = refs[14:]
    x, y, z = pos[0], pos[1], pos[2]
    quarter = pieces[0].shape[0]
    rows = weights[0].shape[0] // 16
    copies = []

    def copy(src, dst):
        made = pltpu.make_async_copy(src, dst, sems.at[len(copies)])
        made.start()
        copies.append(made)

    for j in range(4):
        row = pl.multiple_of((z ^ j) * quarter, quarter)
        copy(pieces[j], g_buf.at[pl.ds(row, quarter), :])
    for j in range(4):
        for k in range(4):
            row = pl.multiple_of(((x ^ j) * 4 + (y ^ k)) * rows, rows)
            for s in range(2):
                to = ((j * 4 + k) * 2 + s) * rows
                copy(weights[s].at[pl.ds(row, rows), :], w_buf.at[pl.ds(to, rows), :])
    for made in copies:
        made.wait()
    half = g_buf.shape[1] // 2
    group = 8 * rows
    for j in range(4):
        left = w_buf[j * group : (j + 1) * group, :]
        part = jnp.dot(left, g_buf[:, :half], preferred_element_type=F32)
        first[j][...] = part.reshape(first[j].shape)
        part = jnp.dot(left, g_buf[:, half:], preferred_element_type=F32)
        part = part.reshape(first[j].shape)
        for k in range(4):
            second[k][j] = part[k]


def call_logits(pos, own, other, first, second, bias, teacher_stat):
    depth, cols = own[0].shape
    half, block = first[0].shape[1:]
    rows, feats = 2 * half, 16 * block
    hbm = pl.BlockSpec(memory_space=pl.ANY)
    vmem = pl.BlockSpec(memory_space=pltpu.VMEM)
    return pl.pallas_call(
        logits_kernel,
        out_shape=(
            jax.ShapeDtypeStruct((cols, rows), F32),
            jax.ShapeDtypeStruct((4, rows), F32),
        ),
        in_specs=[pl.BlockSpec(memory_space=pltpu.SMEM)] + [hbm] * 16 + [vmem] * 2,
        out_specs=(vmem, vmem),
        scratch_shapes=[
            pltpu.VMEM((rows, feats), BF16),
            pltpu.VMEM((feats, cols), BF16),
            pltpu.SemaphoreType.DMA((40,)),
        ],
        compiler_params=pltpu.CompilerParams(vmem_limit_bytes=VMEM_BYTES),
        cost_estimate=pl.CostEstimate(
            flops=2 * rows * feats * cols,
            bytes_accessed=2 * feats * (rows + cols),
            transcendentals=rows * cols,
        ),
        name="logits_block",
    )(pos, *own, *other, *first, *second, bias, teacher_stat)


def call_grad(pos, weights, pieces):
    rows_in, cols = weights[0].shape
    quarter, tokens = pieces[0].shape
    rows = rows_in // 16
    hbm = pl.BlockSpec(memory_space=pl.ANY)
    vmem = pl.BlockSpec(memory_space=pltpu.VMEM)
    out = jax.ShapeDtypeStruct((4, 2 * rows, tokens // 2), F32)
    return pl.pallas_call(
        grad_kernel,
        out_shape=(out,) * 8,
        in_specs=[pl.BlockSpec(memory_space=pltpu.SMEM)] + [hbm] * 6,
        out_specs=(vmem,) * 8,
        scratch_shapes=[
            pltpu.VMEM((2 * rows_in, cols), BF16),
            pltpu.VMEM((cols, tokens), BF16),
            pltpu.SemaphoreType.DMA((36,)),
        ],
        compiler_params=pltpu.CompilerParams(vmem_limit_bytes=VMEM_BYTES),
        cost_estimate=pl.CostEstimate(
            flops=4 * rows_in * cols * tokens,
            bytes_accessed=4 * rows_in * cols + 2 * cols * tokens,
            transcendentals=0,
        ),
        name="grad_block",
    )(pos, *weights, *pieces)


def per_device(teacher_logits, student_hidden, head_weight, head_bias, pairing, targets):
    z, core, x, y, zh = [lax.axis_index(axis) for axis in AXES]
    pos = jnp.stack([x, y, z, core]).astype(jnp.int32)
    rows, vocab_cols = teacher_logits.shape
    quarter = vocab_cols // 4

    feats = in_order(swaps(student_hidden, "zh"), zh)
    feats = in_order(swaps(jnp.concatenate(feats, axis=1), "zl"), z)
    first = jnp.stack(swaps(jnp.concatenate(feats[:2], axis=0), "y"))
    second = jnp.stack(swaps(jnp.concatenate(feats[2:], axis=0), "x"))
    first, second = swaps(first, "x"), swaps(second, "y")

    own = []
    for j in range(4):
        part = lax.dynamic_slice_in_dim(head_weight, (z ^ j) * quarter, quarter, axis=1)
        own.append(swap(part, "zl", j) if j else part)
    other = [swap(part, "co", 1) for part in own]
    other_weight = swap(head_weight, "co", 1)

    flipped = teacher_logits.T
    teacher = []
    for j in range(4):
        part = lax.dynamic_slice_in_dim(flipped, (z ^ j) * quarter, quarter, axis=0)
        teacher.append(swap(part, "zl", j) if j else part)
    teacher = jnp.stack(teacher)
    teacher = jnp.concatenate([teacher, swap(teacher, "co", 1)], axis=0)
    picked = []
    for i in range(4):
        source = jnp.sum(jnp.arange(8, dtype=jnp.int32) * (pairing == 2 * i + core))
        place = ((source >> 1) ^ z) + 4 * ((source & 1) ^ core)
        picked.append(lax.dynamic_index_in_dim(teacher, place, axis=0, keepdims=False))
    teacher = jnp.concatenate(picked, axis=1).astype(F32)
    teacher_peak = jnp.max(teacher, axis=0, keepdims=True)
    teacher_sum = jnp.sum(jnp.exp(teacher - teacher_peak), axis=0, keepdims=True)
    teacher_stat = jnp.concatenate([teacher_peak, teacher_sum], axis=0)
    wanted = jnp.concatenate(in_order(swaps(targets, "zl"), z))

    bias = lax.dynamic_slice_in_dim(head_bias, z * quarter, quarter)[None, :]
    logits, stat = call_logits(pos, own, other, first, second, bias, teacher_stat)

    for axis in ("x", "y", "zl", "zh"):
        stat = join_stats(swaps(stat, axis))
    lse = stat[:2] + jnp.log(stat[2:])
    student_lse, teacher_lse = lse[0:1], lse[1:2]

    log_target = teacher - teacher_lse
    target_prob = jnp.exp(log_target)
    log_student = logits - student_lse
    base = (((x * 4 + y) * 2 + zh) * 4 + z) * quarter
    ids = base + lax.broadcasted_iota(jnp.int32, logits.shape, 0)
    onehot = ids == wanted[None, :]
    grad = 2.0 * jnp.exp(log_student) - target_prob - onehot.astype(F32)
    grad = grad.astype(BF16)
    loss = jnp.sum(
        target_prob * (log_target - log_student) - jnp.where(onehot, logits, 0.0), axis=0
    )
    alone = (x + y + z + zh) == 0
    loss = loss + jnp.where(alone, student_lse[0], 0.0)

    first = call_grad(pos, (head_weight, other_weight), swaps(grad, "zl"))
    first, second = first[:4], first[4:]
    for axis in ("zl", "x", "y", "zh"):
        loss = add_all(swaps(loss, axis))
    row_loss = lax.dynamic_slice_in_dim(loss, z * rows, rows)

    first = add_all([first[0]] + [swap(first[j], "x", j) for j in range(1, 4)])
    second = add_all([second[0]] + [swap(second[j], "y", j) for j in range(1, 4)])
    first = add_all([first[0]] + [swap(first[j], "y", j) for j in range(1, 4)])
    second = add_all([second[0]] + [swap(second[j], "x", j) for j in range(1, 4)])
    total = jnp.concatenate([first, second], axis=1)
    share = head_weight.shape[0] // 32
    total = total.reshape(2, 2, share, total.shape[1])
    mine = jnp.where(zh == 0, total[:, 0], total[:, 1])
    theirs = jnp.where(zh == 0, total[:, 1], total[:, 0])
    total = (mine + swap(theirs, "zh", 1)).astype(BF16)
    sides = in_order([total[0], swap(total[1], "co", 1)], core)
    sides = [side.reshape(share, 4, rows) for side in sides]
    hidden_grad = jnp.stack(sides, axis=2).reshape(share, 8 * rows)
    return hidden_grad, row_loss


def solution(mesh):
    fine = Mesh(mesh.devices.reshape(tuple(AXES.values())), tuple(AXES))
    pair, vocab = ("zl", "co"), ("x", "y", "zh")
    return jax.shard_map(
        per_device,
        mesh=fine,
        in_specs=(P(pair, vocab), P(pair, vocab), P(pair, vocab), P(vocab), P(), P(pair)),
        out_specs=(P(pair + vocab, None), P(pair)),
        check_vma=False,
    )
```

time: 863 us -> 280 us (0.32)
  blocking collectives: 350 us -> 0 us
  waiting for transfers between devices: 445 us -> 121 us
  starting transfers between devices: 3.53 us -> 110 us
  matrix products: 21.5 us -> 0 us
  Pallas kernels: 0 us -> 15.1 us
  local copies, waits for them, and re-layouts: 20.4 us -> 11.1 us
    all_gather x3 -> x0, waiting for transfers between devices: 326 us -> none  [the longest x1 167 us: per_device(): full_weight = lax.all_gather(head_weight, 'pair', axis=0, tiled=True)]
    psum x2 -> x0, blocking collectives: 229 us -> none  [the longest x1 121 us: per_device(): diverge_sum, target_sum = lax.psum((diverge_part, target_part), 'vocab')]
    ppermute x0 -> x68, waiting for transfers between devices: none -> 121 us  [swap(): return lax.ppermute(value, axis, [(i, i ^ flip) for i in range(AXES[axis])])]
    pmax x1 -> x0, blocking collectives: 121 us -> none  [split_lse(): row_peak = lax.pmax(jnp.max(values, axis=1), 'vocab')]
    reduce_scatter x1 -> x0, waiting for transfers between devices: 114 us -> none  [per_device(): lax.psum_scatter(lax.dot_general(weight_block, grad_logits, (((1,), (1,))...]
    ppermute x0 -> x68, starting transfers between devices: none -> 110 us  [swap(): return lax.ppermute(value, axis, [(i, i ^ flip) for i in range(AXES[axis])])]
    dot_general x2 -> x0, matrix products: 21.5 us -> none  [the longest x1 13.1 us: per_device(): lax.dot_general(weight_block, grad_logits, (((1,), (1,)), ((), ())), pref...]
    pallas_call x0 -> x2, Pallas kernels: none -> 15.1 us  [the longest x1 8.06 us: call_logits(): pl.pallas_call(logits_kernel, out_shape=(jax.ShapeDtypeStruct((cols, rows...]
  transfers between devices with their start and end apart: 5 -> 68, of which waited for: 5 -> 27; matrix products, arithmetic and copies ran while one was open for 2% -> 7% of each run, Pallas kernels for 0% -> 0%
where the time goes in v1:
time: 280 us; the launch traced here: 275 us
  waiting for transfers between devices  121 us (43%)
  starting transfers between devices  110 us (39%)
  Pallas kernels  15.1 us (5%)
  local copies, waits for them, and re-layouts  11.1 us (4%)
  other arithmetic  11 us (4%)
  between operations  6.5 us (2%)
    ppermute x68, waiting for transfers between devices, swap(): return lax.ppermute(value, axis, [(i, i ^ flip) for i in range(AXES[axis])])  121 us
    ppermute x68, starting transfers between devices, swap(): return lax.ppermute(value, axis, [(i, i ^ flip) for i in range(AXES[axis])])  110 us
    pallas_call x1, Pallas kernels, call_logits(): pl.pallas_call(logits_kernel, out_shape=(jax.ShapeDtypeStruct((cols, rows...  8.06 us
    pallas_call x1, Pallas kernels, call_grad(): pl.pallas_call(grad_kernel, out_shape=(out,) * 8, in_specs=[pl.BlockSpec(...  7.09 us
  transfers between devices with their start and end apart: 68, of which 27 were waited for; matrix products, arithmetic and copies ran while one was open for 7% of the time, Pallas kernels for 0%

profile of v1, /device:TPU:32, one launch (start us, length us, event | category | flops | bytes accessed | tf_op | source)
XLA Modules:
  0.0 275.0 jit_solution(10467697819449271718)
XLA Ops:
  0.6 6.4 %collective-permute-start.8 = (bf16[128,128]{1,0:T(8,128)(2,1)}, bf16[128,128]{1,0:T(8,128)(2,1)S(1)}, u32[]{:S(2)}, u32[]{:S(2)}) collective-permute-start(bf16[128,128]{1,0:T(8,128)(2,1)} %param.7), channel_id=1, source_target_pairs={{0,1},{1,0},{2,3},{3,2},{4,5},{5,4},{6,7},{7,6},{8,9},{9,8},{10,11... | collective-permute-start | bytes 98312 | tf_op jit(solution)/shard_map/ppermute | solution.py:15
  9.9 3.0 %collective-permute-start.10 = (bf16[128,256]{1,0:T(8,128)(2,1)S(1)}, bf16[128,256]{1,0:T(8,128)(2,1)S(1)}, u32[]{:S(2)}, u32[]{:S(2)}) collective-permute-start(bf16[128,256]{1,0:T(8,128)(2,1)S(1)} %pad_maximum_fusion.7), channel_id=1, source_target_pairs={{0,128},{64,192},{128,0},{192,64},{1,129},{65,193},{129,1},{193,65... | collective-permute-start | bytes 196616 | tf_op jit(solution)/shard_map/ppermute | solution.py:15
  19.1 3.1 %collective-permute-start.19 = (bf16[256,256]{1,0:T(8,128)(2,1)S(1)}, bf16[256,256]{1,0:T(8,128)(2,1)}, u32[]{:S(2)}, u32[]{:S(2)}) collective-permute-start(bf16[256,256]{1,0:T(8,128)(2,1)S(1)} %get-tuple-element.58), channel_id=1, source_target_pairs={{0,16},{8,24},{16,0},{24,8},{1,17},{9,25},{17,1},{25,9},{2,18},{10... | collective-permute-start | bytes 393224 | tf_op jit(solution)/shard_map/ppermute | solution.py:15
  34.9 3.0 %collective-permute-start.13 = (bf16[256,256]{1,0:T(8,128)(2,1)}, bf16[256,256]{1,0:T(8,128)(2,1)S(1)}, u32[]{:S(2)}, u32[]{:S(2)}) collective-permute-start(bf16[256,256]{1,0:T(8,128)(2,1)} %get-tuple-element.60), channel_id=1, source_target_pairs={{0,4},{2,6},{4,0},{6,2},{1,5},{3,7},{5,1},{7,3},{8,12},{10,14},{12... | collective-permute-start | bytes 393224 | tf_op jit(solution)/shard_map/ppermute | solution.py:15
  47.6 5.3 %collective-permute-done.14 = bf16[256,256]{1,0:T(8,128)(2,1)S(1)} collective-permute-done((bf16[256,256]{1,0:T(8,128)(2,1)}, bf16[256,256]{1,0:T(8,128)(2,1)S(1)}, u32[]{:S(2)}, u32[]{:S(2)}) %collective-permute-start.14) | collective-permute-done | bytes 131104 | tf_op jit(solution)/shard_map/ppermute | solution.py:15
  54.1 15.4 %collective-permute-done.2.refs_2_ = bf16[512,512]{1,0:T(8,128)(2,1)} collective-permute-done((bf16[512,512]{1,0:T(8,128)(2,1)}, bf16[512,512]{1,0:T(8,128)(2,1)}, u32[]{:S(2)}, u32[]{:S(2)}) %collective-permute-start.2) | collective-permute-done | bytes 524320 | tf_op jit(solution)/shard_map/ppermute | solution.py:15
  69.4 2.9 %collective-permute-start.22 = (bf16[4,256,256]{2,1,0:T(8,128)(2,1)S(1)}, bf16[4,256,256]{2,1,0:T(8,128)(2,1)S(1)}, u32[]{:S(2)}, u32[]{:S(2)}) collective-permute-start(bf16[4,256,256]{2,1,0:T(8,128)(2,1)S(1)} %pad_maximum_fusion.1.refs_12_), channel_id=1, source_target_pairs={{0,4},{2,6},{4,0},{6,2},{1,5},{3,7},{5,1},{7,3},{8,12},{10,14},{12... | collective-permute-start | bytes 1572872 | tf_op jit(solution)/shard_map/ppermute | solution.py:15
  72.3 5.4 %collective-permute-done.3.refs_3_ = bf16[512,512]{1,0:T(8,128)(2,1)} collective-permute-done((bf16[512,512]{1,0:T(8,128)(2,1)}, bf16[512,512]{1,0:T(8,128)(2,1)}, u32[]{:S(2)}, u32[]{:S(2)}) %collective-permute-start.3) | collective-permute-done | bytes 524320 | tf_op jit(solution)/shard_map/ppermute | solution.py:15
  77.7 3.2 %collective-permute-start.23 = (bf16[4,256,256]{2,1,0:T(8,128)(2,1)S(1)}, bf16[4,256,256]{2,1,0:T(8,128)(2,1)S(1)}, u32[]{:S(2)}, u32[]{:S(2)}) collective-permute-start(bf16[4,256,256]{2,1,0:T(8,128)(2,1)S(1)} %pad_maximum_fusion.1.refs_12_), channel_id=1, source_target_pairs={{0,6},{2,4},{4,2},{6,0},{1,7},{3,5},{5,3},{7,1},{8,14},{10,12},{12... | collective-permute-start | bytes 1572872 | tf_op jit(solution)/shard_map/ppermute | solution.py:15
  83.2 2.8 %collective-permute-start.16 = (bf16[4,256,256]{2,1,0:T(8,128)(2,1)S(1)}, bf16[4,256,256]{2,1,0:T(8,128)(2,1)}, u32[]{:S(2)}, u32[]{:S(2)}) collective-permute-start(bf16[4,256,256]{2,1,0:T(8,128)(2,1)S(1)} %pad_maximum_fusion.refs_8_), channel_id=1, source_target_pairs={{0,16},{8,24},{16,0},{24,8},{1,17},{9,25},{17,1},{25,9},{2,18},{10... | collective-permute-start | bytes 1572872 | tf_op jit(solution)/shard_map/ppermute | solution.py:15
  86.7 4.7 %collective-permute-done.23.refs_15_ = bf16[4,256,256]{2,1,0:T(8,128)(2,1)S(1)} collective-permute-done((bf16[4,256,256]{2,1,0:T(8,128)(2,1)S(1)}, bf16[4,256,256]{2,1,0:T(8,128)(2,1)S(1)}, u32[]{:S(2)}, u32[]{:S(2)}) %collective-permute-start.23) | collective-permute-done | bytes 524320 | tf_op jit(solution)/shard_map/ppermute | solution.py:15
  91.4 4.4 %collective-permute-done.15.refs_9_ = bf16[4,256,256]{2,1,0:T(8,128)(2,1)S(1)} collective-permute-done((bf16[4,256,256]{2,1,0:T(8,128)(2,1)S(1)}, bf16[4,256,256]{2,1,0:T(8,128)(2,1)S(1)}, u32[]{:S(2)}, u32[]{:S(2)}) %collective-permute-start.15) | collective-permute-done | bytes 524320 | tf_op jit(solution)/shard_map/ppermute | solution.py:15
  100.7 4.2 %collective-permute-done.16.refs_10_ = bf16[4,256,256]{2,1,0:T(8,128)(2,1)} collective-permute-done((bf16[4,256,256]{2,1,0:T(8,128)(2,1)S(1)}, bf16[4,256,256]{2,1,0:T(8,128)(2,1)}, u32[]{:S(2)}, u32[]{:S(2)}) %collective-permute-start.16) | collective-permute-done | bytes 524320 | tf_op jit(solution)/shard_map/ppermute | solution.py:15
  104.8 3.6 %collective-permute-done.17.refs_11_ = bf16[4,256,256]{2,1,0:T(8,128)(2,1)} collective-permute-done((bf16[4,256,256]{2,1,0:T(8,128)(2,1)S(1)}, bf16[4,256,256]{2,1,0:T(8,128)(2,1)}, u32[]{:S(2)}, u32[]{:S(2)}) %collective-permute-start.17) | collective-permute-done | bytes 524320 | tf_op jit(solution)/shard_map/ppermute | solution.py:15
  108.5 8.1 %logits_block.1 = (f32[512,512]{1,0:T(8,128)}, f32[4,512]{1,0:T(4,128)}) custom-call(s32[4]{0:T(128)} %pad_add_fusion.1.pos, bf16[512,512]{1,0:T(8,128)(2,1)} %get-tuple-element.37.refs_0_, bf16[512,512]{1,0:T(8,128)(2,1)} %collective-permute-done.1.refs_1_, bf16[512,512]{1,0:T(8,128)(2,1)} %collective-permute-done.2.refs_2_, ...), custom_call_target="tpu_custom_call" | custom-call | flops 2147483648 | bytes 8388608 | tf_op jit(solution)/shard_map/logits_block/pallas_call | solution.py:135
  126.6 2.8 %collective-permute-start.33 = (f32[4,512]{1,0:T(4,128)S(1)}, f32[4,512]{1,0:T(4,128)S(1)}, u32[]{:S(2)}, u32[]{:S(2)}) collective-permute-start(f32[4,512]{1,0:T(4,128)S(1)} %pad_maximum_fusion.9), channel_id=1, source_target_pairs={{0,6},{2,4},{4,2},{6,0},{1,7},{3,5},{5,3},{7,1},{8,14},{10,12},{12... | collective-permute-start | bytes 24584 | tf_op jit(solution)/shard_map/ppermute | solution.py:15
  133.2 10.8 %collective-permute-start.35 = (f32[4,512]{1,0:T(4,128)S(1)}, f32[4,512]{1,0:T(4,128)S(1)}, u32[]{:S(2)}, u32[]{:S(2)}) collective-permute-start(f32[4,512]{1,0:T(4,128)S(1)} %pad_maximum_fusion.10), channel_id=1, source_target_pairs={{0,128},{64,192},{128,0},{192,64},{1,129},{65,193},{129,1},{193,65... | collective-permute-start | bytes 24584 | tf_op jit(solution)/shard_map/ppermute | solution.py:15
  147.7 4.6 %collective-permute-start.37 = (f32[4,512]{1,0:T(4,128)S(1)}, f32[4,512]{1,0:T(4,128)S(1)}, u32[]{:S(2)}, u32[]{:S(2)}) collective-permute-start(f32[4,512]{1,0:T(4,128)S(1)} %pad_maximum_fusion.11), channel_id=1, source_target_pairs={{0,1},{1,0},{2,3},{3,2},{4,5},{5,4},{6,7},{7,6},{8,9},{9,8},{10,11... | collective-permute-start | bytes 24584 | tf_op jit(solution)/shard_map/ppermute | solution.py:15
  152.3 3.1 %collective-permute-done.37 = f32[4,512]{1,0:T(4,128)S(1)} collective-permute-done((f32[4,512]{1,0:T(4,128)S(1)}, f32[4,512]{1,0:T(4,128)S(1)}, u32[]{:S(2)}, u32[]{:S(2)}) %collective-permute-start.37) | collective-permute-done | bytes 8224 | tf_op jit(solution)/shard_map/ppermute | solution.py:15
  161.0 17.5 %collective-permute-done.41.refs_3_ = bf16[512,512]{1,0:T(8,128)(2,1)} collective-permute-done((bf16[512,512]{1,0:T(8,128)(2,1)S(1)}, bf16[512,512]{1,0:T(8,128)(2,1)}, u32[]{:S(2)}, u32[]{:S(2)}) %collective-permute-start.41) | collective-permute-done | bytes 524320 | tf_op jit(solution)/shard_map/ppermute | solution.py:15
  178.5 16.6 %collective-permute-done.42.refs_4_ = bf16[512,512]{1,0:T(8,128)(2,1)} collective-permute-done((bf16[512,512]{1,0:T(8,128)(2,1)S(1)}, bf16[512,512]{1,0:T(8,128)(2,1)}, u32[]{:S(2)}, u32[]{:S(2)}) %collective-permute-start.42) | collective-permute-done | bytes 524320 | tf_op jit(solution)/shard_map/ppermute | solution.py:15
  195.1 9.5 %collective-permute-done.43.refs_5_ = bf16[512,512]{1,0:T(8,128)(2,1)} collective-permute-done((bf16[512,512]{1,0:T(8,128)(2,1)S(1)}, bf16[512,512]{1,0:T(8,128)(2,1)}, u32[]{:S(2)}, u32[]{:S(2)}) %collective-permute-start.43) | collective-permute-done | bytes 524320 | tf_op jit(solution)/shard_map/ppermute | solution.py:15
  204.6 7.1 %grad_block.1 = (f32[4,64,256]{2,1,0:T(8,128)}, f32[4,64,256]{2,1,0:T(8,128)}, f32[4,64,256]{2,1,0:T(8,128)}, f32[4,64,256]{2,1,0:T(8,128)}, f32[4,64,256]{2,1,0...) custom-call(s32[4]{0:T(128)} %pad_add_fusion.1.pos, bf16[512,2048]{1,0:T(8,128)(2,1)} %refs_0_.1, ...), custom_call_target="tpu_custom_call" | custom-call | flops 2147483648 | bytes 6291456 | tf_op jit(solution)/shard_map/grad_block/pallas_call | solution.py:165
  212.0 3.8 %collective-permute-start.45 = (f32[4,64,256]{2,1,0:T(8,128)}, f32[4,64,256]{2,1,0:T(8,128)S(1)}, u32[]{:S(2)}, u32[]{:S(2)}) collective-permute-start(f32[4,64,256]{2,1,0:T(8,128)} %get-tuple-element.16), channel_id=1, source_target_pairs={{0,16},{8,24},{16,0},{24,8},{1,17},{9,25},{17,1},{25,9},{2,18},{10... | collective-permute-start | bytes 786440 | tf_op jit(solution)/shard_map/ppermute | solution.py:15
  223.7 4.0 %collective-permute-start.62 = (f32[512]{0:T(512)S(1)}, f32[512]{0:T(512)S(1)}, u32[]{:S(2)}, u32[]{:S(2)}) collective-permute-start(f32[512]{0:T(512)S(1)} %add_add_fusion.4), channel_id=1, source_target_pairs={{0,16},{8,24},{16,0},{24,8},{1,17},{9,25},{17,1},{25,9},{2,18},{10... | collective-permute-start | bytes 6152 | tf_op jit(solution)/shard_map/ppermute | solution.py:15
  229.6 2.8 %collective-permute-start.52 = (f32[4,64,256]{2,1,0:T(8,128)}, f32[4,64,256]{2,1,0:T(8,128)S(1)}, u32[]{:S(2)}, u32[]{:S(2)}) collective-permute-start(f32[4,64,256]{2,1,0:T(8,128)} %get-tuple-element.21), channel_id=1, source_target_pairs={{0,6},{2,4},{4,2},{6,0},{1,7},{3,5},{5,3},{7,1},{8,14},{10,12},{12... | collective-permute-start | bytes 786440 | tf_op jit(solution)/shard_map/ppermute | solution.py:15
  234.5 4.0 %collective-permute-done.51 = f32[4,64,256]{2,1,0:T(8,128)S(1)} collective-permute-done((f32[4,64,256]{2,1,0:T(8,128)}, f32[4,64,256]{2,1,0:T(8,128)S(1)}, u32[]{:S(2)}, u32[]{:S(2)}) %collective-permute-start.51) | collective-permute-done | bytes 262176 | tf_op jit(solution)/shard_map/ppermute | solution.py:15
  241.0 3.0 %collective-permute-start.49 = (f32[64,256]{1,0:T(8,128)S(1)}, f32[64,256]{1,0:T(8,128)S(1)}, u32[]{:S(2)}, u32[]{:S(2)}) collective-permute-start(f32[64,256]{1,0:T(8,128)S(1)} %get-tuple-element.47), channel_id=1, source_target_pairs={{0,6},{2,4},{4,2},{6,0},{1,7},{3,5},{5,3},{7,1},{8,14},{10,12},{12... | collective-permute-start | bytes 196616 | tf_op jit(solution)/shard_map/ppermute | solution.py:15
  252.8 4.5 %collective-permute-start.56 = (f32[2,16,512]{2,1,0:T(8,128)S(1)}, f32[2,16,512]{2,1,0:T(8,128)S(1)}, u32[]{:S(2)}, u32[]{:S(2)}) collective-permute-start(f32[2,16,512]{2,1,0:T(8,128)S(1)} %select_bitcast_fusion), channel_id=1, source_target_pairs={{0,1},{1,0},{2,3},{3,2},{4,5},{5,4},{6,7},{7,6},{8,9},{9,8},{10,11... | collective-permute-start | bytes 196616 | tf_op jit(solution)/shard_map/ppermute | solution.py:15
  257.5 3.6 %collective-permute-start.65 = (f32[512]{0:T(512)S(1)}, f32[512]{0:T(512)S(1)}, u32[]{:S(2)}, u32[]{:S(2)}) collective-permute-start(f32[512]{0:T(512)S(1)} %add_add_fusion.3), channel_id=1, source_target_pairs={{0,4},{2,6},{4,0},{6,2},{1,5},{3,7},{5,1},{7,3},{8,12},{10,14},{12... | collective-permute-start | bytes 6152 | tf_op jit(solution)/shard_map/ppermute | solution.py:15
  262.7 3.2 %collective-permute-done.66 = f32[512]{0:T(512)S(1)} collective-permute-done((f32[512]{0:T(512)S(1)}, f32[512]{0:T(512)S(1)}, u32[]{:S(2)}, u32[]{:S(2)}) %collective-permute-start.66) | collective-permute-done | bytes 2080 | tf_op jit(solution)/shard_map/ppermute | solution.py:15
  267.4 6.0 %collective-permute-done.67 = f32[512]{0:T(512)S(1)} collective-permute-done((f32[512]{0:T(512)S(1)}, f32[512]{0:T(512)S(1)}, u32[]{:S(2)}, u32[]{:S(2)}) %collective-permute-start.67) | collective-permute-done | bytes 2080 | tf_op jit(solution)/shard_map/ppermute | solution.py:15
  (193 shorter events, 86.3 us)
Async XLA Ops:
  18.5 12.3 %collective-permute-start.26 = (bf16[512,128]{0,1:T(8,128)(2,1)S(1)}, bf16[512,128]{0,1:T(8,128)(2,1)S(1)}, u32[]{:S(2)}, u32[]{:S(2)}) collective-permute-start(bf16[512,128]{0,1:T(8,128)(2,1)S(1)} %get-tuple-element.44), channel_id=1, source_target_pairs={{0,192},{64,128},{128,64},{192,0},{1,193},{65,129},{129,65},{193,1... | collective-permute-start | bytes 393224 | tf_op jit(solution)/shard_map/ppermute | solution.py:15
  19.1 13.9 %collective-permute-start.19 = (bf16[256,256]{1,0:T(8,128)(2,1)S(1)}, bf16[256,256]{1,0:T(8,128)(2,1)}, u32[]{:S(2)}, u32[]{:S(2)}) collective-permute-start(bf16[256,256]{1,0:T(8,128)(2,1)S(1)} %get-tuple-element.58), channel_id=1, source_target_pairs={{0,16},{8,24},{16,0},{24,8},{1,17},{9,25},{17,1},{25,9},{2,18},{10... | collective-permute-start | bytes 393224 | tf_op jit(solution)/shard_map/ppermute | solution.py:15
  22.2 12.0 %collective-permute-start.20 = (bf16[256,256]{1,0:T(8,128)(2,1)S(1)}, bf16[256,256]{1,0:T(8,128)(2,1)}, u32[]{:S(2)}, u32[]{:S(2)}) collective-permute-start(bf16[256,256]{1,0:T(8,128)(2,1)S(1)} %get-tuple-element.58), channel_id=1, source_target_pairs={{0,24},{8,16},{16,8},{24,0},{1,25},{9,17},{17,9},{25,1},{2,26},{10... | collective-permute-start | bytes 393224 | tf_op jit(solution)/shard_map/ppermute | solution.py:15
  30.8 23.1 %collective-permute-start.1 = (bf16[512,512]{1,0:T(8,128)(2,1)}, bf16[512,512]{1,0:T(8,128)(2,1)}, u32[]{:S(2)}, u32[]{:S(2)}) collective-permute-start(bf16[512,512]{1,0:T(8,128)(2,1)} %get-tuple-element.36), channel_id=1, source_target_pairs={{0,64},{64,0},{128,192},{192,128},{1,65},{65,1},{129,193},{193,129... | collective-permute-start | bytes 1572872 | tf_op jit(solution)/shard_map/ppermute | solution.py:15
  33.1 36.4 %collective-permute-start.2 = (bf16[512,512]{1,0:T(8,128)(2,1)}, bf16[512,512]{1,0:T(8,128)(2,1)}, u32[]{:S(2)}, u32[]{:S(2)}) collective-permute-start(bf16[512,512]{1,0:T(8,128)(2,1)} %get-tuple-element.35), channel_id=1, source_target_pairs={{0,128},{64,192},{128,0},{192,64},{1,129},{65,193},{129,1},{193,65... | collective-permute-start | bytes 1572872 | tf_op jit(solution)/shard_map/ppermute | solution.py:15
  34.3 43.4 %collective-permute-start.3 = (bf16[512,512]{1,0:T(8,128)(2,1)}, bf16[512,512]{1,0:T(8,128)(2,1)}, u32[]{:S(2)}, u32[]{:S(2)}) collective-permute-start(bf16[512,512]{1,0:T(8,128)(2,1)} %get-tuple-element.34), channel_id=1, source_target_pairs={{0,192},{64,128},{128,64},{192,0},{1,193},{65,129},{129,65},{193,1... | collective-permute-start | bytes 1572872 | tf_op jit(solution)/shard_map/ppermute | solution.py:15
  34.8 46.0 %collective-permute-start.4 = (bf16[512,512]{1,0:T(8,128)(2,1)}, bf16[512,512]{1,0:T(8,128)(2,1)}, u32[]{:S(2)}, u32[]{:S(2)}) collective-permute-start(bf16[512,512]{1,0:T(8,128)(2,1)} %get-tuple-element.37.refs_0_), channel_id=1, source_target_pairs={{0,32},{32,0},{1,33},{33,1},{2,34},{34,2},{3,35},{35,3},{4,36},{36... | collective-permute-start | bytes 1572872 | tf_op jit(solution)/shard_map/ppermute | solution.py:15
  52.9 30.3 %collective-permute-start.27 = (bf16[4,512,128]{1,2,0:T(8,128)(2,1)S(1)}, bf16[4,512,128]{1,2,0:T(8,128)(2,1)S(1)}, u32[]{:S(2)}, u32[]{:S(2)}) collective-permute-start(bf16[4,512,128]{1,2,0:T(8,128)(2,1)S(1)} %pad_maximum_fusion.2), channel_id=1, source_target_pairs={{0,32},{32,0},{1,33},{33,1},{2,34},{34,2},{3,35},{35,3},{4,36},{36... | collective-permute-start | bytes 1572872 | tf_op jit(solution)/shard_map/ppermute | solution.py:15
  54.0 32.1 %collective-permute-start.21 = (bf16[4,256,256]{2,1,0:T(8,128)(2,1)S(1)}, bf16[4,256,256]{2,1,0:T(8,128)(2,1)S(1)}, u32[]{:S(2)}, u32[]{:S(2)}) collective-permute-start(bf16[4,256,256]{2,1,0:T(8,128)(2,1)S(1)} %pad_maximum_fusion.1.refs_12_), channel_id=1, source_target_pairs={{0,2},{2,0},{4,6},{6,4},{1,3},{3,1},{5,7},{7,5},{8,10},{10,8},{12,... | collective-permute-start | bytes 1572872 | tf_op jit(solution)/shard_map/ppermute | solution.py:15
  69.4 17.2 %collective-permute-start.22 = (bf16[4,256,256]{2,1,0:T(8,128)(2,1)S(1)}, bf16[4,256,256]{2,1,0:T(8,128)(2,1)S(1)}, u32[]{:S(2)}, u32[]{:S(2)}) collective-permute-start(bf16[4,256,256]{2,1,0:T(8,128)(2,1)S(1)} %pad_maximum_fusion.1.refs_12_), channel_id=1, source_target_pairs={{0,4},{2,6},{4,0},{6,2},{1,5},{3,7},{5,1},{7,3},{8,12},{10,14},{12... | collective-permute-start | bytes 1572872 | tf_op jit(solution)/shard_map/ppermute | solution.py:15
  77.7 13.6 %collective-permute-start.23 = (bf16[4,256,256]{2,1,0:T(8,128)(2,1)S(1)}, bf16[4,256,256]{2,1,0:T(8,128)(2,1)S(1)}, u32[]{:S(2)}, u32[]{:S(2)}) collective-permute-start(bf16[4,256,256]{2,1,0:T(8,128)(2,1)S(1)} %pad_maximum_fusion.1.refs_12_), channel_id=1, source_target_pairs={{0,6},{2,4},{4,2},{6,0},{1,7},{3,5},{5,3},{7,1},{8,14},{10,12},{12... | collective-permute-start | bytes 1572872 | tf_op jit(solution)/shard_map/ppermute | solution.py:15
  80.9 14.9 %collective-permute-start.15 = (bf16[4,256,256]{2,1,0:T(8,128)(2,1)S(1)}, bf16[4,256,256]{2,1,0:T(8,128)(2,1)S(1)}, u32[]{:S(2)}, u32[]{:S(2)}) collective-permute-start(bf16[4,256,256]{2,1,0:T(8,128)(2,1)S(1)} %pad_maximum_fusion.refs_8_), channel_id=1, source_target_pairs={{0,8},{8,0},{16,24},{24,16},{1,9},{9,1},{17,25},{25,17},{2,10},{10... | collective-permute-start | bytes 1572872 | tf_op jit(solution)/shard_map/ppermute | solution.py:15
  83.2 21.6 %collective-permute-start.16 = (bf16[4,256,256]{2,1,0:T(8,128)(2,1)S(1)}, bf16[4,256,256]{2,1,0:T(8,128)(2,1)}, u32[]{:S(2)}, u32[]{:S(2)}) collective-permute-start(bf16[4,256,256]{2,1,0:T(8,128)(2,1)S(1)} %pad_maximum_fusion.refs_8_), channel_id=1, source_target_pairs={{0,16},{8,24},{16,0},{24,8},{1,17},{9,25},{17,1},{25,9},{2,18},{10... | collective-permute-start | bytes 1572872 | tf_op jit(solution)/shard_map/ppermute | solution.py:15
  86.1 22.4 %collective-permute-start.17 = (bf16[4,256,256]{2,1,0:T(8,128)(2,1)S(1)}, bf16[4,256,256]{2,1,0:T(8,128)(2,1)}, u32[]{:S(2)}, u32[]{:S(2)}) collective-permute-start(bf16[4,256,256]{2,1,0:T(8,128)(2,1)S(1)} %pad_maximum_fusion.refs_8_), channel_id=1, source_target_pairs={{0,24},{8,16},{16,8},{24,0},{1,25},{9,17},{17,9},{25,1},{2,26},{10... | collective-permute-start | bytes 1572872 | tf_op jit(solution)/shard_map/ppermute | solution.py:15
  86.6 21.8 %collective-permute-start.5 = (bf16[512,512]{1,0:T(8,128)(2,1)}, bf16[512,512]{1,0:T(8,128)(2,1)}, u32[]{:S(2)}, u32[]{:S(2)}) collective-permute-start(bf16[512,512]{1,0:T(8,128)(2,1)} %collective-permute-done.1.refs_1_), channel_id=1, source_target_pairs={{0,32},{32,0},{1,33},{33,1},{2,34},{34,2},{3,35},{35,3},{4,36},{36... | collective-permute-start | bytes 1572872 | tf_op jit(solution)/shard_map/ppermute | solution.py:15
  91.4 17.1 %collective-permute-start.6 = (bf16[512,512]{1,0:T(8,128)(2,1)}, bf16[512,512]{1,0:T(8,128)(2,1)}, u32[]{:S(2)}, u32[]{:S(2)}) collective-permute-start(bf16[512,512]{1,0:T(8,128)(2,1)} %collective-permute-done.2.refs_2_), channel_id=1, source_target_pairs={{0,32},{32,0},{1,33},{33,1},{2,34},{34,2},{3,35},{35,3},{4,36},{36... | collective-permute-start | bytes 1572872 | tf_op jit(solution)/shard_map/ppermute | solution.py:15
  96.6 11.9 %collective-permute-start.7 = (bf16[512,512]{1,0:T(8,128)(2,1)}, bf16[512,512]{1,0:T(8,128)(2,1)}, u32[]{:S(2)}, u32[]{:S(2)}) collective-permute-start(bf16[512,512]{1,0:T(8,128)(2,1)} %collective-permute-done.3.refs_3_), channel_id=1, source_target_pairs={{0,32},{32,0},{1,33},{33,1},{2,34},{34,2},{3,35},{35,3},{4,36},{36... | collective-permute-start | bytes 1572872 | tf_op jit(solution)/shard_map/ppermute | solution.py:15
  130.3 13.7 %collective-permute-start.39 = (s32[128]{0:T(128)S(1)}, s32[128]{0:T(128)S(1)}, u32[]{:S(2)}, u32[]{:S(2)}) collective-permute-start(s32[128]{0:T(128)S(1)} %copy-done.13), channel_id=1, source_target_pairs={{0,128},{64,192},{128,0},{192,64},{1,129},{65,193},{129,1},{193,65... | collective-permute-start | bytes 1544 | tf_op jit(solution)/shard_map/ppermute | solution.py:15
  130.3 15.0 %collective-permute-start.40 = (s32[128]{0:T(128)S(1)}, s32[128]{0:T(128)S(1)}, u32[]{:S(2)}, u32[]{:S(2)}) collective-permute-start(s32[128]{0:T(128)S(1)} %copy-done.13), channel_id=1, source_target_pairs={{0,64},{64,0},{128,192},{192,128},{1,65},{65,1},{129,193},{193,129... | collective-permute-start | bytes 1544 | tf_op jit(solution)/shard_map/ppermute | solution.py:15
  133.0 71.6 %collective-permute-start = (bf16[512,2048]{1,0:T(8,128)(2,1)S(1)}, bf16[512,2048]{1,0:T(8,128)(2,1)}, u32[]{:S(2)}, u32[]{:S(2)}) collective-permute-start(bf16[512,2048]{1,0:T(8,128)(2,1)S(1)} %copy-done.2), channel_id=1, source_target_pairs={{0,32},{32,0},{1,33},{33,1},{2,34},{34,2},{3,35},{35,3},{4,36},{36... | collective-permute-start | bytes 6291464 | tf_op jit(solution)/shard_map/ppermute | solution.py:15
  133.0 12.2 %collective-permute-start.34 = (f32[4,512]{1,0:T(4,128)S(1)}, f32[4,512]{1,0:T(4,128)S(1)}, u32[]{:S(2)}, u32[]{:S(2)}) collective-permute-start(f32[4,512]{1,0:T(4,128)S(1)} %pad_maximum_fusion.10), channel_id=1, source_target_pairs={{0,64},{64,0},{128,192},{192,128},{1,65},{65,1},{129,193},{193,129... | collective-permute-start | bytes 24584 | tf_op jit(solution)/shard_map/ppermute | solution.py:15
  133.2 13.4 %collective-permute-start.35 = (f32[4,512]{1,0:T(4,128)S(1)}, f32[4,512]{1,0:T(4,128)S(1)}, u32[]{:S(2)}, u32[]{:S(2)}) collective-permute-start(f32[4,512]{1,0:T(4,128)S(1)} %pad_maximum_fusion.10), channel_id=1, source_target_pairs={{0,128},{64,192},{128,0},{192,64},{1,129},{65,193},{129,1},{193,65... | collective-permute-start | bytes 24584 | tf_op jit(solution)/shard_map/ppermute | solution.py:15
  157.3 21.3 %collective-permute-start.41 = (bf16[512,512]{1,0:T(8,128)(2,1)S(1)}, bf16[512,512]{1,0:T(8,128)(2,1)}, u32[]{:S(2)}, u32[]{:S(2)}) collective-permute-start(bf16[512,512]{1,0:T(8,128)(2,1)S(1)} %get-tuple-element.39.refs_2_), channel_id=1, source_target_pairs={{0,64},{64,0},{128,192},{192,128},{1,65},{65,1},{129,193},{193,129... | collective-permute-start | bytes 1572872 | tf_op jit(solution)/shard_map/ppermute | solution.py:15
  159.5 35.6 %collective-permute-start.42 = (bf16[512,512]{1,0:T(8,128)(2,1)S(1)}, bf16[512,512]{1,0:T(8,128)(2,1)}, u32[]{:S(2)}, u32[]{:S(2)}) collective-permute-start(bf16[512,512]{1,0:T(8,128)(2,1)S(1)} %get-tuple-element.39.refs_2_), channel_id=1, source_target_pairs={{0,128},{64,192},{128,0},{192,64},{1,129},{65,193},{129,1},{193,65... | collective-permute-start | bytes 1572872 | tf_op jit(solution)/shard_map/ppermute | solution.py:15
  160.2 44.4 %collective-permute-start.43 = (bf16[512,512]{1,0:T(8,128)(2,1)S(1)}, bf16[512,512]{1,0:T(8,128)(2,1)}, u32[]{:S(2)}, u32[]{:S(2)}) collective-permute-start(bf16[512,512]{1,0:T(8,128)(2,1)S(1)} %get-tuple-element.39.refs_2_), channel_id=1, source_target_pairs={{0,192},{64,128},{128,64},{192,0},{1,193},{65,129},{129,65},{193,1... | collective-permute-start | bytes 1572872 | tf_op jit(solution)/shard_map/ppermute | solution.py:15
  211.7 16.0 %collective-permute-start.44 = (f32[4,64,256]{2,1,0:T(8,128)}, f32[4,64,256]{2,1,0:T(8,128)S(1)}, u32[]{:S(2)}, u32[]{:S(2)}) collective-permute-start(f32[4,64,256]{2,1,0:T(8,128)} %get-tuple-element.15), channel_id=1, source_target_pairs={{0,8},{8,0},{16,24},{24,16},{1,9},{9,1},{17,25},{25,17},{2,10},{10... | collective-permute-start | bytes 786440 | tf_op jit(solution)/shard_map/ppermute | solution.py:15
  212.0 15.7 %collective-permute-start.45 = (f32[4,64,256]{2,1,0:T(8,128)}, f32[4,64,256]{2,1,0:T(8,128)S(1)}, u32[]{:S(2)}, u32[]{:S(2)}) collective-permute-start(f32[4,64,256]{2,1,0:T(8,128)} %get-tuple-element.16), channel_id=1, source_target_pairs={{0,16},{8,24},{16,0},{24,8},{1,17},{9,25},{17,1},{25,9},{2,18},{10... | collective-permute-start | bytes 786440 | tf_op jit(solution)/shard_map/ppermute | solution.py:15
  215.8 13.8 %collective-permute-start.46 = (f32[4,64,256]{2,1,0:T(8,128)}, f32[4,64,256]{2,1,0:T(8,128)S(1)}, u32[]{:S(2)}, u32[]{:S(2)}) collective-permute-start(f32[4,64,256]{2,1,0:T(8,128)} %get-tuple-element.17), channel_id=1, source_target_pairs={{0,24},{8,16},{16,8},{24,0},{1,25},{9,17},{17,9},{25,1},{2,26},{10... | collective-permute-start | bytes 786440 | tf_op jit(solution)/shard_map/ppermute | solution.py:15
  223.7 33.7 %collective-permute-start.61 = (f32[512]{0:T(512)S(1)}, f32[512]{0:T(512)S(1)}, u32[]{:S(2)}, u32[]{:S(2)}) collective-permute-start(f32[512]{0:T(512)S(1)} %add_add_fusion.4), channel_id=1, source_target_pairs={{0,8},{8,0},{16,24},{24,16},{1,9},{9,1},{17,25},{25,17},{2,10},{10... | collective-permute-start | bytes 6152 | tf_op jit(solution)/shard_map/ppermute | solution.py:15
  223.7 33.7 %collective-permute-start.62 = (f32[512]{0:T(512)S(1)}, f32[512]{0:T(512)S(1)}, u32[]{:S(2)}, u32[]{:S(2)}) collective-permute-start(f32[512]{0:T(512)S(1)} %add_add_fusion.4), channel_id=1, source_target_pairs={{0,16},{8,24},{16,0},{24,8},{1,17},{9,25},{17,1},{25,9},{2,18},{10... | collective-permute-start | bytes 6152 | tf_op jit(solution)/shard_map/ppermute | solution.py:15
  229.6 11.4 %collective-permute-start.52 = (f32[4,64,256]{2,1,0:T(8,128)}, f32[4,64,256]{2,1,0:T(8,128)S(1)}, u32[]{:S(2)}, u32[]{:S(2)}) collective-permute-start(f32[4,64,256]{2,1,0:T(8,128)} %get-tuple-element.21), channel_id=1, source_target_pairs={{0,6},{2,4},{4,2},{6,0},{1,7},{3,5},{5,3},{7,1},{8,14},{10,12},{12... | collective-permute-start | bytes 786440 | tf_op jit(solution)/shard_map/ppermute | solution.py:15
  262.2 11.8 %collective-permute-start.57 = (bf16[16,512]{1,0:T(8,128)(2,1)S(1)}, bf16[16,512]{1,0:T(8,128)(2,1)S(1)}, u32[]{:S(2)}, u32[]{:S(2)}) collective-permute-start(bf16[16,512]{1,0:T(8,128)(2,1)S(1)} %slice_bitcast_fusion.9), channel_id=1, source_target_pairs={{0,32},{32,0},{1,33},{33,1},{2,34},{34,2},{3,35},{35,3},{4,36},{36... | collective-permute-start | bytes 49160 | tf_op jit(solution)/shard_map/ppermute | solution.py:15
  (50 other events, 516.4 us)

commit v2 on v1

v2 whole, which is shorter than its diff:
```python
import jax
import jax.numpy as jnp
from jax import lax
from jax.experimental import pallas as pl
from jax.experimental.pallas import tpu as pltpu
from jax.sharding import Mesh, PartitionSpec as P

AXES = {"zl": 4, "co": 2, "x": 4, "y": 4, "zh": 2}
VMEM_BYTES = 56 * 1024 * 1024
F32 = jnp.float32
BF16 = jnp.bfloat16


def swap(value, axis, flip):
    return lax.ppermute(value, axis, [(i, i ^ flip) for i in range(AXES[axis])])


def swaps(value, axis):
    return [value] + [swap(value, axis, j) for j in range(1, AXES[axis])]


def add_all(parts):
    if len(parts) == 2:
        return parts[0] + parts[1]
    return (parts[0] + parts[1]) + (parts[2] + parts[3])


def in_order(parts, place):
    low = (place & 1) == 1
    if len(parts) == 2:
        return [jnp.where(low, parts[1], parts[0]), jnp.where(low, parts[0], parts[1])]
    high = (place & 2) == 2
    out = []
    for i in range(4):
        out.append(
            jnp.where(
                high,
                jnp.where(low, parts[i ^ 3], parts[i ^ 2]),
                jnp.where(low, parts[i ^ 1], parts[i]),
            )
        )
    return out


def join_stats(parts):
    peak = parts[0][:2]
    for part in parts[1:]:
        peak = jnp.maximum(peak, part[:2])
    sums, divs = [], []
    for part in parts:
        scale = jnp.exp(part[:2] - peak)
        sums.append(part[2:4] * scale)
        divs.append(part[4:5] * scale[1:2])
    rest = add_all([part[5:] for part in parts])
    return jnp.concatenate([peak, add_all(sums), add_all(divs), rest], axis=0)


def logits_kernel(pairing, *refs):
    own, other = refs[0:4], refs[4:8]
    feats, bias, wanted, logits, teacher, stat, x_buf, w_buf, t_buf, sems = refs[8:]
    z, core, x, y, zh = [lax.axis_index(axis) for axis in AXES]
    rows = t_buf.shape[1]
    depth = own[0].shape[0] - rows
    block = feats.shape[2]
    copies = []

    def copy(src, dst):
        made = pltpu.make_async_copy(src, dst, sems.at[len(copies)])
        made.start()
        copies.append(made)

    for j in range(4):
        for pieces, side, place in ((own, core, j), (other, 1 - core, 4 + j)):
            row = pl.multiple_of((2 * (z ^ j) + side) * depth, depth)
            copy(pieces[j].at[pl.ds(0, depth), :], w_buf.at[pl.ds(row, depth), :])
            copy(pieces[j].at[pl.ds(depth, rows), :], t_buf.at[place])
    for j in range(16):
        copy(feats.at[j], x_buf.at[:, pl.ds(j * block, block)])
    for made in copies:
        made.wait()
    cols = logits.shape[0]
    base = (((x * 4 + y) * 2 + zh) * 4 + z) * cols
    step = cols // 2
    for c in range(0, cols, step):
        part = jnp.dot(x_buf[...], w_buf[:, c : c + step], preferred_element_type=F32)
        part = part + bias[:, pl.ds(pl.multiple_of(z * cols + c, step), step)]
        logits[c : c + step, :] = part.T
    values = logits[...]
    peak = jnp.max(values, axis=0, keepdims=True)
    for i in range(4):
        source = jnp.int32(0)
        for s in range(8):
            source = jnp.where(pairing[s] == 2 * i + core, s, source)
        place = ((source >> 1) ^ z) + 4 * ((source & 1) ^ core)
        teacher[:, i * rows : (i + 1) * rows] = t_buf[place].astype(F32).T
    target = teacher[...]
    target_peak = jnp.max(target, axis=0, keepdims=True)
    weight = jnp.exp(target - target_peak)
    ids = base + lax.broadcasted_iota(jnp.int32, values.shape, 0)
    hit = jnp.where(ids == wanted[...], values, 0.0)
    stat[...] = jnp.zeros_like(stat)
    stat[0:1, :] = peak
    stat[1:2, :] = target_peak
    stat[2:3, :] = jnp.sum(jnp.exp(values - peak), axis=0, keepdims=True)
    stat[3:4, :] = jnp.sum(weight, axis=0, keepdims=True)
    stat[4:5, :] = jnp.sum(weight * (target - values), axis=0, keepdims=True)
    stat[5:6, :] = jnp.sum(hit, axis=0, keepdims=True)


def grad_kernel(*refs):
    weights, pieces = refs[0:2], refs[2:6]
    first, second = refs[6:10], refs[10:14]
    w_buf, g_buf, sems = refs[14:]
    z, _, x, y, _ = [lax.axis_index(axis) for axis in AXES]
    quarter = pieces[0].shape[0]
    rows = weights[0].shape[0] // 16
    copies = []

    def copy(src, dst):
        made = pltpu.make_async_copy(src, dst, sems.at[len(copies)])
        made.start()
        copies.append(made)

    for j in range(4):
        row = pl.multiple_of((z ^ j) * quarter, quarter)
        copy(pieces[j], g_buf.at[pl.ds(row, quarter), :])
    for j in range(4):
        for k in range(4):
            row = pl.multiple_of(((x ^ j) * 4 + (y ^ k)) * rows, rows)
            for s in range(2):
                to = ((j * 4 + k) * 2 + s) * rows
                copy(weights[s].at[pl.ds(row, rows), :], w_buf.at[pl.ds(to, rows), :])
    for made in copies:
        made.wait()
    half = g_buf.shape[1] // 2
    group = 8 * rows
    for j in range(4):
        left = w_buf[j * group : (j + 1) * group, :]
        part = jnp.dot(left, g_buf[:, :half], preferred_element_type=F32)
        first[j][...] = part.reshape(first[j].shape)
        part = jnp.dot(left, g_buf[:, half:], preferred_element_type=F32)
        part = part.reshape(first[j].shape)
        for k in range(4):
            second[k][j] = part[k]


def call_logits(pairing, own, other, feats, bias, wanted):
    cols = own[0].shape[1]
    rows, depth = feats.shape[1], 16 * feats.shape[2]
    group = rows // 4
    hbm = pl.BlockSpec(memory_space=pl.ANY)
    vmem = pl.BlockSpec(memory_space=pltpu.VMEM)
    return pl.pallas_call(
        logits_kernel,
        out_shape=(
            jax.ShapeDtypeStruct((cols, rows), F32),
            jax.ShapeDtypeStruct((cols, rows), F32),
            jax.ShapeDtypeStruct((8, rows), F32),
        ),
        in_specs=[pl.BlockSpec(memory_space=pltpu.SMEM)] + [hbm] * 9 + [vmem] * 2,
        out_specs=(vmem, vmem, vmem),
        scratch_shapes=[
            pltpu.VMEM((rows, depth), BF16),
            pltpu.VMEM((depth, cols), BF16),
            pltpu.VMEM((8, group, cols), BF16),
            pltpu.SemaphoreType.DMA((32,)),
        ],
        compiler_params=pltpu.CompilerParams(vmem_limit_bytes=VMEM_BYTES),
        cost_estimate=pl.CostEstimate(
            flops=2 * rows * depth * cols,
            bytes_accessed=2 * depth * (rows + cols),
            transcendentals=rows * cols,
        ),
        name="logits_block",
    )(pairing, *own, *other, feats, bias, wanted)


def call_grad(weights, pieces):
    rows_in, cols = weights[0].shape
    quarter, tokens = pieces[0].shape
    rows = rows_in // 16
    hbm = pl.BlockSpec(memory_space=pl.ANY)
    vmem = pl.BlockSpec(memory_space=pltpu.VMEM)
    out = jax.ShapeDtypeStruct((4, 2 * rows, tokens // 2), F32)
    return pl.pallas_call(
        grad_kernel,
        out_shape=(out,) * 8,
        in_specs=[hbm] * 6,
        out_specs=(vmem,) * 8,
        scratch_shapes=[
            pltpu.VMEM((2 * rows_in, cols), BF16),
            pltpu.VMEM((cols, tokens), BF16),
            pltpu.SemaphoreType.DMA((36,)),
        ],
        compiler_params=pltpu.CompilerParams(vmem_limit_bytes=VMEM_BYTES),
        cost_estimate=pl.CostEstimate(
            flops=4 * rows_in * cols * tokens,
            bytes_accessed=4 * rows_in * cols + 2 * cols * tokens,
            transcendentals=0,
        ),
        name="grad_block",
    )(*weights, *pieces)


def after(value, *others):
    return lax.optimization_barrier((value, *others))[0]


def per_device(teacher_logits, student_hidden, head_weight, head_bias, pairing, targets):
    z, core, x, y, zh = [lax.axis_index(axis) for axis in AXES]
    rows, vocab_cols = teacher_logits.shape
    quarter = vocab_cols // 4
    base = (((x * 4 + y) * 2 + zh) * 4 + z) * quarter
    feats = in_order(swaps(student_hidden, "zh"), zh)
    gathered = swaps(jnp.concatenate(feats, axis=1), "zl")
    wanted = jnp.concatenate(in_order(swaps(after(targets, feats[0]), "zl"), z))[None, :]

    both = jnp.concatenate([head_weight, teacher_logits], axis=0)
    own = [lax.dynamic_slice_in_dim(both, (z ^ j) * quarter, quarter, axis=1) for j in range(4)]
    own[1:] = [swap(after(own[j], gathered[1]), "zl", j) for j in range(1, 4)]
    other = [swap(part, "co", 1) for part in own]

    feats = after(jnp.concatenate(in_order(gathered, z), axis=0), wanted)
    feats = lax.all_to_all(jnp.broadcast_to(feats, (16, *feats.shape)), ("x", "y"), 0, 0, tiled=True)
    logits, teacher, stat = call_logits(pairing, own, other, feats, head_bias[None, :], wanted)

    for axis, place in (("x", x), ("y", y), ("zl", z), ("zh", zh)):
        stat = join_stats(in_order(swaps(stat, axis), place))
    student_lse = stat[0:1] + jnp.log(stat[2:3])
    teacher_lse = stat[1:2] + jnp.log(stat[3:4])
    loss = stat[4:5] / stat[3:4] - teacher_lse + 2.0 * student_lse - stat[5:6]
    row_loss = lax.dynamic_slice_in_dim(loss[0], z * rows, rows)

    target_prob = jnp.exp(teacher - teacher_lse)
    ids = base + lax.broadcasted_iota(jnp.int32, logits.shape, 0)
    onehot = (ids == wanted).astype(F32)
    grad = (2.0 * jnp.exp(logits - student_lse) - target_prob - onehot).astype(BF16)

    other_weight = swap(after(head_weight, grad), "co", 1)
    first = call_grad((head_weight, other_weight), swaps(grad, "zl"))
    first, second = first[:4], first[4:]
    first = add_all([first[0]] + [swap(first[j], "x", j) for j in range(1, 4)])
    second = add_all([second[0]] + [swap(second[j], "y", j) for j in range(1, 4)])
    first = add_all([first[0]] + [swap(first[j], "y", j) for j in range(1, 4)])
    second = add_all([second[0]] + [swap(second[j], "x", j) for j in range(1, 4)])
    total = jnp.concatenate([first, second], axis=1)
    share = head_weight.shape[0] // 32
    total = total.reshape(2, 2, share, total.shape[1])
    mine = jnp.where(zh == 0, total[:, 0], total[:, 1])
    theirs = jnp.where(zh == 0, total[:, 1], total[:, 0])
    total = (mine + swap(theirs, "zh", 1)).astype(BF16)
    sides = in_order([total[0], swap(total[1], "co", 1)], core)
    sides = [side.reshape(share, 4, rows) for side in sides]
    hidden_grad = jnp.stack(sides, axis=2).reshape(share, 8 * rows)
    return hidden_grad, row_loss


def solution(mesh):
    fine = Mesh(mesh.devices.reshape(tuple(AXES.values())), tuple(AXES))
    pair, vocab = ("zl", "co"), ("x", "y", "zh")
    return jax.shard_map(
        per_device,
        mesh=fine,
        in_specs=(P(pair, vocab), P(pair, vocab), P(pair, vocab), P(vocab), P(), P(pair)),
        out_specs=(P(pair + vocab, None), P(pair)),
        check_vma=False,
    )
```

time: 280 us -> 237 us (0.85); the launches traced: 275 us -> 236 us
  starting transfers between devices: 110 us -> 69.9 us
  waiting for transfers between devices: 121 us -> 135 us
  between operations: 6.5 us -> 1.06 us
  local copies, waits for them, and re-layouts: 11.1 us -> 7.78 us
  other arithmetic: 11 us -> 7.81 us
    ppermute x68 -> x42, starting transfers between devices: 110 us -> 62.7 us  [swap(): return lax.ppermute(value, axis, [(i, i ^ flip) for i in range(AXES[axis])])]
    ppermute x68 -> x42, waiting for transfers between devices: 121 us -> 135 us  [swap(): return lax.ppermute(value, axis, [(i, i ^ flip) for i in range(AXES[axis])])]
    all_to_all x0 -> x1, starting transfers between devices: none -> 7.22 us  [per_device(): lax.all_to_all(jnp.broadcast_to(feats, (16, *feats.shape)), ('x', 'y'), 0...]
    dynamic_slice x9 -> x1, local copies, waits for them, and re-layouts: 7.42 us -> 0.32 us  [per_device(): lax.dynamic_slice_in_dim(both, (z ^ j) * quarter, quarter, axis=1)]
    another operation x6 -> x0, other arithmetic: 3.51 us -> none  [the longest x2 1.73 us: per_device(): first = jnp.stack(swaps(jnp.concatenate(feats[:2], axis=0), 'y'))]
    reduce_sum x3 -> x0, other arithmetic: 2.82 us -> none  [the longest x1 1.84 us: per_device(): jnp.sum(target_prob * (log_target - log_student) - jnp.where(onehot, logi...]
  transfers between devices with their start and end apart: 68 -> 43, of which waited for: 27 -> 25; matrix products, arithmetic and copies ran while one was open for 7% -> 2% of each run, Pallas kernels for 0% -> 0%
where the time goes in v2:
time: 237 us; the launch traced here: 236 us
  waiting for transfers between devices  135 us (57%)
  starting transfers between devices  69.9 us (29%)
  Pallas kernels  15.1 us (6%)
  other arithmetic  7.81 us (3%)
  local copies, waits for them, and re-layouts  7.78 us (3%)
    ppermute x42, waiting for transfers between devices, swap(): return lax.ppermute(value, axis, [(i, i ^ flip) for i in range(AXES[axis])])  135 us
    ppermute x42, starting transfers between devices, swap(): return lax.ppermute(value, axis, [(i, i ^ flip) for i in range(AXES[axis])])  62.7 us
    pallas_call x1, Pallas kernels, call_logits(): pl.pallas_call(logits_kernel, out_shape=(jax.ShapeDtypeStruct((cols, rows...  8.68 us
    all_to_all x1, starting transfers between devices, per_device(): lax.all_to_all(jnp.broadcast_to(feats, (16, *feats.shape)), ('x', 'y'), 0...  7.22 us
    pallas_call x1, Pallas kernels, call_grad(): pl.pallas_call(grad_kernel, out_shape=(out,) * 8, in_specs=[hbm] * 6, out...  6.42 us
  transfers between devices with their start and end apart: 43, of which 25 were waited for; matrix products, arithmetic and copies ran while one was open for 2% of the time, Pallas kernels for 0%

profile of v2, /device:TPU:32, one launch (start us, length us, event | category | flops | bytes accessed | tf_op | source)
XLA Modules:
  0.0 236.4 jit_solution(7320871548657269055)
XLA Ops:
  0.6 6.4 %collective-permute-start = (bf16[128,128]{1,0:T(8,128)(2,1)}, bf16[128,128]{1,0:T(8,128)(2,1)S(1)}, u32[]{:S(2)}, u32[]{:S(2)}) collective-permute-start(bf16[128,128]{1,0:T(8,128)(2,1)} %param.7), channel_id=1, source_target_pairs={{0,1},{1,0},{2,3},{3,2},{4,5},{5,4},{6,7},{7,6},{8,9},{9,8},{10,11... | collective-permute-start | bytes 98312 | tf_op jit(solution)/shard_map/ppermute | solution.py:15
  7.0 2.1 collective-permute-done
  11.5 2.2 collective-permute-start.12
  22.3 2.4 %broadcast_in_dim.10 = bf16[16,512,256]{2,1,0:T(8,128)(2,1)} broadcast(bf16[512,256]{1,0:T(8,128)(2,1)S(1)} %pad_maximum_fusion), dimensions={1,2} | broadcast | bytes 4456448 | tf_op jit(solution)/shard_map/broadcast_in_dim | solution.py:224
  24.7 7.2 %all-to-all-start = ((bf16[16,512,256]{2,1,0:T(8,128)(2,1)}), bf16[16,512,256]{2,1,0:T(8,128)(2,1)}, u32[]{:S(2)}, u32[]{:S(2)}) async-start(bf16[16,512,256]{2,1,0:T(8,128)(2,1)} %broadcast_in_dim.10), calls=%async_computation | async-start | bytes 8388608 | tf_op jit(solution)/shard_map/all_to_all | solution.py:224
  33.4 2.6 %collective-permute-start.3 = (bf16[640,512]{1,0:T(8,128)(2,1)S(1)}, bf16[640,512]{1,0:T(8,128)(2,1)S(1)}, u32[]{:S(2)}, u32[]{:S(2)}) collective-permute-start(bf16[640,512]{1,0:T(8,128)(2,1)S(1)} %get-tuple-element.20), channel_id=1, source_target_pairs={{0,128},{64,192},{128,0},{192,64},{1,129},{65,193},{129,1},{193,65... | collective-permute-start | bytes 1966088 | tf_op jit(solution)/shard_map/ppermute | solution.py:15
  36.0 2.1 collective-permute-start.4
  38.1 37.0 %collective-permute-done.3.refs_2_ = bf16[640,512]{1,0:T(8,128)(2,1)S(1)} collective-permute-done((bf16[640,512]{1,0:T(8,128)(2,1)S(1)}, bf16[640,512]{1,0:T(8,128)(2,1)S(1)}, u32[]{:S(2)}, u32[]{:S(2)}) %collective-permute-start.3) | collective-permute-done | bytes 655392 | tf_op jit(solution)/shard_map/ppermute | solution.py:15
  75.1 14.8 %collective-permute-done.4.refs_3_ = bf16[640,512]{1,0:T(8,128)(2,1)S(1)} collective-permute-done((bf16[640,512]{1,0:T(8,128)(2,1)S(1)}, bf16[640,512]{1,0:T(8,128)(2,1)S(1)}, u32[]{:S(2)}, u32[]{:S(2)}) %collective-permute-start.4) | collective-permute-done | bytes 655392 | tf_op jit(solution)/shard_map/ppermute | solution.py:15
  93.1 8.7 %logits_block.1 = (f32[512,512]{1,0:T(8,128)}, f32[512,512]{1,0:T(8,128)}, f32[8,512]{1,0:T(8,128)}) custom-call(s32[8]{0:T(128)} %pairing.1, bf16[640,512]{1,0:T(8,128)(2,1)} %copy-done, bf16[640,512]{1,0:T(8,128)(2,1)} %copy-done.4, bf16[640,512]{1,0:T(8,128)(2,1)} %copy-done.2, bf16[640,512]{1,0:T(8,128)(2,1)} %copy-done.3, bf16[640,512]{1,0:T(8,128)(2,1)} %copy-done.5, ...), custom_call_target="tpu_custom_call" | custom-call | flops 2147483648 | bytes 8388608 | tf_op jit(solution)/shard_map/logits_block/pallas_call | solution.py:153
  101.8 2.9 %collective-permute-start.14 = (f32[8,512]{1,0:T(8,128)}, f32[8,512]{1,0:T(8,128)S(1)}, u32[]{:S(2)}, u32[]{:S(2)}) collective-permute-start(f32[8,512]{1,0:T(8,128)} %get-tuple-element.25), channel_id=1, source_target_pairs={{0,24},{8,16},{16,8},{24,0},{1,25},{9,17},{17,9},{25,1},{2,26},{10... | collective-permute-start | bytes 49160 | tf_op jit(solution)/shard_map/ppermute | solution.py:15
  107.0 3.1 %collective-permute-done.15 = f32[8,512]{1,0:T(8,128)S(1)} collective-permute-done((f32[8,512]{1,0:T(8,128)}, f32[8,512]{1,0:T(8,128)S(1)}, u32[]{:S(2)}, u32[]{:S(2)}) %collective-permute-start.15) | collective-permute-done | bytes 16416 | tf_op jit(solution)/shard_map/ppermute | solution.py:15
  111.0 2.8 %collective-permute-start.17 = (f32[8,512]{1,0:T(8,128)S(1)}, f32[8,512]{1,0:T(8,128)S(1)}, u32[]{:S(2)}, u32[]{:S(2)}) collective-permute-start(f32[8,512]{1,0:T(8,128)S(1)} %pad_maximum_fusion.4), channel_id=1, source_target_pairs={{0,6},{2,4},{4,2},{6,0},{1,7},{3,5},{5,3},{7,1},{8,14},{10,12},{12... | collective-permute-start | bytes 49160 | tf_op jit(solution)/shard_map/ppermute | solution.py:15
  116.0 3.0 %collective-permute-done.18 = f32[8,512]{1,0:T(8,128)S(1)} collective-permute-done((f32[8,512]{1,0:T(8,128)S(1)}, f32[8,512]{1,0:T(8,128)S(1)}, u32[]{:S(2)}, u32[]{:S(2)}) %collective-permute-start.18) | collective-permute-done | bytes 16416 | tf_op jit(solution)/shard_map/ppermute | solution.py:15
  122.9 2.6 %collective-permute-done.21 = f32[8,512]{1,0:T(8,128)S(1)} collective-permute-done((f32[8,512]{1,0:T(8,128)S(1)}, f32[8,512]{1,0:T(8,128)S(1)}, u32[]{:S(2)}, u32[]{:S(2)}) %collective-permute-start.21) | collective-permute-done | bytes 16416 | tf_op jit(solution)/shard_map/ppermute | solution.py:15
  125.6 4.3 %collective-permute-start.23 = (f32[8,512]{1,0:T(8,128)S(1)}, f32[8,512]{1,0:T(8,128)S(1)}, u32[]{:S(2)}, u32[]{:S(2)}) collective-permute-start(f32[8,512]{1,0:T(8,128)S(1)} %pad_maximum_fusion.6), channel_id=1, source_target_pairs={{0,1},{1,0},{2,3},{3,2},{4,5},{5,4},{6,7},{7,6},{8,9},{9,8},{10,11... | collective-permute-start | bytes 49160 | tf_op jit(solution)/shard_map/ppermute | solution.py:15
  129.9 3.4 %collective-permute-done.23 = f32[8,512]{1,0:T(8,128)S(1)} collective-permute-done((f32[8,512]{1,0:T(8,128)S(1)}, f32[8,512]{1,0:T(8,128)S(1)}, u32[]{:S(2)}, u32[]{:S(2)}) %collective-permute-start.23) | collective-permute-done | bytes 16416 | tf_op jit(solution)/shard_map/ppermute | solution.py:15
  133.4 1.9 subtract_convert_fusion.refs_2_
  139.0 19.6 %collective-permute-done.25.refs_3_ = bf16[512,512]{1,0:T(8,128)(2,1)S(1)} collective-permute-done((bf16[512,512]{1,0:T(8,128)(2,1)S(1)}, bf16[512,512]{1,0:T(8,128)(2,1)S(1)}, u32[]{:S(2)}, u32[]{:S(2)}) %collective-permute-start.25) | collective-permute-done | bytes 524320 | tf_op jit(solution)/shard_map/ppermute | solution.py:15
  158.6 13.9 %collective-permute-done.26.refs_4_ = bf16[512,512]{1,0:T(8,128)(2,1)S(1)} collective-permute-done((bf16[512,512]{1,0:T(8,128)(2,1)S(1)}, bf16[512,512]{1,0:T(8,128)(2,1)S(1)}, u32[]{:S(2)}, u32[]{:S(2)}) %collective-permute-start.26) | collective-permute-done | bytes 524320 | tf_op jit(solution)/shard_map/ppermute | solution.py:15
  172.5 12.2 %collective-permute-done.27.refs_5_ = bf16[512,512]{1,0:T(8,128)(2,1)S(1)} collective-permute-done((bf16[512,512]{1,0:T(8,128)(2,1)S(1)}, bf16[512,512]{1,0:T(8,128)(2,1)S(1)}, u32[]{:S(2)}, u32[]{:S(2)}) %collective-permute-start.27) | collective-permute-done | bytes 524320 | tf_op jit(solution)/shard_map/ppermute | solution.py:15
  186.8 6.4 %grad_block.1 = (f32[4,64,256]{2,1,0:T(8,128)}, f32[4,64,256]{2,1,0:T(8,128)}, f32[4,64,256]{2,1,0:T(8,128)}, f32[4,64,256]{2,1,0:T(8,128)}, f32[4,64,256]{2,1,0...) custom-call(bf16[512,2048]{1,0:T(8,128)(2,1)} %refs_0_.1, ...), custom_call_target="tpu_custom_call" | custom-call | flops 2147483648 | bytes 6291456 | tf_op jit(solution)/shard_map/grad_block/pallas_call | solution.py:185
  193.6 2.6 %collective-permute-start.29 = (f32[4,64,256]{2,1,0:T(8,128)}, f32[4,64,256]{2,1,0:T(8,128)S(1)}, u32[]{:S(2)}, u32[]{:S(2)}) collective-permute-start(f32[4,64,256]{2,1,0:T(8,128)} %get-tuple-element.30), channel_id=1, source_target_pairs={{0,16},{8,24},{16,0},{24,8},{1,17},{9,25},{17,1},{25,9},{2,18},{10... | collective-permute-start | bytes 786440 | tf_op jit(solution)/shard_map/ppermute | solution.py:15
  198.3 2.6 %collective-permute-start.35 = (f32[4,64,256]{2,1,0:T(8,128)}, f32[4,64,256]{2,1,0:T(8,128)S(1)}, u32[]{:S(2)}, u32[]{:S(2)}) collective-permute-start(f32[4,64,256]{2,1,0:T(8,128)} %get-tuple-element.34), channel_id=1, source_target_pairs={{0,4},{2,6},{4,0},{6,2},{1,5},{3,7},{5,1},{7,3},{8,12},{10,14},{12... | collective-permute-start | bytes 786440 | tf_op jit(solution)/shard_map/ppermute | solution.py:15
  200.9 1.9 collective-permute-done.28
  204.2 3.4 %collective-permute-done.29 = f32[4,64,256]{2,1,0:T(8,128)S(1)} collective-permute-done((f32[4,64,256]{2,1,0:T(8,128)}, f32[4,64,256]{2,1,0:T(8,128)S(1)}, u32[]{:S(2)}, u32[]{:S(2)}) %collective-permute-start.29) | collective-permute-done | bytes 262176 | tf_op jit(solution)/shard_map/ppermute | solution.py:15
  207.7 2.6 %collective-permute-done.30 = f32[4,64,256]{2,1,0:T(8,128)S(1)} collective-permute-done((f32[4,64,256]{2,1,0:T(8,128)}, f32[4,64,256]{2,1,0:T(8,128)S(1)}, u32[]{:S(2)}, u32[]{:S(2)}) %collective-permute-start.30) | collective-permute-done | bytes 262176 | tf_op jit(solution)/shard_map/ppermute | solution.py:15
  211.6 2.6 %collective-permute-start.32 = (f32[64,256]{1,0:T(8,128)S(1)}, f32[64,256]{1,0:T(8,128)S(1)}, u32[]{:S(2)}, u32[]{:S(2)}) collective-permute-start(f32[64,256]{1,0:T(8,128)S(1)} %get-tuple-element.63), channel_id=1, source_target_pairs={{0,4},{2,6},{4,0},{6,2},{1,5},{3,7},{5,1},{7,3},{8,12},{10,14},{12... | collective-permute-start | bytes 196616 | tf_op jit(solution)/shard_map/ppermute | solution.py:15
  217.2 3.3 %collective-permute-start.38 = (f32[64,256]{1,0:T(8,128)S(1)}, f32[64,256]{1,0:T(8,128)S(1)}, u32[]{:S(2)}, u32[]{:S(2)}) collective-permute-start(f32[64,256]{1,0:T(8,128)S(1)} %get-tuple-element.66), channel_id=1, source_target_pairs={{0,16},{8,24},{16,0},{24,8},{1,17},{9,25},{17,1},{25,9},{2,18},{10... | collective-permute-start | bytes 196616 | tf_op jit(solution)/shard_map/ppermute | solution.py:15
  223.4 2.5 %collective-permute-done.39 = f32[64,256]{1,0:T(8,128)S(1)} collective-permute-done((f32[64,256]{1,0:T(8,128)S(1)}, f32[64,256]{1,0:T(8,128)S(1)}, u32[]{:S(2)}, u32[]{:S(2)}) %collective-permute-start.39) | collective-permute-done | bytes 65568 | tf_op jit(solution)/shard_map/ppermute | solution.py:15
  226.0 4.4 %collective-permute-start.40 = (f32[2,16,512]{2,1,0:T(8,128)S(1)}, f32[2,16,512]{2,1,0:T(8,128)S(1)}, u32[]{:S(2)}, u32[]{:S(2)}) collective-permute-start(f32[2,16,512]{2,1,0:T(8,128)S(1)} %select_bitcast_fusion), channel_id=1, source_target_pairs={{0,1},{1,0},{2,3},{3,2},{4,5},{5,4},{6,7},{7,6},{8,9},{9,8},{10,11... | collective-permute-start | bytes 196616 | tf_op jit(solution)/shard_map/ppermute | solution.py:15
  230.5 3.8 %collective-permute-done.40 = f32[2,16,512]{2,1,0:T(8,128)S(1)} collective-permute-done((f32[2,16,512]{2,1,0:T(8,128)S(1)}, f32[2,16,512]{2,1,0:T(8,128)S(1)}, u32[]{:S(2)}, u32[]{:S(2)}) %collective-permute-start.40) | collective-permute-done | bytes 65568 | tf_op jit(solution)/shard_map/ppermute | solution.py:15
  (135 shorter events, 43.9 us)
Async XLA Ops:
  0.6 8.5 %collective-permute-start = (bf16[128,128]{1,0:T(8,128)(2,1)}, bf16[128,128]{1,0:T(8,128)(2,1)S(1)}, u32[]{:S(2)}, u32[]{:S(2)}) collective-permute-start(bf16[128,128]{1,0:T(8,128)(2,1)} %param.7), channel_id=1, source_target_pairs={{0,1},{1,0},{2,3},{3,2},{4,5},{5,4},{6,7},{7,6},{8,9},{9,8},{10,11... | collective-permute-start | bytes 98312 | tf_op jit(solution)/shard_map/ppermute | solution.py:15
  9.9 7.5 %collective-permute-start.11 = (s32[128]{0:T(128)}, s32[128]{0:T(128)S(1)}, u32[]{:S(2)}, u32[]{:S(2)}) collective-permute-start(s32[128]{0:T(128)} %param.11), channel_id=1, source_target_pairs={{0,192},{64,128},{128,64},{192,0},{1,193},{65,129},{129,65},{193,1... | collective-permute-start | bytes 1544 | tf_op jit(solution)/shard_map/ppermute | solution.py:15
  11.5 6.3 %collective-permute-start.12 = (s32[128]{0:T(128)}, s32[128]{0:T(128)S(1)}, u32[]{:S(2)}, u32[]{:S(2)}) collective-permute-start(s32[128]{0:T(128)} %param.11), channel_id=1, source_target_pairs={{0,128},{64,192},{128,0},{192,64},{1,129},{65,193},{129,1},{193,65... | collective-permute-start | bytes 1544 | tf_op jit(solution)/shard_map/ppermute | solution.py:15
  14.3 5.0 %collective-permute-start.1 = (bf16[128,256]{1,0:T(8,128)(2,1)S(1)}, bf16[128,256]{1,0:T(8,128)(2,1)S(1)}, u32[]{:S(2)}, u32[]{:S(2)}) collective-permute-start(bf16[128,256]{1,0:T(8,128)(2,1)S(1)} %pad_maximum_fusion.2), channel_id=1, source_target_pairs={{0,64},{64,0},{128,192},{192,128},{1,65},{65,1},{129,193},{193,129... | collective-permute-start | bytes 196616 | tf_op jit(solution)/shard_map/ppermute | solution.py:15
  15.8 5.2 %collective-permute-start.10 = (bf16[128,256]{1,0:T(8,128)(2,1)S(1)}, bf16[128,256]{1,0:T(8,128)(2,1)S(1)}, u32[]{:S(2)}, u32[]{:S(2)}) collective-permute-start(bf16[128,256]{1,0:T(8,128)(2,1)S(1)} %pad_maximum_fusion.2), channel_id=1, source_target_pairs={{0,128},{64,192},{128,0},{192,64},{1,129},{65,193},{129,1},{193,65... | collective-permute-start | bytes 196616 | tf_op jit(solution)/shard_map/ppermute | solution.py:15
  24.7 68.3 %all-to-all-start = ((bf16[16,512,256]{2,1,0:T(8,128)(2,1)}), bf16[16,512,256]{2,1,0:T(8,128)(2,1)}, u32[]{:S(2)}, u32[]{:S(2)}) async-start(bf16[16,512,256]{2,1,0:T(8,128)(2,1)} %broadcast_in_dim.10), calls=%async_computation | async-start | bytes 8388608 | tf_op jit(solution)/shard_map/all_to_all | solution.py:224
  33.4 41.8 %collective-permute-start.3 = (bf16[640,512]{1,0:T(8,128)(2,1)S(1)}, bf16[640,512]{1,0:T(8,128)(2,1)S(1)}, u32[]{:S(2)}, u32[]{:S(2)}) collective-permute-start(bf16[640,512]{1,0:T(8,128)(2,1)S(1)} %get-tuple-element.20), channel_id=1, source_target_pairs={{0,128},{64,192},{128,0},{192,64},{1,129},{65,193},{129,1},{193,65... | collective-permute-start | bytes 1966088 | tf_op jit(solution)/shard_map/ppermute | solution.py:15
  36.0 53.9 %collective-permute-start.4 = (bf16[640,512]{1,0:T(8,128)(2,1)S(1)}, bf16[640,512]{1,0:T(8,128)(2,1)S(1)}, u32[]{:S(2)}, u32[]{:S(2)}) collective-permute-start(bf16[640,512]{1,0:T(8,128)(2,1)S(1)} %get-tuple-element.21), channel_id=1, source_target_pairs={{0,192},{64,128},{128,64},{192,0},{1,193},{65,129},{129,65},{193,1... | collective-permute-start | bytes 1966088 | tf_op jit(solution)/shard_map/ppermute | solution.py:15
  38.1 51.8 %collective-permute-start.2 = (bf16[640,512]{1,0:T(8,128)(2,1)S(1)}, bf16[640,512]{1,0:T(8,128)(2,1)S(1)}, u32[]{:S(2)}, u32[]{:S(2)}) collective-permute-start(bf16[640,512]{1,0:T(8,128)(2,1)S(1)} %get-tuple-element.19), channel_id=1, source_target_pairs={{0,64},{64,0},{128,192},{192,128},{1,65},{65,1},{129,193},{193,129... | collective-permute-start | bytes 1966088 | tf_op jit(solution)/shard_map/ppermute | solution.py:15
  38.1 52.3 %collective-permute-start.5 = (bf16[640,512]{1,0:T(8,128)(2,1)S(1)}, bf16[640,512]{1,0:T(8,128)(2,1)S(1)}, u32[]{:S(2)}, u32[]{:S(2)}) collective-permute-start(bf16[640,512]{1,0:T(8,128)(2,1)S(1)} %get-tuple-element.61.refs_0_), channel_id=1, source_target_pairs={{0,32},{32,0},{1,33},{33,1},{2,34},{34,2},{3,35},{35,3},{4,36},{36... | collective-permute-start | bytes 1966088 | tf_op jit(solution)/shard_map/ppermute | solution.py:15
  75.1 15.3 %collective-permute-start.7 = (bf16[640,512]{1,0:T(8,128)(2,1)S(1)}, bf16[640,512]{1,0:T(8,128)(2,1)S(1)}, u32[]{:S(2)}, u32[]{:S(2)}) collective-permute-start(bf16[640,512]{1,0:T(8,128)(2,1)S(1)} %collective-permute-done.3.refs_2_), channel_id=1, source_target_pairs={{0,32},{32,0},{1,33},{33,1},{2,34},{34,2},{3,35},{35,3},{4,36},{36... | collective-permute-start | bytes 1966088 | tf_op jit(solution)/shard_map/ppermute | solution.py:15
  101.8 5.2 %collective-permute-start.14 = (f32[8,512]{1,0:T(8,128)}, f32[8,512]{1,0:T(8,128)S(1)}, u32[]{:S(2)}, u32[]{:S(2)}) collective-permute-start(f32[8,512]{1,0:T(8,128)} %get-tuple-element.25), channel_id=1, source_target_pairs={{0,24},{8,16},{16,8},{24,0},{1,25},{9,17},{17,9},{25,1},{2,26},{10... | collective-permute-start | bytes 49160 | tf_op jit(solution)/shard_map/ppermute | solution.py:15
  104.7 5.5 %collective-permute-start.15 = (f32[8,512]{1,0:T(8,128)}, f32[8,512]{1,0:T(8,128)S(1)}, u32[]{:S(2)}, u32[]{:S(2)}) collective-permute-start(f32[8,512]{1,0:T(8,128)} %get-tuple-element.25), channel_id=1, source_target_pairs={{0,16},{8,24},{16,0},{24,8},{1,17},{9,25},{17,1},{25,9},{2,18},{10... | collective-permute-start | bytes 49160 | tf_op jit(solution)/shard_map/ppermute | solution.py:15
  111.0 5.0 %collective-permute-start.17 = (f32[8,512]{1,0:T(8,128)S(1)}, f32[8,512]{1,0:T(8,128)S(1)}, u32[]{:S(2)}, u32[]{:S(2)}) collective-permute-start(f32[8,512]{1,0:T(8,128)S(1)} %pad_maximum_fusion.4), channel_id=1, source_target_pairs={{0,6},{2,4},{4,2},{6,0},{1,7},{3,5},{5,3},{7,1},{8,14},{10,12},{12... | collective-permute-start | bytes 49160 | tf_op jit(solution)/shard_map/ppermute | solution.py:15
  113.7 5.2 %collective-permute-start.18 = (f32[8,512]{1,0:T(8,128)S(1)}, f32[8,512]{1,0:T(8,128)S(1)}, u32[]{:S(2)}, u32[]{:S(2)}) collective-permute-start(f32[8,512]{1,0:T(8,128)S(1)} %pad_maximum_fusion.4), channel_id=1, source_target_pairs={{0,4},{2,6},{4,0},{6,2},{1,5},{3,7},{5,1},{7,3},{8,12},{10,14},{12... | collective-permute-start | bytes 49160 | tf_op jit(solution)/shard_map/ppermute | solution.py:15
  125.6 7.7 %collective-permute-start.23 = (f32[8,512]{1,0:T(8,128)S(1)}, f32[8,512]{1,0:T(8,128)S(1)}, u32[]{:S(2)}, u32[]{:S(2)}) collective-permute-start(f32[8,512]{1,0:T(8,128)S(1)} %pad_maximum_fusion.6), channel_id=1, source_target_pairs={{0,1},{1,0},{2,3},{3,2},{4,5},{5,4},{6,7},{7,6},{8,9},{9,8},{10,11... | collective-permute-start | bytes 49160 | tf_op jit(solution)/shard_map/ppermute | solution.py:15
  135.3 49.4 %collective-permute-start.24 = (bf16[512,2048]{1,0:T(8,128)(2,1)S(1)}, bf16[512,2048]{1,0:T(8,128)(2,1)S(1)}, u32[]{:S(2)}, u32[]{:S(2)}) collective-permute-start(bf16[512,2048]{1,0:T(8,128)(2,1)S(1)} %copy-done.1), channel_id=1, source_target_pairs={{0,32},{32,0},{1,33},{33,1},{2,34},{34,2},{3,35},{35,3},{4,36},{36... | collective-permute-start | bytes 6291464 | tf_op jit(solution)/shard_map/ppermute | solution.py:15
  135.4 23.1 %collective-permute-start.25 = (bf16[512,512]{1,0:T(8,128)(2,1)S(1)}, bf16[512,512]{1,0:T(8,128)(2,1)S(1)}, u32[]{:S(2)}, u32[]{:S(2)}) collective-permute-start(bf16[512,512]{1,0:T(8,128)(2,1)S(1)} %subtract_convert_fusion.refs_2_), channel_id=1, source_target_pairs={{0,64},{64,0},{128,192},{192,128},{1,65},{65,1},{129,193},{193,129... | collective-permute-start | bytes 1572872 | tf_op jit(solution)/shard_map/ppermute | solution.py:15
  136.4 36.1 %collective-permute-start.26 = (bf16[512,512]{1,0:T(8,128)(2,1)S(1)}, bf16[512,512]{1,0:T(8,128)(2,1)S(1)}, u32[]{:S(2)}, u32[]{:S(2)}) collective-permute-start(bf16[512,512]{1,0:T(8,128)(2,1)S(1)} %subtract_convert_fusion.refs_2_), channel_id=1, source_target_pairs={{0,128},{64,192},{128,0},{192,64},{1,129},{65,193},{129,1},{193,65... | collective-permute-start | bytes 1572872 | tf_op jit(solution)/shard_map/ppermute | solution.py:15
  137.7 47.0 %collective-permute-start.27 = (bf16[512,512]{1,0:T(8,128)(2,1)S(1)}, bf16[512,512]{1,0:T(8,128)(2,1)S(1)}, u32[]{:S(2)}, u32[]{:S(2)}) collective-permute-start(bf16[512,512]{1,0:T(8,128)(2,1)S(1)} %subtract_convert_fusion.refs_2_), channel_id=1, source_target_pairs={{0,192},{64,128},{128,64},{192,0},{1,193},{65,129},{129,65},{193,1... | collective-permute-start | bytes 1572872 | tf_op jit(solution)/shard_map/ppermute | solution.py:15
  193.3 9.5 %collective-permute-start.28 = (f32[4,64,256]{2,1,0:T(8,128)}, f32[4,64,256]{2,1,0:T(8,128)S(1)}, u32[]{:S(2)}, u32[]{:S(2)}) collective-permute-start(f32[4,64,256]{2,1,0:T(8,128)} %get-tuple-element.29), channel_id=1, source_target_pairs={{0,8},{8,0},{16,24},{24,16},{1,9},{9,1},{17,25},{25,17},{2,10},{10... | collective-permute-start | bytes 786440 | tf_op jit(solution)/shard_map/ppermute | solution.py:15
  193.6 14.1 %collective-permute-start.29 = (f32[4,64,256]{2,1,0:T(8,128)}, f32[4,64,256]{2,1,0:T(8,128)S(1)}, u32[]{:S(2)}, u32[]{:S(2)}) collective-permute-start(f32[4,64,256]{2,1,0:T(8,128)} %get-tuple-element.30), channel_id=1, source_target_pairs={{0,16},{8,24},{16,0},{24,8},{1,17},{9,25},{17,1},{25,9},{2,18},{10... | collective-permute-start | bytes 786440 | tf_op jit(solution)/shard_map/ppermute | solution.py:15
  196.2 14.0 %collective-permute-start.30 = (f32[4,64,256]{2,1,0:T(8,128)}, f32[4,64,256]{2,1,0:T(8,128)S(1)}, u32[]{:S(2)}, u32[]{:S(2)}) collective-permute-start(f32[4,64,256]{2,1,0:T(8,128)} %get-tuple-element.31), channel_id=1, source_target_pairs={{0,24},{8,16},{16,8},{24,0},{1,25},{9,17},{17,9},{25,1},{2,26},{10... | collective-permute-start | bytes 786440 | tf_op jit(solution)/shard_map/ppermute | solution.py:15
  198.0 16.2 %collective-permute-start.34 = (f32[4,64,256]{2,1,0:T(8,128)}, f32[4,64,256]{2,1,0:T(8,128)S(1)}, u32[]{:S(2)}, u32[]{:S(2)}) collective-permute-start(f32[4,64,256]{2,1,0:T(8,128)} %get-tuple-element.33), channel_id=1, source_target_pairs={{0,2},{2,0},{4,6},{6,4},{1,3},{3,1},{5,7},{7,5},{8,10},{10,8},{12,... | collective-permute-start | bytes 786440 | tf_op jit(solution)/shard_map/ppermute | solution.py:15
  198.3 17.8 %collective-permute-start.35 = (f32[4,64,256]{2,1,0:T(8,128)}, f32[4,64,256]{2,1,0:T(8,128)S(1)}, u32[]{:S(2)}, u32[]{:S(2)}) collective-permute-start(f32[4,64,256]{2,1,0:T(8,128)} %get-tuple-element.34), channel_id=1, source_target_pairs={{0,4},{2,6},{4,0},{6,2},{1,5},{3,7},{5,1},{7,3},{8,12},{10,14},{12... | collective-permute-start | bytes 786440 | tf_op jit(solution)/shard_map/ppermute | solution.py:15
  202.8 13.3 %collective-permute-start.36 = (f32[4,64,256]{2,1,0:T(8,128)}, f32[4,64,256]{2,1,0:T(8,128)S(1)}, u32[]{:S(2)}, u32[]{:S(2)}) collective-permute-start(f32[4,64,256]{2,1,0:T(8,128)} %get-tuple-element.35), channel_id=1, source_target_pairs={{0,6},{2,4},{4,2},{6,0},{1,7},{3,5},{5,3},{7,1},{8,14},{10,12},{12... | collective-permute-start | bytes 786440 | tf_op jit(solution)/shard_map/ppermute | solution.py:15
  211.3 9.2 %collective-permute-start.31 = (f32[64,256]{1,0:T(8,128)S(1)}, f32[64,256]{1,0:T(8,128)S(1)}, u32[]{:S(2)}, u32[]{:S(2)}) collective-permute-start(f32[64,256]{1,0:T(8,128)S(1)} %get-tuple-element.64), channel_id=1, source_target_pairs={{0,2},{2,0},{4,6},{6,4},{1,3},{3,1},{5,7},{7,5},{8,10},{10,8},{12,... | collective-permute-start | bytes 196616 | tf_op jit(solution)/shard_map/ppermute | solution.py:15
  211.6 10.3 %collective-permute-start.32 = (f32[64,256]{1,0:T(8,128)S(1)}, f32[64,256]{1,0:T(8,128)S(1)}, u32[]{:S(2)}, u32[]{:S(2)}) collective-permute-start(f32[64,256]{1,0:T(8,128)S(1)} %get-tuple-element.63), channel_id=1, source_target_pairs={{0,4},{2,6},{4,0},{6,2},{1,5},{3,7},{5,1},{7,3},{8,12},{10,14},{12... | collective-permute-start | bytes 196616 | tf_op jit(solution)/shard_map/ppermute | solution.py:15
  214.2 7.7 %collective-permute-start.33 = (f32[64,256]{1,0:T(8,128)S(1)}, f32[64,256]{1,0:T(8,128)S(1)}, u32[]{:S(2)}, u32[]{:S(2)}) collective-permute-start(f32[64,256]{1,0:T(8,128)S(1)} %get-tuple-element.62), channel_id=1, source_target_pairs={{0,6},{2,4},{4,2},{6,0},{1,7},{3,5},{5,3},{7,1},{8,14},{10,12},{12... | collective-permute-start | bytes 196616 | tf_op jit(solution)/shard_map/ppermute | solution.py:15
  217.2 6.2 %collective-permute-start.38 = (f32[64,256]{1,0:T(8,128)S(1)}, f32[64,256]{1,0:T(8,128)S(1)}, u32[]{:S(2)}, u32[]{:S(2)}) collective-permute-start(f32[64,256]{1,0:T(8,128)S(1)} %get-tuple-element.66), channel_id=1, source_target_pairs={{0,16},{8,24},{16,0},{24,8},{1,17},{9,25},{17,1},{25,9},{2,18},{10... | collective-permute-start | bytes 196616 | tf_op jit(solution)/shard_map/ppermute | solution.py:15
  220.5 5.5 %collective-permute-start.39 = (f32[64,256]{1,0:T(8,128)S(1)}, f32[64,256]{1,0:T(8,128)S(1)}, u32[]{:S(2)}, u32[]{:S(2)}) collective-permute-start(f32[64,256]{1,0:T(8,128)S(1)} %get-tuple-element.65), channel_id=1, source_target_pairs={{0,24},{8,16},{16,8},{24,0},{1,25},{9,17},{17,9},{25,1},{2,26},{10... | collective-permute-start | bytes 196616 | tf_op jit(solution)/shard_map/ppermute | solution.py:15
  226.0 8.3 %collective-permute-start.40 = (f32[2,16,512]{2,1,0:T(8,128)S(1)}, f32[2,16,512]{2,1,0:T(8,128)S(1)}, u32[]{:S(2)}, u32[]{:S(2)}) collective-permute-start(f32[2,16,512]{2,1,0:T(8,128)S(1)} %select_bitcast_fusion), channel_id=1, source_target_pairs={{0,1},{1,0},{2,3},{3,2},{4,5},{5,4},{6,7},{7,6},{8,9},{9,8},{10,11... | collective-permute-start | bytes 196616 | tf_op jit(solution)/shard_map/ppermute | solution.py:15
  (26 other events, 265.1 us)

commit v3 on v2

--- a/solution.py
+++ b/solution.py
@@ -57,11 +57,13 @@
 
 def logits_kernel(pairing, *refs):
     own, other = refs[0:4], refs[4:8]
-    feats, bias, wanted, logits, teacher, stat, x_buf, w_buf, t_buf, sems = refs[8:]
+    feats, bias, logits, teacher, wanted, stat, x_buf, w_buf, t_buf, d_buf, sems = refs[8:]
     z, core, x, y, zh = [lax.axis_index(axis) for axis in AXES]
     rows = t_buf.shape[1]
-    depth = own[0].shape[0] - rows
+    depth = own[0].shape[0] - rows - 16
     block = feats.shape[2]
+    cols = logits.shape[0]
+    base = (((x * 4 + y) * 2 + zh) * 4 + z) * cols
     copies = []
 
     def copy(src, dst):
@@ -69,24 +71,37 @@
         made.start()
         copies.append(made)
 
-    for j in range(4):
-        for pieces, side, place in ((own, core, j), (other, 1 - core, 4 + j)):
+    span = 4 * block
+    for j in range(4):
+        for pieces, side in ((own, core), (other, 1 - core)):
             row = pl.multiple_of((2 * (z ^ j) + side) * depth, depth)
             copy(pieces[j].at[pl.ds(0, depth), :], w_buf.at[pl.ds(row, depth), :])
+        for k in range(4):
+            col = pl.multiple_of((z ^ j) * span + k * block, block)
+            copy(feats.at[(z ^ j) * 4 + k], x_buf.at[:, pl.ds(col, block)])
+    for j in range(4):
+        for pieces, place in ((own, j), (other, 4 + j)):
             copy(pieces[j].at[pl.ds(depth, rows), :], t_buf.at[place])
-    for j in range(16):
-        copy(feats.at[j], x_buf.at[:, pl.ds(j * block, block)])
-    for made in copies:
+        copy(own[j].at[pl.ds(depth + rows, 16), :], d_buf.at[j])
+    for j in range(4):
+        for made in copies[6 * j : 6 * j + 6]:
+            made.wait()
+        at = pl.ds(pl.multiple_of((z ^ j) * span, span), span)
+        part = jnp.dot(x_buf[:, at], w_buf[at, :], preferred_element_type=F32)
+        if j == 0:
+            teacher[...] = part + bias[:, pl.ds(pl.multiple_of(z * cols, cols), cols)]
+        else:
+            teacher[...] += part
+    logits[...] = teacher[...].T
+    for made in copies[24:]:
         made.wait()
-    cols = logits.shape[0]
-    base = (((x * 4 + y) * 2 + zh) * 4 + z) * cols
-    step = cols // 2
-    for c in range(0, cols, step):
-        part = jnp.dot(x_buf[...], w_buf[:, c : c + step], preferred_element_type=F32)
-        part = part + bias[:, pl.ds(pl.multiple_of(z * cols + c, step), step)]
-        logits[c : c + step, :] = part.T
     values = logits[...]
     peak = jnp.max(values, axis=0, keepdims=True)
+    for j in range(4):
+        digits = d_buf[j].astype(F32)
+        ids = digits[0:1, :rows] * 256.0 + digits[1:2, :rows]
+        at = pl.ds(pl.multiple_of((z ^ j) * rows, rows), rows)
+        wanted[:, at] = ids.astype(jnp.int32)
     for i in range(4):
         source = jnp.int32(0)
         for s in range(8):
@@ -108,9 +123,9 @@
 
 
 def grad_kernel(*refs):
-    weights, pieces = refs[0:2], refs[2:6]
-    first, second = refs[6:10], refs[10:14]
-    w_buf, g_buf, sems = refs[14:]
+    weights, pieces = refs[0:2], refs[2:8]
+    first, second = refs[8:12], refs[12:16]
+    w_buf, g_buf, sems = refs[16:]
     z, _, x, y, _ = [lax.axis_index(axis) for axis in AXES]
     quarter = pieces[0].shape[0]
     rows = weights[0].shape[0] // 16
@@ -121,20 +136,23 @@
         made.start()
         copies.append(made)
 
-    for j in range(4):
-        row = pl.multiple_of((z ^ j) * quarter, quarter)
-        copy(pieces[j], g_buf.at[pl.ds(row, quarter), :])
+    for piece, j, part in zip(pieces, (0, 1, 2, 2, 3, 3), (0, 0, 0, 1, 0, 1)):
+        size = piece.shape[0]
+        row = pl.multiple_of((z ^ j) * quarter + part * size, size)
+        copy(piece, g_buf.at[pl.ds(row, size), :])
     for j in range(4):
         for k in range(4):
             row = pl.multiple_of(((x ^ j) * 4 + (y ^ k)) * rows, rows)
             for s in range(2):
                 to = ((j * 4 + k) * 2 + s) * rows
                 copy(weights[s].at[pl.ds(row, rows), :], w_buf.at[pl.ds(to, rows), :])
-    for made in copies:
+    for made in copies[:6]:
         made.wait()
     half = g_buf.shape[1] // 2
     group = 8 * rows
     for j in range(4):
+        for made in copies[6 + 8 * j : 14 + 8 * j]:
+            made.wait()
         left = w_buf[j * group : (j + 1) * group, :]
         part = jnp.dot(left, g_buf[:, :half], preferred_element_type=F32)
         first[j][...] = part.reshape(first[j].shape)
@@ -144,7 +162,7 @@
             second[k][j] = part[k]
 
 
-def call_logits(pairing, own, other, feats, bias, wanted):
+def call_logits(pairing, own, other, feats, bias):
     cols = own[0].shape[1]
     rows, depth = feats.shape[1], 16 * feats.shape[2]
     group = rows // 4
@@ -155,15 +173,17 @@
         out_shape=(
             jax.ShapeDtypeStruct((cols, rows), F32),
             jax.ShapeDtypeStruct((cols, rows), F32),
+            jax.ShapeDtypeStruct((1, rows), jnp.int32),
             jax.ShapeDtypeStruct((8, rows), F32),
         ),
-        in_specs=[pl.BlockSpec(memory_space=pltpu.SMEM)] + [hbm] * 9 + [vmem] * 2,
-        out_specs=(vmem, vmem, vmem),
+        in_specs=[pl.BlockSpec(memory_space=pltpu.SMEM)] + [hbm] * 9 + [vmem],
+        out_specs=(vmem,) * 4,
         scratch_shapes=[
             pltpu.VMEM((rows, depth), BF16),
             pltpu.VMEM((depth, cols), BF16),
             pltpu.VMEM((8, group, cols), BF16),
-            pltpu.SemaphoreType.DMA((32,)),
+            pltpu.VMEM((4, 16, cols), BF16),
+            pltpu.SemaphoreType.DMA((36,)),
         ],
         compiler_params=pltpu.CompilerParams(vmem_limit_bytes=VMEM_BYTES),
         cost_estimate=pl.CostEstimate(
@@ -172,7 +192,7 @@
             transcendentals=rows * cols,
         ),
         name="logits_block",
-    )(pairing, *own, *other, feats, bias, wanted)
+    )(pairing, *own, *other, feats, bias)
 
 
 def call_grad(weights, pieces):
@@ -185,12 +205,12 @@
     return pl.pallas_call(
         grad_kernel,
         out_shape=(out,) * 8,
-        in_specs=[hbm] * 6,
+        in_specs=[hbm] * 8,
         out_specs=(vmem,) * 8,
         scratch_shapes=[
             pltpu.VMEM((2 * rows_in, cols), BF16),
             pltpu.VMEM((cols, tokens), BF16),
-            pltpu.SemaphoreType.DMA((36,)),
+            pltpu.SemaphoreType.DMA((38,)),
         ],
         compiler_params=pltpu.CompilerParams(vmem_limit_bytes=VMEM_BYTES),
         cost_estimate=pl.CostEstimate(
@@ -213,16 +233,19 @@
     base = (((x * 4 + y) * 2 + zh) * 4 + z) * quarter
     feats = in_order(swaps(student_hidden, "zh"), zh)
     gathered = swaps(jnp.concatenate(feats, axis=1), "zl")
-    wanted = jnp.concatenate(in_order(swaps(after(targets, feats[0]), "zl"), z))[None, :]
-
-    both = jnp.concatenate([head_weight, teacher_logits], axis=0)
+
+    digits = jnp.stack([targets >> 8, targets & 255]).astype(BF16)
+    digits = jnp.tile(jnp.pad(digits, ((0, 14), (0, quarter - rows))), (1, 4))
+    both = jnp.concatenate([head_weight, teacher_logits, digits], axis=0)
     own = [lax.dynamic_slice_in_dim(both, (z ^ j) * quarter, quarter, axis=1) for j in range(4)]
     own[1:] = [swap(after(own[j], gathered[1]), "zl", j) for j in range(1, 4)]
     other = [swap(part, "co", 1) for part in own]
 
-    feats = after(jnp.concatenate(in_order(gathered, z), axis=0), wanted)
+    feats = jnp.concatenate(in_order(gathered, z), axis=0)
     feats = lax.all_to_all(jnp.broadcast_to(feats, (16, *feats.shape)), ("x", "y"), 0, 0, tiled=True)
-    logits, teacher, stat = call_logits(pairing, own, other, feats, head_bias[None, :], wanted)
+    logits, teacher, wanted, stat = call_logits(
+        pairing, own, other, feats, head_bias[None, :]
+    )
 
     for axis, place in (("x", x), ("y", y), ("zl", z), ("zh", zh)):
         stat = join_stats(in_order(swaps(stat, axis), place))
@@ -237,7 +260,9 @@
     grad = (2.0 * jnp.exp(logits - student_lse) - target_prob - onehot).astype(BF16)
 
     other_weight = swap(after(head_weight, grad), "co", 1)
-    first = call_grad((head_weight, other_weight), swaps(grad, "zl"))
+    skips = [swap(part, "zl", 2) for part in jnp.split(grad, 2, axis=0)]
+    pieces = [grad, swap(grad, "zl", 1), *skips, *[swap(part, "zl", 1) for part in skips]]
+    first = call_grad((head_weight, other_weight), pieces)
     first, second = first[:4], first[4:]
     first = add_all([first[0]] + [swap(first[j], "x", j) for j in range(1, 4)])
     second = add_all([second[0]] + [swap(second[j], "y", j) for j in range(1, 4)])

time: 237 us -> 222 us (0.937)
  waiting for transfers between devices: 135 us -> 123 us
    ppermute x42 -> x41, waiting for transfers between devices: 135 us -> 123 us  [swap(): return lax.ppermute(value, axis, [(i, i ^ flip) for i in range(AXES[axis])])]
    ppermute x42 -> x41, starting transfers between devices: 62.7 us -> 61.9 us  [swap(): return lax.ppermute(value, axis, [(i, i ^ flip) for i in range(AXES[axis])])]
  transfers between devices with their start and end apart: 43 -> 42, of which waited for: 25 -> 26; matrix products, arithmetic and copies ran while one was open for 2% -> 1% of each run, Pallas kernels for 0% -> 0%
where the time goes in v3:
time: 222 us; the launch traced here: 220 us
  waiting for transfers between devices  123 us (55%)
  starting transfers between devices  68.9 us (31%)
  Pallas kernels  13 us (6%)
  local copies, waits for them, and re-layouts  7.66 us (3%)
  other arithmetic  6.58 us (3%)
    ppermute x41, waiting for transfers between devices, swap(): return lax.ppermute(value, axis, [(i, i ^ flip) for i in range(AXES[axis])])  123 us
    ppermute x41, starting transfers between devices, swap(): return lax.ppermute(value, axis, [(i, i ^ flip) for i in range(AXES[axis])])  61.9 us
    all_to_all x1, starting transfers between devices, per_device(): lax.all_to_all(jnp.broadcast_to(feats, (16, *feats.shape)), ('x', 'y'), 0...  7 us
    pallas_call x1, Pallas kernels, call_logits(): pl.pallas_call(logits_kernel, out_shape=(jax.ShapeDtypeStruct((cols, rows...  6.97 us
    pallas_call x1, Pallas kernels, call_grad(): pl.pallas_call(grad_kernel, out_shape=(out,) * 8, in_specs=[hbm] * 8, out...  6.03 us
  transfers between devices with their start and end apart: 42, of which 26 were waited for; matrix products, arithmetic and copies ran while one was open for 1% of the time, Pallas kernels for 0%

profile of v3, /device:TPU:32, one launch (start us, length us, event | category | flops | bytes accessed | tf_op | source)
XLA Modules:
  0.0 219.8 jit_solution(8284628841186413591)
XLA Ops:
  0.6 6.4 %collective-permute-start = (bf16[128,128]{1,0:T(8,128)(2,1)}, bf16[128,128]{1,0:T(8,128)(2,1)S(1)}, u32[]{:S(2)}, u32[]{:S(2)}) collective-permute-start(bf16[128,128]{1,0:T(8,128)(2,1)} %param.7), channel_id=1, source_target_pairs={{0,1},{1,0},{2,3},{3,2},{4,5},{5,4},{6,7},{7,6},{8,9},{9,8},{10,11... | collective-permute-start | bytes 98312 | tf_op jit(solution)/shard_map/ppermute | solution.py:15
  7.0 2.1 collective-permute-done
  14.6 2.8 %collective-permute-done.10 = bf16[128,256]{1,0:T(8,128)(2,1)S(1)} collective-permute-done((bf16[128,256]{1,0:T(8,128)(2,1)S(1)}, bf16[128,256]{1,0:T(8,128)(2,1)S(1)}, u32[]{:S(2)}, u32[]{:S(2)}) %collective-permute-start.10) | collective-permute-done | bytes 65568 | tf_op jit(solution)/shard_map/ppermute | solution.py:15
  18.1 2.4 %broadcast_in_dim.6 = bf16[16,512,256]{2,1,0:T(8,128)(2,1)} broadcast(bf16[512,256]{1,0:T(8,128)(2,1)S(1)} %pad_maximum_fusion), dimensions={1,2} | broadcast | bytes 4456448 | tf_op jit(solution)/shard_map/broadcast_in_dim | solution.py:245
  20.6 7.0 %all-to-all-start = ((bf16[16,512,256]{2,1,0:T(8,128)(2,1)}), bf16[16,512,256]{2,1,0:T(8,128)(2,1)}, u32[]{:S(2)}, u32[]{:S(2)}) async-start(bf16[16,512,256]{2,1,0:T(8,128)(2,1)} %broadcast_in_dim.6), calls=%async_computation | async-start | bytes 8388608 | tf_op jit(solution)/shard_map/all_to_all | solution.py:245
  29.0 2.6 %collective-permute-start.3 = (bf16[656,512]{1,0:T(8,128)(2,1)S(1)}, bf16[656,512]{1,0:T(8,128)(2,1)S(1)}, u32[]{:S(2)}, u32[]{:S(2)}) collective-permute-start(bf16[656,512]{1,0:T(8,128)(2,1)S(1)} %get-tuple-element.19), channel_id=1, source_target_pairs={{0,128},{64,192},{128,0},{192,64},{1,129},{65,193},{129,1},{193,65... | collective-permute-start | bytes 2015240 | tf_op jit(solution)/shard_map/ppermute | solution.py:15
  31.6 2.1 collective-permute-start.4
  33.7 38.7 %collective-permute-done.3.refs_2_ = bf16[656,512]{1,0:T(8,128)(2,1)S(1)} collective-permute-done((bf16[656,512]{1,0:T(8,128)(2,1)S(1)}, bf16[656,512]{1,0:T(8,128)(2,1)S(1)}, u32[]{:S(2)}, u32[]{:S(2)}) %collective-permute-start.3) | collective-permute-done | bytes 671776 | tf_op jit(solution)/shard_map/ppermute | solution.py:15
  72.4 15.0 %collective-permute-done.4.refs_3_ = bf16[656,512]{1,0:T(8,128)(2,1)S(1)} collective-permute-done((bf16[656,512]{1,0:T(8,128)(2,1)S(1)}, bf16[656,512]{1,0:T(8,128)(2,1)S(1)}, u32[]{:S(2)}, u32[]{:S(2)}) %collective-permute-start.4) | collective-permute-done | bytes 671776 | tf_op jit(solution)/shard_map/ppermute | solution.py:15
  90.6 7.0 %logits_block.1 = (f32[512,512]{1,0:T(8,128)}, f32[512,512]{1,0:T(8,128)}, s32[1,512]{1,0:T(1,128)}, f32[8,512]{1,0:T(8,128)}) custom-call(s32[8]{0:T(128)} %pairing.1, bf16[656,512]{1,0:T(8,128)(2,1)} %copy-done, bf16[656,512]{1,0:T(8,128)(2,1)} %copy-done.5, bf16[656,512]{1,0:T(8,128)(2,1)} %copy-done.3, bf16[656,512]{1,0:T(8,128)(2,1)} %copy-done.4, ...), custom_call_target="tpu_custom_call" | custom-call | flops 2147483648 | bytes 8388608 | tf_op jit(solution)/shard_map/logits_block/pallas_call | solution.py:171
  97.6 2.9 %collective-permute-start.11 = (f32[8,512]{1,0:T(8,128)}, f32[8,512]{1,0:T(8,128)S(1)}, u32[]{:S(2)}, u32[]{:S(2)}) collective-permute-start(f32[8,512]{1,0:T(8,128)} %get-tuple-element.22), channel_id=1, source_target_pairs={{0,24},{8,16},{16,8},{24,0},{1,25},{9,17},{17,9},{25,1},{2,26},{10... | collective-permute-start | bytes 49160 | tf_op jit(solution)/shard_map/ppermute | solution.py:15
  102.8 3.1 %collective-permute-done.12 = f32[8,512]{1,0:T(8,128)S(1)} collective-permute-done((f32[8,512]{1,0:T(8,128)}, f32[8,512]{1,0:T(8,128)S(1)}, u32[]{:S(2)}, u32[]{:S(2)}) %collective-permute-start.12) | collective-permute-done | bytes 16416 | tf_op jit(solution)/shard_map/ppermute | solution.py:15
  106.7 2.9 %collective-permute-start.14 = (f32[8,512]{1,0:T(8,128)S(1)}, f32[8,512]{1,0:T(8,128)S(1)}, u32[]{:S(2)}, u32[]{:S(2)}) collective-permute-start(f32[8,512]{1,0:T(8,128)S(1)} %pad_maximum_fusion.4), channel_id=1, source_target_pairs={{0,6},{2,4},{4,2},{6,0},{1,7},{3,5},{5,3},{7,1},{8,14},{10,12},{12... | collective-permute-start | bytes 49160 | tf_op jit(solution)/shard_map/ppermute | solution.py:15
  112.0 3.0 %collective-permute-done.15 = f32[8,512]{1,0:T(8,128)S(1)} collective-permute-done((f32[8,512]{1,0:T(8,128)S(1)}, f32[8,512]{1,0:T(8,128)S(1)}, u32[]{:S(2)}, u32[]{:S(2)}) %collective-permute-start.15) | collective-permute-done | bytes 16416 | tf_op jit(solution)/shard_map/ppermute | solution.py:15
  118.9 2.6 %collective-permute-done.18 = f32[8,512]{1,0:T(8,128)S(1)} collective-permute-done((f32[8,512]{1,0:T(8,128)S(1)}, f32[8,512]{1,0:T(8,128)S(1)}, u32[]{:S(2)}, u32[]{:S(2)}) %collective-permute-start.18) | collective-permute-done | bytes 16416 | tf_op jit(solution)/shard_map/ppermute | solution.py:15
  121.6 4.8 %collective-permute-start.20 = (f32[8,512]{1,0:T(8,128)S(1)}, f32[8,512]{1,0:T(8,128)S(1)}, u32[]{:S(2)}, u32[]{:S(2)}) collective-permute-start(f32[8,512]{1,0:T(8,128)S(1)} %pad_maximum_fusion.6), channel_id=1, source_target_pairs={{0,1},{1,0},{2,3},{3,2},{4,5},{5,4},{6,7},{7,6},{8,9},{9,8},{10,11... | collective-permute-start | bytes 49160 | tf_op jit(solution)/shard_map/ppermute | solution.py:15
  126.4 2.9 %collective-permute-done.20 = f32[8,512]{1,0:T(8,128)S(1)} collective-permute-done((f32[8,512]{1,0:T(8,128)S(1)}, f32[8,512]{1,0:T(8,128)S(1)}, u32[]{:S(2)}, u32[]{:S(2)}) %collective-permute-start.20) | collective-permute-done | bytes 16416 | tf_op jit(solution)/shard_map/ppermute | solution.py:15
  135.5 16.7 %collective-permute-done.23.refs_4_ = bf16[256,512]{1,0:T(8,128)(2,1)S(1)} collective-permute-done((bf16[256,512]{1,0:T(8,128)(2,1)S(1)}, bf16[256,512]{1,0:T(8,128)(2,1)S(1)}, u32[]{:S(2)}, u32[]{:S(2)}) %collective-permute-start.23) | collective-permute-done | bytes 262176 | tf_op jit(solution)/shard_map/ppermute | solution.py:15
  152.2 5.6 %collective-permute-done.24.refs_5_ = bf16[256,512]{1,0:T(8,128)(2,1)S(1)} collective-permute-done((bf16[256,512]{1,0:T(8,128)(2,1)S(1)}, bf16[256,512]{1,0:T(8,128)(2,1)S(1)}, u32[]{:S(2)}, u32[]{:S(2)}) %collective-permute-start.24) | collective-permute-done | bytes 262176 | tf_op jit(solution)/shard_map/ppermute | solution.py:15
  157.7 2.2 %collective-permute-start.26 = (bf16[256,512]{1,0:T(8,128)(2,1)S(1)}, bf16[256,512]{1,0:T(8,128)(2,1)S(1)}, u32[]{:S(2)}, u32[]{:S(2)}) collective-permute-start(bf16[256,512]{1,0:T(8,128)(2,1)S(1)} %collective-permute-done.24.refs_5_), channel_id=1, source_target_pairs={{0,64},{64,0},{128,192},{192,128},{1,65},{65,1},{129,193},{193,129... | collective-permute-start | bytes 786440 | tf_op jit(solution)/shard_map/ppermute | solution.py:15
  160.0 3.2 %collective-permute-done.25.refs_6_ = bf16[256,512]{1,0:T(8,128)(2,1)S(1)} collective-permute-done((bf16[256,512]{1,0:T(8,128)(2,1)S(1)}, bf16[256,512]{1,0:T(8,128)(2,1)S(1)}, u32[]{:S(2)}, u32[]{:S(2)}) %collective-permute-start.25) | collective-permute-done | bytes 262176 | tf_op jit(solution)/shard_map/ppermute | solution.py:15
  163.2 5.1 %collective-permute-done.26.refs_7_ = bf16[256,512]{1,0:T(8,128)(2,1)S(1)} collective-permute-done((bf16[256,512]{1,0:T(8,128)(2,1)S(1)}, bf16[256,512]{1,0:T(8,128)(2,1)S(1)}, u32[]{:S(2)}, u32[]{:S(2)}) %collective-permute-start.26) | collective-permute-done | bytes 262176 | tf_op jit(solution)/shard_map/ppermute | solution.py:15
  170.4 6.0 %grad_block.1 = (f32[4,64,256]{2,1,0:T(8,128)}, f32[4,64,256]{2,1,0:T(8,128)}, f32[4,64,256]{2,1,0:T(8,128)}, f32[4,64,256]{2,1,0:T(8,128)}, f32[4,64,256]{2,1,0...) custom-call(bf16[512,2048]{1,0:T(8,128)(2,1)} %refs_0_.1, ...), custom_call_target="tpu_custom_call" | custom-call | flops 2147483648 | bytes 6291456 | tf_op jit(solution)/shard_map/grad_block/pallas_call | solution.py:205
  176.7 2.6 %collective-permute-start.28 = (f32[4,64,256]{2,1,0:T(8,128)}, f32[4,64,256]{2,1,0:T(8,128)S(1)}, u32[]{:S(2)}, u32[]{:S(2)}) collective-permute-start(f32[4,64,256]{2,1,0:T(8,128)} %get-tuple-element.28), channel_id=1, source_target_pairs={{0,16},{8,24},{16,0},{24,8},{1,17},{9,25},{17,1},{25,9},{2,18},{10... | collective-permute-start | bytes 786440 | tf_op jit(solution)/shard_map/ppermute | solution.py:15
  181.4 2.6 %collective-permute-start.34 = (f32[4,64,256]{2,1,0:T(8,128)}, f32[4,64,256]{2,1,0:T(8,128)S(1)}, u32[]{:S(2)}, u32[]{:S(2)}) collective-permute-start(f32[4,64,256]{2,1,0:T(8,128)} %get-tuple-element.32), channel_id=1, source_target_pairs={{0,4},{2,6},{4,0},{6,2},{1,5},{3,7},{5,1},{7,3},{8,12},{10,14},{12... | collective-permute-start | bytes 786440 | tf_op jit(solution)/shard_map/ppermute | solution.py:15
  187.3 3.8 %collective-permute-done.28 = f32[4,64,256]{2,1,0:T(8,128)S(1)} collective-permute-done((f32[4,64,256]{2,1,0:T(8,128)}, f32[4,64,256]{2,1,0:T(8,128)S(1)}, u32[]{:S(2)}, u32[]{:S(2)}) %collective-permute-start.28) | collective-permute-done | bytes 262176 | tf_op jit(solution)/shard_map/ppermute | solution.py:15
  191.1 2.6 %collective-permute-done.29 = f32[4,64,256]{2,1,0:T(8,128)S(1)} collective-permute-done((f32[4,64,256]{2,1,0:T(8,128)}, f32[4,64,256]{2,1,0:T(8,128)S(1)}, u32[]{:S(2)}, u32[]{:S(2)}) %collective-permute-start.29) | collective-permute-done | bytes 262176 | tf_op jit(solution)/shard_map/ppermute | solution.py:15
  195.1 2.6 %collective-permute-start.31 = (f32[64,256]{1,0:T(8,128)S(1)}, f32[64,256]{1,0:T(8,128)S(1)}, u32[]{:S(2)}, u32[]{:S(2)}) collective-permute-start(f32[64,256]{1,0:T(8,128)S(1)} %get-tuple-element.63), channel_id=1, source_target_pairs={{0,4},{2,6},{4,0},{6,2},{1,5},{3,7},{5,1},{7,3},{8,12},{10,14},{12... | collective-permute-start | bytes 196616 | tf_op jit(solution)/shard_map/ppermute | solution.py:15
  201.4 2.5 %collective-permute-start.37 = (f32[64,256]{1,0:T(8,128)S(1)}, f32[64,256]{1,0:T(8,128)S(1)}, u32[]{:S(2)}, u32[]{:S(2)}) collective-permute-start(f32[64,256]{1,0:T(8,128)S(1)} %get-tuple-element.66), channel_id=1, source_target_pairs={{0,16},{8,24},{16,0},{24,8},{1,17},{9,25},{17,1},{25,9},{2,18},{10... | collective-permute-start | bytes 196616 | tf_op jit(solution)/shard_map/ppermute | solution.py:15
  207.2 2.2 %collective-permute-done.38 = f32[64,256]{1,0:T(8,128)S(1)} collective-permute-done((f32[64,256]{1,0:T(8,128)S(1)}, f32[64,256]{1,0:T(8,128)S(1)}, u32[]{:S(2)}, u32[]{:S(2)}) %collective-permute-start.38) | collective-permute-done | bytes 65568 | tf_op jit(solution)/shard_map/ppermute | solution.py:15
  209.5 4.8 %collective-permute-start.39 = (f32[2,16,512]{2,1,0:T(8,128)S(1)}, f32[2,16,512]{2,1,0:T(8,128)S(1)}, u32[]{:S(2)}, u32[]{:S(2)}) collective-permute-start(f32[2,16,512]{2,1,0:T(8,128)S(1)} %select_bitcast_fusion), channel_id=1, source_target_pairs={{0,1},{1,0},{2,3},{3,2},{4,5},{5,4},{6,7},{7,6},{8,9},{9,8},{10,11... | collective-permute-start | bytes 196616 | tf_op jit(solution)/shard_map/ppermute | solution.py:15
  214.3 3.4 %collective-permute-done.39 = f32[2,16,512]{2,1,0:T(8,128)S(1)} collective-permute-done((f32[2,16,512]{2,1,0:T(8,128)S(1)}, f32[2,16,512]{2,1,0:T(8,128)S(1)}, u32[]{:S(2)}, u32[]{:S(2)}) %collective-permute-start.39) | collective-permute-done | bytes 65568 | tf_op jit(solution)/shard_map/ppermute | solution.py:15
  (141 shorter events, 44.4 us)
Async XLA Ops:
  0.6 8.5 %collective-permute-start = (bf16[128,128]{1,0:T(8,128)(2,1)}, bf16[128,128]{1,0:T(8,128)(2,1)S(1)}, u32[]{:S(2)}, u32[]{:S(2)}) collective-permute-start(bf16[128,128]{1,0:T(8,128)(2,1)} %param.7), channel_id=1, source_target_pairs={{0,1},{1,0},{2,3},{3,2},{4,5},{5,4},{6,7},{7,6},{8,9},{9,8},{10,11... | collective-permute-start | bytes 98312 | tf_op jit(solution)/shard_map/ppermute | solution.py:15
  11.5 5.9 %collective-permute-start.10 = (bf16[128,256]{1,0:T(8,128)(2,1)S(1)}, bf16[128,256]{1,0:T(8,128)(2,1)S(1)}, u32[]{:S(2)}, u32[]{:S(2)}) collective-permute-start(bf16[128,256]{1,0:T(8,128)(2,1)S(1)} %pad_maximum_fusion.2), channel_id=1, source_target_pairs={{0,128},{64,192},{128,0},{192,64},{1,129},{65,193},{129,1},{193,65... | collective-permute-start | bytes 196616 | tf_op jit(solution)/shard_map/ppermute | solution.py:15
  13.1 4.9 %collective-permute-start.9 = (bf16[128,256]{1,0:T(8,128)(2,1)S(1)}, bf16[128,256]{1,0:T(8,128)(2,1)S(1)}, u32[]{:S(2)}, u32[]{:S(2)}) collective-permute-start(bf16[128,256]{1,0:T(8,128)(2,1)S(1)} %pad_maximum_fusion.2), channel_id=1, source_target_pairs={{0,192},{64,128},{128,64},{192,0},{1,193},{65,129},{129,65},{193,1... | collective-permute-start | bytes 196616 | tf_op jit(solution)/shard_map/ppermute | solution.py:15
  20.6 70.0 %all-to-all-start = ((bf16[16,512,256]{2,1,0:T(8,128)(2,1)}), bf16[16,512,256]{2,1,0:T(8,128)(2,1)}, u32[]{:S(2)}, u32[]{:S(2)}) async-start(bf16[16,512,256]{2,1,0:T(8,128)(2,1)} %broadcast_in_dim.6), calls=%async_computation | async-start | bytes 8388608 | tf_op jit(solution)/shard_map/all_to_all | solution.py:245
  29.0 43.4 %collective-permute-start.3 = (bf16[656,512]{1,0:T(8,128)(2,1)S(1)}, bf16[656,512]{1,0:T(8,128)(2,1)S(1)}, u32[]{:S(2)}, u32[]{:S(2)}) collective-permute-start(bf16[656,512]{1,0:T(8,128)(2,1)S(1)} %get-tuple-element.19), channel_id=1, source_target_pairs={{0,128},{64,192},{128,0},{192,64},{1,129},{65,193},{129,1},{193,65... | collective-permute-start | bytes 2015240 | tf_op jit(solution)/shard_map/ppermute | solution.py:15
  31.6 55.8 %collective-permute-start.4 = (bf16[656,512]{1,0:T(8,128)(2,1)S(1)}, bf16[656,512]{1,0:T(8,128)(2,1)S(1)}, u32[]{:S(2)}, u32[]{:S(2)}) collective-permute-start(bf16[656,512]{1,0:T(8,128)(2,1)S(1)} %get-tuple-element.20), channel_id=1, source_target_pairs={{0,192},{64,128},{128,64},{192,0},{1,193},{65,129},{129,65},{193,1... | collective-permute-start | bytes 2015240 | tf_op jit(solution)/shard_map/ppermute | solution.py:15
  33.7 53.7 %collective-permute-start.2 = (bf16[656,512]{1,0:T(8,128)(2,1)S(1)}, bf16[656,512]{1,0:T(8,128)(2,1)S(1)}, u32[]{:S(2)}, u32[]{:S(2)}) collective-permute-start(bf16[656,512]{1,0:T(8,128)(2,1)S(1)} %get-tuple-element.18), channel_id=1, source_target_pairs={{0,64},{64,0},{128,192},{192,128},{1,65},{65,1},{129,193},{193,129... | collective-permute-start | bytes 2015240 | tf_op jit(solution)/shard_map/ppermute | solution.py:15
  33.7 54.2 %collective-permute-start.5 = (bf16[656,512]{1,0:T(8,128)(2,1)S(1)}, bf16[656,512]{1,0:T(8,128)(2,1)S(1)}, u32[]{:S(2)}, u32[]{:S(2)}) collective-permute-start(bf16[656,512]{1,0:T(8,128)(2,1)S(1)} %get-tuple-element.59.refs_0_), channel_id=1, source_target_pairs={{0,32},{32,0},{1,33},{33,1},{2,34},{34,2},{3,35},{35,3},{4,36},{36... | collective-permute-start | bytes 2015240 | tf_op jit(solution)/shard_map/ppermute | solution.py:15
  72.4 15.5 %collective-permute-start.7 = (bf16[656,512]{1,0:T(8,128)(2,1)S(1)}, bf16[656,512]{1,0:T(8,128)(2,1)S(1)}, u32[]{:S(2)}, u32[]{:S(2)}) collective-permute-start(bf16[656,512]{1,0:T(8,128)(2,1)S(1)} %collective-permute-done.3.refs_2_), channel_id=1, source_target_pairs={{0,32},{32,0},{1,33},{33,1},{2,34},{34,2},{3,35},{35,3},{4,36},{36... | collective-permute-start | bytes 2015240 | tf_op jit(solution)/shard_map/ppermute | solution.py:15
  97.6 5.2 %collective-permute-start.11 = (f32[8,512]{1,0:T(8,128)}, f32[8,512]{1,0:T(8,128)S(1)}, u32[]{:S(2)}, u32[]{:S(2)}) collective-permute-start(f32[8,512]{1,0:T(8,128)} %get-tuple-element.22), channel_id=1, source_target_pairs={{0,24},{8,16},{16,8},{24,0},{1,25},{9,17},{17,9},{25,1},{2,26},{10... | collective-permute-start | bytes 49160 | tf_op jit(solution)/shard_map/ppermute | solution.py:15
  100.5 5.5 %collective-permute-start.12 = (f32[8,512]{1,0:T(8,128)}, f32[8,512]{1,0:T(8,128)S(1)}, u32[]{:S(2)}, u32[]{:S(2)}) collective-permute-start(f32[8,512]{1,0:T(8,128)} %get-tuple-element.22), channel_id=1, source_target_pairs={{0,16},{8,24},{16,0},{24,8},{1,17},{9,25},{17,1},{25,9},{2,18},{10... | collective-permute-start | bytes 49160 | tf_op jit(solution)/shard_map/ppermute | solution.py:15
  106.7 5.2 %collective-permute-start.14 = (f32[8,512]{1,0:T(8,128)S(1)}, f32[8,512]{1,0:T(8,128)S(1)}, u32[]{:S(2)}, u32[]{:S(2)}) collective-permute-start(f32[8,512]{1,0:T(8,128)S(1)} %pad_maximum_fusion.4), channel_id=1, source_target_pairs={{0,6},{2,4},{4,2},{6,0},{1,7},{3,5},{5,3},{7,1},{8,14},{10,12},{12... | collective-permute-start | bytes 49160 | tf_op jit(solution)/shard_map/ppermute | solution.py:15
  109.7 5.2 %collective-permute-start.15 = (f32[8,512]{1,0:T(8,128)S(1)}, f32[8,512]{1,0:T(8,128)S(1)}, u32[]{:S(2)}, u32[]{:S(2)}) collective-permute-start(f32[8,512]{1,0:T(8,128)S(1)} %pad_maximum_fusion.4), channel_id=1, source_target_pairs={{0,4},{2,6},{4,0},{6,2},{1,5},{3,7},{5,1},{7,3},{8,12},{10,14},{12... | collective-permute-start | bytes 49160 | tf_op jit(solution)/shard_map/ppermute | solution.py:15
  121.6 7.7 %collective-permute-start.20 = (f32[8,512]{1,0:T(8,128)S(1)}, f32[8,512]{1,0:T(8,128)S(1)}, u32[]{:S(2)}, u32[]{:S(2)}) collective-permute-start(f32[8,512]{1,0:T(8,128)S(1)} %pad_maximum_fusion.6), channel_id=1, source_target_pairs={{0,1},{1,0},{2,3},{3,2},{4,5},{5,4},{6,7},{7,6},{8,9},{9,8},{10,11... | collective-permute-start | bytes 49160 | tf_op jit(solution)/shard_map/ppermute | solution.py:15
  131.4 37.0 %collective-permute-start.21 = (bf16[512,2048]{1,0:T(8,128)(2,1)S(1)}, bf16[512,2048]{1,0:T(8,128)(2,1)S(1)}, u32[]{:S(2)}, u32[]{:S(2)}) collective-permute-start(bf16[512,2048]{1,0:T(8,128)(2,1)S(1)} %copy-done.2), channel_id=1, source_target_pairs={{0,32},{32,0},{1,33},{33,1},{2,34},{34,2},{3,35},{35,3},{4,36},{36... | collective-permute-start | bytes 6291464 | tf_op jit(solution)/shard_map/ppermute | solution.py:15
  131.5 28.5 %collective-permute-start.22 = (bf16[512,512]{1,0:T(8,128)(2,1)S(1)}, bf16[512,512]{1,0:T(8,128)(2,1)S(1)}, u32[]{:S(2)}, u32[]{:S(2)}) collective-permute-start(bf16[512,512]{1,0:T(8,128)(2,1)S(1)} %subtract_convert_fusion.refs_2_), channel_id=1, source_target_pairs={{0,64},{64,0},{128,192},{192,128},{1,65},{65,1},{129,193},{193,129... | collective-permute-start | bytes 1572872 | tf_op jit(solution)/shard_map/ppermute | solution.py:15
  132.4 19.7 %collective-permute-start.23 = (bf16[256,512]{1,0:T(8,128)(2,1)S(1)}, bf16[256,512]{1,0:T(8,128)(2,1)S(1)}, u32[]{:S(2)}, u32[]{:S(2)}) collective-permute-start(bf16[256,512]{1,0:T(8,128)(2,1)S(1)} %get-tuple-element.61), channel_id=1, source_target_pairs={{0,128},{64,192},{128,0},{192,64},{1,129},{65,193},{129,1},{193,65... | collective-permute-start | bytes 786440 | tf_op jit(solution)/shard_map/ppermute | solution.py:15
  133.9 23.8 %collective-permute-start.24 = (bf16[256,512]{1,0:T(8,128)(2,1)S(1)}, bf16[256,512]{1,0:T(8,128)(2,1)S(1)}, u32[]{:S(2)}, u32[]{:S(2)}) collective-permute-start(bf16[256,512]{1,0:T(8,128)(2,1)S(1)} %get-tuple-element.60), channel_id=1, source_target_pairs={{0,128},{64,192},{128,0},{192,64},{1,129},{65,193},{129,1},{193,65... | collective-permute-start | bytes 786440 | tf_op jit(solution)/shard_map/ppermute | solution.py:15
  152.2 11.0 %collective-permute-start.25 = (bf16[256,512]{1,0:T(8,128)(2,1)S(1)}, bf16[256,512]{1,0:T(8,128)(2,1)S(1)}, u32[]{:S(2)}, u32[]{:S(2)}) collective-permute-start(bf16[256,512]{1,0:T(8,128)(2,1)S(1)} %collective-permute-done.23.refs_4_), channel_id=1, source_target_pairs={{0,64},{64,0},{128,192},{192,128},{1,65},{65,1},{129,193},{193,129... | collective-permute-start | bytes 786440 | tf_op jit(solution)/shard_map/ppermute | solution.py:15
  157.7 10.6 %collective-permute-start.26 = (bf16[256,512]{1,0:T(8,128)(2,1)S(1)}, bf16[256,512]{1,0:T(8,128)(2,1)S(1)}, u32[]{:S(2)}, u32[]{:S(2)}) collective-permute-start(bf16[256,512]{1,0:T(8,128)(2,1)S(1)} %collective-permute-done.24.refs_5_), channel_id=1, source_target_pairs={{0,64},{64,0},{128,192},{192,128},{1,65},{65,1},{129,193},{193,129... | collective-permute-start | bytes 786440 | tf_op jit(solution)/shard_map/ppermute | solution.py:15
  176.4 9.5 %collective-permute-start.27 = (f32[4,64,256]{2,1,0:T(8,128)}, f32[4,64,256]{2,1,0:T(8,128)S(1)}, u32[]{:S(2)}, u32[]{:S(2)}) collective-permute-start(f32[4,64,256]{2,1,0:T(8,128)} %get-tuple-element.27), channel_id=1, source_target_pairs={{0,8},{8,0},{16,24},{24,16},{1,9},{9,1},{17,25},{25,17},{2,10},{10... | collective-permute-start | bytes 786440 | tf_op jit(solution)/shard_map/ppermute | solution.py:15
  176.7 14.4 %collective-permute-start.28 = (f32[4,64,256]{2,1,0:T(8,128)}, f32[4,64,256]{2,1,0:T(8,128)S(1)}, u32[]{:S(2)}, u32[]{:S(2)}) collective-permute-start(f32[4,64,256]{2,1,0:T(8,128)} %get-tuple-element.28), channel_id=1, source_target_pairs={{0,16},{8,24},{16,0},{24,8},{1,17},{9,25},{17,1},{25,9},{2,18},{10... | collective-permute-start | bytes 786440 | tf_op jit(solution)/shard_map/ppermute | solution.py:15
  179.4 14.3 %collective-permute-start.29 = (f32[4,64,256]{2,1,0:T(8,128)}, f32[4,64,256]{2,1,0:T(8,128)S(1)}, u32[]{:S(2)}, u32[]{:S(2)}) collective-permute-start(f32[4,64,256]{2,1,0:T(8,128)} %get-tuple-element.29), channel_id=1, source_target_pairs={{0,24},{8,16},{16,8},{24,0},{1,25},{9,17},{17,9},{25,1},{2,26},{10... | collective-permute-start | bytes 786440 | tf_op jit(solution)/shard_map/ppermute | solution.py:15
  181.2 16.5 %collective-permute-start.33 = (f32[4,64,256]{2,1,0:T(8,128)}, f32[4,64,256]{2,1,0:T(8,128)S(1)}, u32[]{:S(2)}, u32[]{:S(2)}) collective-permute-start(f32[4,64,256]{2,1,0:T(8,128)} %get-tuple-element.31), channel_id=1, source_target_pairs={{0,2},{2,0},{4,6},{6,4},{1,3},{3,1},{5,7},{7,5},{8,10},{10,8},{12,... | collective-permute-start | bytes 786440 | tf_op jit(solution)/shard_map/ppermute | solution.py:15
  181.4 18.1 %collective-permute-start.34 = (f32[4,64,256]{2,1,0:T(8,128)}, f32[4,64,256]{2,1,0:T(8,128)S(1)}, u32[]{:S(2)}, u32[]{:S(2)}) collective-permute-start(f32[4,64,256]{2,1,0:T(8,128)} %get-tuple-element.32), channel_id=1, source_target_pairs={{0,4},{2,6},{4,0},{6,2},{1,5},{3,7},{5,1},{7,3},{8,12},{10,14},{12... | collective-permute-start | bytes 786440 | tf_op jit(solution)/shard_map/ppermute | solution.py:15
  185.9 13.6 %collective-permute-start.35 = (f32[4,64,256]{2,1,0:T(8,128)}, f32[4,64,256]{2,1,0:T(8,128)S(1)}, u32[]{:S(2)}, u32[]{:S(2)}) collective-permute-start(f32[4,64,256]{2,1,0:T(8,128)} %get-tuple-element.33), channel_id=1, source_target_pairs={{0,6},{2,4},{4,2},{6,0},{1,7},{3,5},{5,3},{7,1},{8,14},{10,12},{12... | collective-permute-start | bytes 786440 | tf_op jit(solution)/shard_map/ppermute | solution.py:15
  194.7 9.2 %collective-permute-start.30 = (f32[64,256]{1,0:T(8,128)S(1)}, f32[64,256]{1,0:T(8,128)S(1)}, u32[]{:S(2)}, u32[]{:S(2)}) collective-permute-start(f32[64,256]{1,0:T(8,128)S(1)} %get-tuple-element.64), channel_id=1, source_target_pairs={{0,2},{2,0},{4,6},{6,4},{1,3},{3,1},{5,7},{7,5},{8,10},{10,8},{12,... | collective-permute-start | bytes 196616 | tf_op jit(solution)/shard_map/ppermute | solution.py:15
  195.1 10.3 %collective-permute-start.31 = (f32[64,256]{1,0:T(8,128)S(1)}, f32[64,256]{1,0:T(8,128)S(1)}, u32[]{:S(2)}, u32[]{:S(2)}) collective-permute-start(f32[64,256]{1,0:T(8,128)S(1)} %get-tuple-element.63), channel_id=1, source_target_pairs={{0,4},{2,6},{4,0},{6,2},{1,5},{3,7},{5,1},{7,3},{8,12},{10,14},{12... | collective-permute-start | bytes 196616 | tf_op jit(solution)/shard_map/ppermute | solution.py:15
  197.7 7.7 %collective-permute-start.32 = (f32[64,256]{1,0:T(8,128)S(1)}, f32[64,256]{1,0:T(8,128)S(1)}, u32[]{:S(2)}, u32[]{:S(2)}) collective-permute-start(f32[64,256]{1,0:T(8,128)S(1)} %get-tuple-element.62), channel_id=1, source_target_pairs={{0,6},{2,4},{4,2},{6,0},{1,7},{3,5},{5,3},{7,1},{8,14},{10,12},{12... | collective-permute-start | bytes 196616 | tf_op jit(solution)/shard_map/ppermute | solution.py:15
  201.4 5.8 %collective-permute-start.37 = (f32[64,256]{1,0:T(8,128)S(1)}, f32[64,256]{1,0:T(8,128)S(1)}, u32[]{:S(2)}, u32[]{:S(2)}) collective-permute-start(f32[64,256]{1,0:T(8,128)S(1)} %get-tuple-element.66), channel_id=1, source_target_pairs={{0,16},{8,24},{16,0},{24,8},{1,17},{9,25},{17,1},{25,9},{2,18},{10... | collective-permute-start | bytes 196616 | tf_op jit(solution)/shard_map/ppermute | solution.py:15
  203.9 5.5 %collective-permute-start.38 = (f32[64,256]{1,0:T(8,128)S(1)}, f32[64,256]{1,0:T(8,128)S(1)}, u32[]{:S(2)}, u32[]{:S(2)}) collective-permute-start(f32[64,256]{1,0:T(8,128)S(1)} %get-tuple-element.65), channel_id=1, source_target_pairs={{0,24},{8,16},{16,8},{24,0},{1,25},{9,17},{17,9},{25,1},{2,26},{10... | collective-permute-start | bytes 196616 | tf_op jit(solution)/shard_map/ppermute | solution.py:15
  209.5 8.3 %collective-permute-start.39 = (f32[2,16,512]{2,1,0:T(8,128)S(1)}, f32[2,16,512]{2,1,0:T(8,128)S(1)}, u32[]{:S(2)}, u32[]{:S(2)}) collective-permute-start(f32[2,16,512]{2,1,0:T(8,128)S(1)} %select_bitcast_fusion), channel_id=1, source_target_pairs={{0,1},{1,0},{2,3},{3,2},{4,5},{5,4},{6,7},{7,6},{8,9},{9,8},{10,11... | collective-permute-start | bytes 196616 | tf_op jit(solution)/shard_map/ppermute | solution.py:15
  (27 other events, 219.3 us)

commit v4 on v3

--- a/solution.py
+++ b/solution.py
@@ -55,15 +55,13 @@
     return jnp.concatenate([peak, add_all(sums), add_all(divs), rest], axis=0)
 
 
-def logits_kernel(pairing, *refs):
+def logits_kernel(*refs):
     own, other = refs[0:4], refs[4:8]
-    feats, bias, logits, teacher, wanted, stat, x_buf, w_buf, t_buf, d_buf, sems = refs[8:]
-    z, core, x, y, zh = [lax.axis_index(axis) for axis in AXES]
-    rows = t_buf.shape[1]
-    depth = own[0].shape[0] - rows - 16
+    feats, bias, logits, stat, x_buf, w_buf, total, sems = refs[8:]
+    z, core = lax.axis_index("zl"), lax.axis_index("co")
+    depth = own[0].shape[0]
     block = feats.shape[2]
     cols = logits.shape[0]
-    base = (((x * 4 + y) * 2 + zh) * 4 + z) * cols
     copies = []
 
     def copy(src, dst):
@@ -75,30 +73,32 @@
     for j in range(4):
         for pieces, side in ((own, core), (other, 1 - core)):
             row = pl.multiple_of((2 * (z ^ j) + side) * depth, depth)
-            copy(pieces[j].at[pl.ds(0, depth), :], w_buf.at[pl.ds(row, depth), :])
+            copy(pieces[j], w_buf.at[pl.ds(row, depth), :])
         for k in range(4):
             col = pl.multiple_of((z ^ j) * span + k * block, block)
             copy(feats.at[(z ^ j) * 4 + k], x_buf.at[:, pl.ds(col, block)])
-    for j in range(4):
-        for pieces, place in ((own, j), (other, 4 + j)):
-            copy(pieces[j].at[pl.ds(depth, rows), :], t_buf.at[place])
-        copy(own[j].at[pl.ds(depth + rows, 16), :], d_buf.at[j])
     for j in range(4):
         for made in copies[6 * j : 6 * j + 6]:
             made.wait()
         at = pl.ds(pl.multiple_of((z ^ j) * span, span), span)
         part = jnp.dot(x_buf[:, at], w_buf[at, :], preferred_element_type=F32)
         if j == 0:
-            teacher[...] = part + bias[:, pl.ds(pl.multiple_of(z * cols, cols), cols)]
+            total[...] = part + bias[:, pl.ds(pl.multiple_of(z * cols, cols), cols)]
         else:
-            teacher[...] += part
-    logits[...] = teacher[...].T
-    for made in copies[24:]:
-        made.wait()
-    values = logits[...]
+            total[...] += part
+    values = total[...].T
+    logits[...] = values
     peak = jnp.max(values, axis=0, keepdims=True)
-    for j in range(4):
-        digits = d_buf[j].astype(F32)
+    stat[0:1, :] = peak
+    stat[1:2, :] = jnp.sum(jnp.exp(values - peak), axis=0, keepdims=True)
+
+
+def teacher_kernel(pairing, marks, logits, student, teacher, wanted, stat):
+    z, core, x, y, zh = [lax.axis_index(axis) for axis in AXES]
+    rows, cols = marks.shape[1] - 16, marks.shape[2]
+    base = (((x * 4 + y) * 2 + zh) * 4 + z) * cols
+    for j in range(4):
+        digits = marks[j, rows:, :].astype(F32)
         ids = digits[0:1, :rows] * 256.0 + digits[1:2, :rows]
         at = pl.ds(pl.multiple_of((z ^ j) * rows, rows), rows)
         wanted[:, at] = ids.astype(jnp.int32)
@@ -107,16 +107,17 @@
         for s in range(8):
             source = jnp.where(pairing[s] == 2 * i + core, s, source)
         place = ((source >> 1) ^ z) + 4 * ((source & 1) ^ core)
-        teacher[:, i * rows : (i + 1) * rows] = t_buf[place].astype(F32).T
+        teacher[:, i * rows : (i + 1) * rows] = marks[place, :rows, :].astype(F32).T
+    values = logits[...]
     target = teacher[...]
     target_peak = jnp.max(target, axis=0, keepdims=True)
     weight = jnp.exp(target - target_peak)
     ids = base + lax.broadcasted_iota(jnp.int32, values.shape, 0)
     hit = jnp.where(ids == wanted[...], values, 0.0)
     stat[...] = jnp.zeros_like(stat)
-    stat[0:1, :] = peak
+    stat[0:1, :] = student[0:1, :]
     stat[1:2, :] = target_peak
-    stat[2:3, :] = jnp.sum(jnp.exp(values - peak), axis=0, keepdims=True)
+    stat[2:3, :] = student[1:2, :]
     stat[3:4, :] = jnp.sum(weight, axis=0, keepdims=True)
     stat[4:5, :] = jnp.sum(weight * (target - values), axis=0, keepdims=True)
     stat[5:6, :] = jnp.sum(hit, axis=0, keepdims=True)
@@ -162,28 +163,24 @@
             second[k][j] = part[k]
 
 
-def call_logits(pairing, own, other, feats, bias):
+def call_logits(own, other, feats, bias):
     cols = own[0].shape[1]
     rows, depth = feats.shape[1], 16 * feats.shape[2]
-    group = rows // 4
     hbm = pl.BlockSpec(memory_space=pl.ANY)
     vmem = pl.BlockSpec(memory_space=pltpu.VMEM)
     return pl.pallas_call(
         logits_kernel,
         out_shape=(
             jax.ShapeDtypeStruct((cols, rows), F32),
-            jax.ShapeDtypeStruct((cols, rows), F32),
-            jax.ShapeDtypeStruct((1, rows), jnp.int32),
-            jax.ShapeDtypeStruct((8, rows), F32),
-        ),
-        in_specs=[pl.BlockSpec(memory_space=pltpu.SMEM)] + [hbm] * 9 + [vmem],
-        out_specs=(vmem,) * 4,
+            jax.ShapeDtypeStruct((2, rows), F32),
+        ),
+        in_specs=[hbm] * 9 + [vmem],
+        out_specs=(vmem,) * 2,
         scratch_shapes=[
             pltpu.VMEM((rows, depth), BF16),
             pltpu.VMEM((depth, cols), BF16),
-            pltpu.VMEM((8, group, cols), BF16),
-            pltpu.VMEM((4, 16, cols), BF16),
-            pltpu.SemaphoreType.DMA((36,)),
+            pltpu.VMEM((rows, cols), F32),
+            pltpu.SemaphoreType.DMA((24,)),
         ],
         compiler_params=pltpu.CompilerParams(vmem_limit_bytes=VMEM_BYTES),
         cost_estimate=pl.CostEstimate(
@@ -192,7 +189,29 @@
             transcendentals=rows * cols,
         ),
         name="logits_block",
-    )(pairing, *own, *other, feats, bias)
+    )(*own, *other, feats, bias)
+
+
+def call_teacher(pairing, marks, logits, student):
+    cols, rows = logits.shape
+    vmem = pl.BlockSpec(memory_space=pltpu.VMEM)
+    return pl.pallas_call(
+        teacher_kernel,
+        out_shape=(
+            jax.ShapeDtypeStruct((cols, rows), F32),
+            jax.ShapeDtypeStruct((1, rows), jnp.int32),
+            jax.ShapeDtypeStruct((8, rows), F32),
+        ),
+        in_specs=[pl.BlockSpec(memory_space=pltpu.SMEM)] + [vmem] * 3,
+        out_specs=(vmem,) * 3,
+        compiler_params=pltpu.CompilerParams(vmem_limit_bytes=VMEM_BYTES),
+        cost_estimate=pl.CostEstimate(
+            flops=8 * rows * cols,
+            bytes_accessed=12 * rows * cols,
+            transcendentals=rows * cols,
+        ),
+        name="teacher_block",
+    )(pairing, marks, logits, student)
 
 
 def call_grad(weights, pieces):
@@ -234,18 +253,25 @@
     feats = in_order(swaps(student_hidden, "zh"), zh)
     gathered = swaps(jnp.concatenate(feats, axis=1), "zl")
 
+    own = [
+        lax.dynamic_slice_in_dim(head_weight, (z ^ j) * quarter, quarter, axis=1)
+        for j in range(4)
+    ]
+    own[1:] = [swap(after(own[j], gathered[1]), "zl", j) for j in range(1, 4)]
+    other = [swap(part, "co", 1) for part in own]
+
     digits = jnp.stack([targets >> 8, targets & 255]).astype(BF16)
     digits = jnp.tile(jnp.pad(digits, ((0, 14), (0, quarter - rows))), (1, 4))
-    both = jnp.concatenate([head_weight, teacher_logits, digits], axis=0)
-    own = [lax.dynamic_slice_in_dim(both, (z ^ j) * quarter, quarter, axis=1) for j in range(4)]
-    own[1:] = [swap(after(own[j], gathered[1]), "zl", j) for j in range(1, 4)]
-    other = [swap(part, "co", 1) for part in own]
-
+    marks = jnp.concatenate([teacher_logits, digits], axis=0)
+    marks = [lax.dynamic_slice_in_dim(marks, (z ^ j) * quarter, quarter, axis=1) for j in range(4)]
+    marks[1:] = [swap(after(marks[j], *gathered[1:]), "zl", j) for j in range(1, 4)]
     feats = jnp.concatenate(in_order(gathered, z), axis=0)
     feats = lax.all_to_all(jnp.broadcast_to(feats, (16, *feats.shape)), ("x", "y"), 0, 0, tiled=True)
-    logits, teacher, wanted, stat = call_logits(
-        pairing, own, other, feats, head_bias[None, :]
-    )
+    logits, stat = call_logits(own, other, feats, head_bias[None, :])
+    stat, *marks = lax.optimization_barrier((stat, *marks))
+    marks = jnp.stack(marks)
+    marks = jnp.concatenate([marks, swap(marks, "co", 1)], axis=0)
+    teacher, wanted, stat = call_teacher(pairing, marks, logits, stat)
 
     for axis, place in (("x", x), ("y", y), ("zl", z), ("zh", zh)):
         stat = join_stats(in_order(swaps(stat, axis), place))
@@ -259,7 +285,7 @@
     onehot = (ids == wanted).astype(F32)
     grad = (2.0 * jnp.exp(logits - student_lse) - target_prob - onehot).astype(BF16)
 
-    other_weight = swap(after(head_weight, grad), "co", 1)
+    other_weight = swap(after(head_weight, own[1]), "co", 1)
     skips = [swap(part, "zl", 2) for part in jnp.split(grad, 2, axis=0)]
     pieces = [grad, swap(grad, "zl", 1), *skips, *[swap(part, "zl", 1) for part in skips]]
     first = call_grad((head_weight, other_weight), pieces)

time: 222 us -> 215 us (0.968)
  waiting for transfers between devices: 123 us -> 114 us
  Pallas kernels: 13 us -> 15.4 us
    ppermute x41 -> x45, waiting for transfers between devices: 123 us -> 114 us  [swap(): return lax.ppermute(value, axis, [(i, i ^ flip) for i in range(AXES[axis])])]
    pallas_call x0 -> x1, Pallas kernels: none -> 3.18 us  [call_teacher(): pl.pallas_call(teacher_kernel, out_shape=(jax.ShapeDtypeStruct((cols, row...]
    ppermute x41 -> x45, starting transfers between devices: 61.9 us -> 62.8 us  [swap(): return lax.ppermute(value, axis, [(i, i ^ flip) for i in range(AXES[axis])])]
  transfers between devices with their start and end apart: 42 -> 46, of which waited for: 26 -> 29; matrix products, arithmetic and copies ran while one was open for 1% -> 2% of each run, Pallas kernels for 0% -> 3%
where the time goes in v4:
time: 215 us; the launch traced here: 213 us
  waiting for transfers between devices  114 us (53%)
  starting transfers between devices  70 us (33%)
  Pallas kernels  15.4 us (7%)
  local copies, waits for them, and re-layouts  6.95 us (3%)
  other arithmetic  5.39 us (3%)
    ppermute x45, waiting for transfers between devices, swap(): return lax.ppermute(value, axis, [(i, i ^ flip) for i in range(AXES[axis])])  114 us
    ppermute x45, starting transfers between devices, swap(): return lax.ppermute(value, axis, [(i, i ^ flip) for i in range(AXES[axis])])  62.8 us
    all_to_all x1, starting transfers between devices, per_device(): lax.all_to_all(jnp.broadcast_to(feats, (16, *feats.shape)), ('x', 'y'), 0...  7.22 us
    pallas_call x1, Pallas kernels, call_logits(): pl.pallas_call(logits_kernel, out_shape=(jax.ShapeDtypeStruct((cols, rows...  6.18 us
    pallas_call x1, Pallas kernels, call_grad(): pl.pallas_call(grad_kernel, out_shape=(out,) * 8, in_specs=[hbm] * 8, out...  6.07 us
  transfers between devices with their start and end apart: 46, of which 29 were waited for; matrix products, arithmetic and copies ran while one was open for 2% of the time, Pallas kernels for 3%

profile of v4, /device:TPU:32, one launch (start us, length us, event | category | flops | bytes accessed | tf_op | source)
XLA Modules:
  0.0 212.8 jit_solution(3536634384509778438)
XLA Ops:
  0.6 6.4 %collective-permute-start = (bf16[128,128]{1,0:T(8,128)(2,1)}, bf16[128,128]{1,0:T(8,128)(2,1)S(1)}, u32[]{:S(2)}, u32[]{:S(2)}) collective-permute-start(bf16[128,128]{1,0:T(8,128)(2,1)} %param.7), channel_id=1, source_target_pairs={{0,1},{1,0},{2,3},{3,2},{4,5},{5,4},{6,7},{7,6},{8,9},{9,8},{10,11... | collective-permute-start | bytes 98312 | tf_op jit(solution)/shard_map/ppermute | solution.py:15
  7.0 2.1 collective-permute-done
  14.8 2.9 %collective-permute-done.10 = bf16[128,256]{1,0:T(8,128)(2,1)S(1)} collective-permute-done((bf16[128,256]{1,0:T(8,128)(2,1)S(1)}, bf16[128,256]{1,0:T(8,128)(2,1)S(1)}, u32[]{:S(2)}, u32[]{:S(2)}) %collective-permute-start.10) | collective-permute-done | bytes 65568 | tf_op jit(solution)/shard_map/ppermute | solution.py:15
  18.8 2.4 %broadcast_in_dim.6 = bf16[16,512,256]{2,1,0:T(8,128)(2,1)} broadcast(bf16[512,256]{1,0:T(8,128)(2,1)S(1)} %pad_maximum_fusion.1), dimensions={1,2} | broadcast | bytes 4456448 | tf_op jit(solution)/shard_map/broadcast_in_dim | solution.py:269
  21.2 7.2 %all-to-all-start = ((bf16[16,512,256]{2,1,0:T(8,128)(2,1)}), bf16[16,512,256]{2,1,0:T(8,128)(2,1)}, u32[]{:S(2)}, u32[]{:S(2)}) async-start(bf16[16,512,256]{2,1,0:T(8,128)(2,1)} %broadcast_in_dim.6), calls=%async_computation | async-start | bytes 8388608 | tf_op jit(solution)/shard_map/all_to_all | solution.py:269
  32.4 18.3 %collective-permute-done.2.refs_1_ = bf16[512,512]{1,0:T(8,128)(2,1)S(1)} collective-permute-done((bf16[512,512]{1,0:T(8,128)(2,1)S(1)}, bf16[512,512]{1,0:T(8,128)(2,1)S(1)}, u32[]{:S(2)}, u32[]{:S(2)}) %collective-permute-start.2) | collective-permute-done | bytes 524320 | tf_op jit(solution)/shard_map/ppermute | solution.py:15
  50.8 15.4 %collective-permute-done.4.refs_2_ = bf16[512,512]{1,0:T(8,128)(2,1)S(1)} collective-permute-done((bf16[512,512]{1,0:T(8,128)(2,1)S(1)}, bf16[512,512]{1,0:T(8,128)(2,1)S(1)}, u32[]{:S(2)}, u32[]{:S(2)}) %collective-permute-start.4) | collective-permute-done | bytes 524320 | tf_op jit(solution)/shard_map/ppermute | solution.py:15
  66.2 9.7 %collective-permute-done.5.refs_3_ = bf16[512,512]{1,0:T(8,128)(2,1)S(1)} collective-permute-done((bf16[512,512]{1,0:T(8,128)(2,1)S(1)}, bf16[512,512]{1,0:T(8,128)(2,1)S(1)}, u32[]{:S(2)}, u32[]{:S(2)}) %collective-permute-start.5) | collective-permute-done | bytes 524320 | tf_op jit(solution)/shard_map/ppermute | solution.py:15
  81.1 6.2 %logits_block.1 = (f32[512,512]{1,0:T(8,128)}, f32[2,512]{1,0:T(2,128)}) custom-call(bf16[512,512]{1,0:T(8,128)(2,1)} %copy-done.3, bf16[512,512]{1,0:T(8,128)(2,1)} %copy-done.5, bf16[512,512]{1,0:T(8,128)(2,1)} %copy-done.6, bf16[512,512]{1,0:T(8,128)(2,1)} %copy-done.7, bf16[512,512]{1,0:T(8,128)(2,1)} %copy-done.8, bf16[512,512]{1,0:T(8,128)(2,1)} %copy-done.9, ...), custom_call_target="tpu_custom_call" | custom-call | flops 2147483648 | bytes 8388608 | tf_op jit(solution)/shard_map/logits_block/pallas_call | solution.py:171
  89.2 4.5 %collective-permute-done.14 = bf16[144,512]{1,0:T(8,128)(2,1)S(1)} collective-permute-done((bf16[144,512]{1,0:T(8,128)(2,1)S(1)}, bf16[144,512]{1,0:T(8,128)(2,1)S(1)}, u32[]{:S(2)}, u32[]{:S(2)}) %collective-permute-start.14) | collective-permute-done | bytes 147488 | tf_op jit(solution)/shard_map/ppermute | solution.py:15
  97.2 3.2 %teacher_block.1 = (f32[512,512]{1,0:T(8,128)}, s32[1,512]{1,0:T(1,128)}, f32[8,512]{1,0:T(8,128)}) custom-call(s32[8]{0:T(128)} %pairing.1, bf16[8,144,512]{2,1,0:T(8,128)(2,1)} %copy-done.4, f32[512,512]{1,0:T(8,128)} %get-tuple-element.31.logits, f32[2,512]{1,0:T(2,128)} %get-tuple-element.40.student), custom_call_target="tpu_custom_call" | custom-call | flops 2097152 | bytes 3145728 | tf_op jit(solution)/shard_map/teacher_block/pallas_call | solution.py:198
  100.3 2.8 %collective-permute-start.16 = (f32[8,512]{1,0:T(8,128)}, f32[8,512]{1,0:T(8,128)S(1)}, u32[]{:S(2)}, u32[]{:S(2)}) collective-permute-start(f32[8,512]{1,0:T(8,128)} %get-tuple-element.41), channel_id=1, source_target_pairs={{0,24},{8,16},{16,8},{24,0},{1,25},{9,17},{17,9},{25,1},{2,26},{10... | collective-permute-start | bytes 49160 | tf_op jit(solution)/shard_map/ppermute | solution.py:15
  105.5 3.1 %collective-permute-done.17 = f32[8,512]{1,0:T(8,128)S(1)} collective-permute-done((f32[8,512]{1,0:T(8,128)}, f32[8,512]{1,0:T(8,128)S(1)}, u32[]{:S(2)}, u32[]{:S(2)}) %collective-permute-start.17) | collective-permute-done | bytes 16416 | tf_op jit(solution)/shard_map/ppermute | solution.py:15
  109.4 2.8 %collective-permute-start.19 = (f32[8,512]{1,0:T(8,128)S(1)}, f32[8,512]{1,0:T(8,128)S(1)}, u32[]{:S(2)}, u32[]{:S(2)}) collective-permute-start(f32[8,512]{1,0:T(8,128)S(1)} %pad_maximum_fusion.5), channel_id=1, source_target_pairs={{0,6},{2,4},{4,2},{6,0},{1,7},{3,5},{5,3},{7,1},{8,14},{10,12},{12... | collective-permute-start | bytes 49160 | tf_op jit(solution)/shard_map/ppermute | solution.py:15
  114.4 3.0 %collective-permute-done.20 = f32[8,512]{1,0:T(8,128)S(1)} collective-permute-done((f32[8,512]{1,0:T(8,128)S(1)}, f32[8,512]{1,0:T(8,128)S(1)}, u32[]{:S(2)}, u32[]{:S(2)}) %collective-permute-start.20) | collective-permute-done | bytes 16416 | tf_op jit(solution)/shard_map/ppermute | solution.py:15
  119.1 2.0 collective-permute-start.24
  123.1 4.6 %collective-permute-start.25 = (f32[8,512]{1,0:T(8,128)S(1)}, f32[8,512]{1,0:T(8,128)S(1)}, u32[]{:S(2)}, u32[]{:S(2)}) collective-permute-start(f32[8,512]{1,0:T(8,128)S(1)} %pad_maximum_fusion.7), channel_id=1, source_target_pairs={{0,1},{1,0},{2,3},{3,2},{4,5},{5,4},{6,7},{7,6},{8,9},{9,8},{10,11... | collective-permute-start | bytes 49160 | tf_op jit(solution)/shard_map/ppermute | solution.py:15
  127.7 3.1 %collective-permute-done.25 = f32[8,512]{1,0:T(8,128)S(1)} collective-permute-done((f32[8,512]{1,0:T(8,128)S(1)}, f32[8,512]{1,0:T(8,128)S(1)}, u32[]{:S(2)}, u32[]{:S(2)}) %collective-permute-start.25) | collective-permute-done | bytes 16416 | tf_op jit(solution)/shard_map/ppermute | solution.py:15
  137.5 16.4 %collective-permute-done.27.refs_4_ = bf16[256,512]{1,0:T(8,128)(2,1)S(1)} collective-permute-done((bf16[256,512]{1,0:T(8,128)(2,1)S(1)}, bf16[256,512]{1,0:T(8,128)(2,1)S(1)}, u32[]{:S(2)}, u32[]{:S(2)}) %collective-permute-start.27) | collective-permute-done | bytes 262176 | tf_op jit(solution)/shard_map/ppermute | solution.py:15
  153.9 5.6 %collective-permute-done.28.refs_5_ = bf16[256,512]{1,0:T(8,128)(2,1)S(1)} collective-permute-done((bf16[256,512]{1,0:T(8,128)(2,1)S(1)}, bf16[256,512]{1,0:T(8,128)(2,1)S(1)}, u32[]{:S(2)}, u32[]{:S(2)}) %collective-permute-start.28) | collective-permute-done | bytes 262176 | tf_op jit(solution)/shard_map/ppermute | solution.py:15
  159.5 4.1 %collective-permute-done.29.refs_6_ = bf16[256,512]{1,0:T(8,128)(2,1)S(1)} collective-permute-done((bf16[256,512]{1,0:T(8,128)(2,1)S(1)}, bf16[256,512]{1,0:T(8,128)(2,1)S(1)}, u32[]{:S(2)}, u32[]{:S(2)}) %collective-permute-start.29) | collective-permute-done | bytes 262176 | tf_op jit(solution)/shard_map/ppermute | solution.py:15
  163.7 2.8 %collective-permute-done.30.refs_7_ = bf16[256,512]{1,0:T(8,128)(2,1)S(1)} collective-permute-done((bf16[256,512]{1,0:T(8,128)(2,1)S(1)}, bf16[256,512]{1,0:T(8,128)(2,1)S(1)}, u32[]{:S(2)}, u32[]{:S(2)}) %collective-permute-start.30) | collective-permute-done | bytes 262176 | tf_op jit(solution)/shard_map/ppermute | solution.py:15
  167.2 6.1 %grad_block.1 = (f32[4,64,256]{2,1,0:T(8,128)}, f32[4,64,256]{2,1,0:T(8,128)}, f32[4,64,256]{2,1,0:T(8,128)}, f32[4,64,256]{2,1,0:T(8,128)}, f32[4,64,256]{2,1,0...) custom-call(bf16[512,2048]{1,0:T(8,128)(2,1)} %refs_0_.1, ...), custom_call_target="tpu_custom_call" | custom-call | flops 2147483648 | bytes 6291456 | tf_op jit(solution)/shard_map/grad_block/pallas_call | solution.py:224
  173.6 2.6 %collective-permute-start.32 = (f32[4,64,256]{2,1,0:T(8,128)}, f32[4,64,256]{2,1,0:T(8,128)S(1)}, u32[]{:S(2)}, u32[]{:S(2)}) collective-permute-start(f32[4,64,256]{2,1,0:T(8,128)} %get-tuple-element.46), channel_id=1, source_target_pairs={{0,16},{8,24},{16,0},{24,8},{1,17},{9,25},{17,1},{25,9},{2,18},{10... | collective-permute-start | bytes 786440 | tf_op jit(solution)/shard_map/ppermute | solution.py:15
  178.4 2.6 %collective-permute-start.38 = (f32[4,64,256]{2,1,0:T(8,128)}, f32[4,64,256]{2,1,0:T(8,128)S(1)}, u32[]{:S(2)}, u32[]{:S(2)}) collective-permute-start(f32[4,64,256]{2,1,0:T(8,128)} %get-tuple-element.50), channel_id=1, source_target_pairs={{0,4},{2,6},{4,0},{6,2},{1,5},{3,7},{5,1},{7,3},{8,12},{10,14},{12... | collective-permute-start | bytes 786440 | tf_op jit(solution)/shard_map/ppermute | solution.py:15
  182.8 2.2 %collective-permute-done.32 = f32[4,64,256]{2,1,0:T(8,128)S(1)} collective-permute-done((f32[4,64,256]{2,1,0:T(8,128)}, f32[4,64,256]{2,1,0:T(8,128)S(1)}, u32[]{:S(2)}, u32[]{:S(2)}) %collective-permute-start.32) | collective-permute-done | bytes 262176 | tf_op jit(solution)/shard_map/ppermute | solution.py:15
  185.0 2.5 %collective-permute-done.33 = f32[4,64,256]{2,1,0:T(8,128)S(1)} collective-permute-done((f32[4,64,256]{2,1,0:T(8,128)}, f32[4,64,256]{2,1,0:T(8,128)S(1)}, u32[]{:S(2)}, u32[]{:S(2)}) %collective-permute-start.33) | collective-permute-done | bytes 262176 | tf_op jit(solution)/shard_map/ppermute | solution.py:15
  188.9 2.6 %collective-permute-start.35 = (f32[64,256]{1,0:T(8,128)S(1)}, f32[64,256]{1,0:T(8,128)S(1)}, u32[]{:S(2)}, u32[]{:S(2)}) collective-permute-start(f32[64,256]{1,0:T(8,128)S(1)} %get-tuple-element.85), channel_id=1, source_target_pairs={{0,4},{2,6},{4,0},{6,2},{1,5},{3,7},{5,1},{7,3},{8,12},{10,14},{12... | collective-permute-start | bytes 196616 | tf_op jit(solution)/shard_map/ppermute | solution.py:15
  193.6 3.3 %collective-permute-start.41 = (f32[64,256]{1,0:T(8,128)S(1)}, f32[64,256]{1,0:T(8,128)S(1)}, u32[]{:S(2)}, u32[]{:S(2)}) collective-permute-start(f32[64,256]{1,0:T(8,128)S(1)} %get-tuple-element.88), channel_id=1, source_target_pairs={{0,16},{8,24},{16,0},{24,8},{1,17},{9,25},{17,1},{25,9},{2,18},{10... | collective-permute-start | bytes 196616 | tf_op jit(solution)/shard_map/ppermute | solution.py:15
  199.8 2.5 %collective-permute-done.42 = f32[64,256]{1,0:T(8,128)S(1)} collective-permute-done((f32[64,256]{1,0:T(8,128)S(1)}, f32[64,256]{1,0:T(8,128)S(1)}, u32[]{:S(2)}, u32[]{:S(2)}) %collective-permute-start.42) | collective-permute-done | bytes 65568 | tf_op jit(solution)/shard_map/ppermute | solution.py:15
  202.4 4.2 %collective-permute-start.43 = (f32[2,16,512]{2,1,0:T(8,128)S(1)}, f32[2,16,512]{2,1,0:T(8,128)S(1)}, u32[]{:S(2)}, u32[]{:S(2)}) collective-permute-start(f32[2,16,512]{2,1,0:T(8,128)S(1)} %select_bitcast_fusion), channel_id=1, source_target_pairs={{0,1},{1,0},{2,3},{3,2},{4,5},{5,4},{6,7},{7,6},{8,9},{9,8},{10,11... | collective-permute-start | bytes 196616 | tf_op jit(solution)/shard_map/ppermute | solution.py:15
  206.7 4.1 %collective-permute-done.43 = f32[2,16,512]{2,1,0:T(8,128)S(1)} collective-permute-done((f32[2,16,512]{2,1,0:T(8,128)S(1)}, f32[2,16,512]{2,1,0:T(8,128)S(1)}, u32[]{:S(2)}, u32[]{:S(2)}) %collective-permute-start.43) | collective-permute-done | bytes 65568 | tf_op jit(solution)/shard_map/ppermute | solution.py:15
  (162 shorter events, 50.2 us)
Async XLA Ops:
  0.6 8.5 %collective-permute-start = (bf16[128,128]{1,0:T(8,128)(2,1)}, bf16[128,128]{1,0:T(8,128)(2,1)S(1)}, u32[]{:S(2)}, u32[]{:S(2)}) collective-permute-start(bf16[128,128]{1,0:T(8,128)(2,1)} %param.7), channel_id=1, source_target_pairs={{0,1},{1,0},{2,3},{3,2},{4,5},{5,4},{6,7},{7,6},{8,9},{9,8},{10,11... | collective-permute-start | bytes 98312 | tf_op jit(solution)/shard_map/ppermute | solution.py:15
  11.5 6.2 %collective-permute-start.10 = (bf16[128,256]{1,0:T(8,128)(2,1)S(1)}, bf16[128,256]{1,0:T(8,128)(2,1)S(1)}, u32[]{:S(2)}, u32[]{:S(2)}) collective-permute-start(bf16[128,256]{1,0:T(8,128)(2,1)S(1)} %pad_maximum_fusion.3), channel_id=1, source_target_pairs={{0,192},{64,128},{128,64},{192,0},{1,193},{65,129},{129,65},{193,1... | collective-permute-start | bytes 196616 | tf_op jit(solution)/shard_map/ppermute | solution.py:15
  21.2 59.9 %all-to-all-start = ((bf16[16,512,256]{2,1,0:T(8,128)(2,1)}), bf16[16,512,256]{2,1,0:T(8,128)(2,1)}, u32[]{:S(2)}, u32[]{:S(2)}) async-start(bf16[16,512,256]{2,1,0:T(8,128)(2,1)} %broadcast_in_dim.6), calls=%async_computation | async-start | bytes 8388608 | tf_op jit(solution)/shard_map/all_to_all | solution.py:269
  28.8 22.0 %collective-permute-start.2 = (bf16[512,512]{1,0:T(8,128)(2,1)S(1)}, bf16[512,512]{1,0:T(8,128)(2,1)S(1)}, u32[]{:S(2)}, u32[]{:S(2)}) collective-permute-start(bf16[512,512]{1,0:T(8,128)(2,1)S(1)} %get-tuple-element.27), channel_id=1, source_target_pairs={{0,64},{64,0},{128,192},{192,128},{1,65},{65,1},{129,193},{193,129... | collective-permute-start | bytes 1572872 | tf_op jit(solution)/shard_map/ppermute | solution.py:15
  30.7 35.5 %collective-permute-start.4 = (bf16[512,512]{1,0:T(8,128)(2,1)S(1)}, bf16[512,512]{1,0:T(8,128)(2,1)S(1)}, u32[]{:S(2)}, u32[]{:S(2)}) collective-permute-start(bf16[512,512]{1,0:T(8,128)(2,1)S(1)} %get-tuple-element.29), channel_id=1, source_target_pairs={{0,128},{64,192},{128,0},{192,64},{1,129},{65,193},{129,1},{193,65... | collective-permute-start | bytes 1572872 | tf_op jit(solution)/shard_map/ppermute | solution.py:15
  31.3 44.5 %collective-permute-start.5 = (bf16[512,512]{1,0:T(8,128)(2,1)S(1)}, bf16[512,512]{1,0:T(8,128)(2,1)S(1)}, u32[]{:S(2)}, u32[]{:S(2)}) collective-permute-start(bf16[512,512]{1,0:T(8,128)(2,1)S(1)} %get-tuple-element.30), channel_id=1, source_target_pairs={{0,192},{64,128},{128,64},{192,0},{1,193},{65,129},{129,65},{193,1... | collective-permute-start | bytes 1572872 | tf_op jit(solution)/shard_map/ppermute | solution.py:15
  32.4 44.5 %collective-permute-start.6 = (bf16[512,512]{1,0:T(8,128)(2,1)S(1)}, bf16[512,512]{1,0:T(8,128)(2,1)S(1)}, u32[]{:S(2)}, u32[]{:S(2)}) collective-permute-start(bf16[512,512]{1,0:T(8,128)(2,1)S(1)} %get-tuple-element.76.refs_0_), channel_id=1, source_target_pairs={{0,32},{32,0},{1,33},{33,1},{2,34},{34,2},{3,35},{35,3},{4,36},{36... | collective-permute-start | bytes 1572872 | tf_op jit(solution)/shard_map/ppermute | solution.py:15
  50.8 28.0 %collective-permute-start.7 = (bf16[512,512]{1,0:T(8,128)(2,1)S(1)}, bf16[512,512]{1,0:T(8,128)(2,1)S(1)}, u32[]{:S(2)}, u32[]{:S(2)}) collective-permute-start(bf16[512,512]{1,0:T(8,128)(2,1)S(1)} %collective-permute-done.2.refs_1_), channel_id=1, source_target_pairs={{0,32},{32,0},{1,33},{33,1},{2,34},{34,2},{3,35},{35,3},{4,36},{36... | collective-permute-start | bytes 1572872 | tf_op jit(solution)/shard_map/ppermute | solution.py:15
  66.2 14.1 %collective-permute-start.8 = (bf16[512,512]{1,0:T(8,128)(2,1)S(1)}, bf16[512,512]{1,0:T(8,128)(2,1)S(1)}, u32[]{:S(2)}, u32[]{:S(2)}) collective-permute-start(bf16[512,512]{1,0:T(8,128)(2,1)S(1)} %collective-permute-done.4.refs_2_), channel_id=1, source_target_pairs={{0,32},{32,0},{1,33},{33,1},{2,34},{34,2},{3,35},{35,3},{4,36},{36... | collective-permute-start | bytes 1572872 | tf_op jit(solution)/shard_map/ppermute | solution.py:15
  76.7 10.6 %collective-permute-start.12 = (bf16[144,512]{1,0:T(8,128)(2,1)}, bf16[144,512]{1,0:T(8,128)(2,1)S(1)}, u32[]{:S(2)}, u32[]{:S(2)}) collective-permute-start(bf16[144,512]{1,0:T(8,128)(2,1)} %get-tuple-element.33), channel_id=1, source_target_pairs={{0,64},{64,0},{128,192},{192,128},{1,65},{65,1},{129,193},{193,129... | collective-permute-start | bytes 442376 | tf_op jit(solution)/shard_map/ppermute | solution.py:15
  76.8 12.3 %collective-permute-start.13 = (bf16[144,512]{1,0:T(8,128)(2,1)S(1)}, bf16[144,512]{1,0:T(8,128)(2,1)S(1)}, u32[]{:S(2)}, u32[]{:S(2)}) collective-permute-start(bf16[144,512]{1,0:T(8,128)(2,1)S(1)} %get-tuple-element.34), channel_id=1, source_target_pairs={{0,128},{64,192},{128,0},{192,64},{1,129},{65,193},{129,1},{193,65... | collective-permute-start | bytes 442376 | tf_op jit(solution)/shard_map/ppermute | solution.py:15
  78.7 15.0 %collective-permute-start.14 = (bf16[144,512]{1,0:T(8,128)(2,1)S(1)}, bf16[144,512]{1,0:T(8,128)(2,1)S(1)}, u32[]{:S(2)}, u32[]{:S(2)}) collective-permute-start(bf16[144,512]{1,0:T(8,128)(2,1)S(1)} %get-tuple-element.35), channel_id=1, source_target_pairs={{0,192},{64,128},{128,64},{192,0},{1,193},{65,129},{129,65},{193,1... | collective-permute-start | bytes 442376 | tf_op jit(solution)/shard_map/ppermute | solution.py:15
  103.1 5.5 %collective-permute-start.17 = (f32[8,512]{1,0:T(8,128)}, f32[8,512]{1,0:T(8,128)S(1)}, u32[]{:S(2)}, u32[]{:S(2)}) collective-permute-start(f32[8,512]{1,0:T(8,128)} %get-tuple-element.41), channel_id=1, source_target_pairs={{0,16},{8,24},{16,0},{24,8},{1,17},{9,25},{17,1},{25,9},{2,18},{10... | collective-permute-start | bytes 49160 | tf_op jit(solution)/shard_map/ppermute | solution.py:15
  121.1 38.4 %collective-permute-start.3 = (bf16[512,2048]{1,0:T(8,128)(2,1)S(1)}, bf16[512,2048]{1,0:T(8,128)(2,1)S(1)}, u32[]{:S(2)}, u32[]{:S(2)}) collective-permute-start(bf16[512,2048]{1,0:T(8,128)(2,1)S(1)} %copy-done.2), channel_id=1, source_target_pairs={{0,32},{32,0},{1,33},{33,1},{2,34},{34,2},{3,35},{35,3},{4,36},{36... | collective-permute-start | bytes 6291464 | tf_op jit(solution)/shard_map/ppermute | solution.py:15
  123.1 7.7 %collective-permute-start.25 = (f32[8,512]{1,0:T(8,128)S(1)}, f32[8,512]{1,0:T(8,128)S(1)}, u32[]{:S(2)}, u32[]{:S(2)}) collective-permute-start(f32[8,512]{1,0:T(8,128)S(1)} %pad_maximum_fusion.7), channel_id=1, source_target_pairs={{0,1},{1,0},{2,3},{3,2},{4,5},{5,4},{6,7},{7,6},{8,9},{9,8},{10,11... | collective-permute-start | bytes 49160 | tf_op jit(solution)/shard_map/ppermute | solution.py:15
  132.5 27.0 %collective-permute-start.26 = (bf16[512,512]{1,0:T(8,128)(2,1)S(1)}, bf16[512,512]{1,0:T(8,128)(2,1)S(1)}, u32[]{:S(2)}, u32[]{:S(2)}) collective-permute-start(bf16[512,512]{1,0:T(8,128)(2,1)S(1)} %subtract_convert_fusion.refs_2_), channel_id=1, source_target_pairs={{0,64},{64,0},{128,192},{192,128},{1,65},{65,1},{129,193},{193,129... | collective-permute-start | bytes 1572872 | tf_op jit(solution)/shard_map/ppermute | solution.py:15
  134.5 19.4 %collective-permute-start.27 = (bf16[256,512]{1,0:T(8,128)(2,1)S(1)}, bf16[256,512]{1,0:T(8,128)(2,1)S(1)}, u32[]{:S(2)}, u32[]{:S(2)}) collective-permute-start(bf16[256,512]{1,0:T(8,128)(2,1)S(1)} %get-tuple-element.83), channel_id=1, source_target_pairs={{0,128},{64,192},{128,0},{192,64},{1,129},{65,193},{129,1},{193,65... | collective-permute-start | bytes 786440 | tf_op jit(solution)/shard_map/ppermute | solution.py:15
  135.5 24.0 %collective-permute-start.28 = (bf16[256,512]{1,0:T(8,128)(2,1)S(1)}, bf16[256,512]{1,0:T(8,128)(2,1)S(1)}, u32[]{:S(2)}, u32[]{:S(2)}) collective-permute-start(bf16[256,512]{1,0:T(8,128)(2,1)S(1)} %get-tuple-element.82), channel_id=1, source_target_pairs={{0,128},{64,192},{128,0},{192,64},{1,129},{65,193},{129,1},{193,65... | collective-permute-start | bytes 786440 | tf_op jit(solution)/shard_map/ppermute | solution.py:15
  153.9 9.8 %collective-permute-start.29 = (bf16[256,512]{1,0:T(8,128)(2,1)S(1)}, bf16[256,512]{1,0:T(8,128)(2,1)S(1)}, u32[]{:S(2)}, u32[]{:S(2)}) collective-permute-start(bf16[256,512]{1,0:T(8,128)(2,1)S(1)} %collective-permute-done.27.refs_4_), channel_id=1, source_target_pairs={{0,64},{64,0},{128,192},{192,128},{1,65},{65,1},{129,193},{193,129... | collective-permute-start | bytes 786440 | tf_op jit(solution)/shard_map/ppermute | solution.py:15
  159.5 7.0 %collective-permute-start.30 = (bf16[256,512]{1,0:T(8,128)(2,1)S(1)}, bf16[256,512]{1,0:T(8,128)(2,1)S(1)}, u32[]{:S(2)}, u32[]{:S(2)}) collective-permute-start(bf16[256,512]{1,0:T(8,128)(2,1)S(1)} %collective-permute-done.28.refs_5_), channel_id=1, source_target_pairs={{0,64},{64,0},{128,192},{192,128},{1,65},{65,1},{129,193},{193,129... | collective-permute-start | bytes 786440 | tf_op jit(solution)/shard_map/ppermute | solution.py:15
  173.3 7.9 %collective-permute-start.31 = (f32[4,64,256]{2,1,0:T(8,128)}, f32[4,64,256]{2,1,0:T(8,128)S(1)}, u32[]{:S(2)}, u32[]{:S(2)}) collective-permute-start(f32[4,64,256]{2,1,0:T(8,128)} %get-tuple-element.45), channel_id=1, source_target_pairs={{0,8},{8,0},{16,24},{24,16},{1,9},{9,1},{17,25},{25,17},{2,10},{10... | collective-permute-start | bytes 786440 | tf_op jit(solution)/shard_map/ppermute | solution.py:15
  173.6 11.4 %collective-permute-start.32 = (f32[4,64,256]{2,1,0:T(8,128)}, f32[4,64,256]{2,1,0:T(8,128)S(1)}, u32[]{:S(2)}, u32[]{:S(2)}) collective-permute-start(f32[4,64,256]{2,1,0:T(8,128)} %get-tuple-element.46), channel_id=1, source_target_pairs={{0,16},{8,24},{16,0},{24,8},{1,17},{9,25},{17,1},{25,9},{2,18},{10... | collective-permute-start | bytes 786440 | tf_op jit(solution)/shard_map/ppermute | solution.py:15
  176.3 11.3 %collective-permute-start.33 = (f32[4,64,256]{2,1,0:T(8,128)}, f32[4,64,256]{2,1,0:T(8,128)S(1)}, u32[]{:S(2)}, u32[]{:S(2)}) collective-permute-start(f32[4,64,256]{2,1,0:T(8,128)} %get-tuple-element.47), channel_id=1, source_target_pairs={{0,24},{8,16},{16,8},{24,0},{1,25},{9,17},{17,9},{25,1},{2,26},{10... | collective-permute-start | bytes 786440 | tf_op jit(solution)/shard_map/ppermute | solution.py:15
  178.1 13.4 %collective-permute-start.37 = (f32[4,64,256]{2,1,0:T(8,128)}, f32[4,64,256]{2,1,0:T(8,128)S(1)}, u32[]{:S(2)}, u32[]{:S(2)}) collective-permute-start(f32[4,64,256]{2,1,0:T(8,128)} %get-tuple-element.49), channel_id=1, source_target_pairs={{0,2},{2,0},{4,6},{6,4},{1,3},{3,1},{5,7},{7,5},{8,10},{10,8},{12,... | collective-permute-start | bytes 786440 | tf_op jit(solution)/shard_map/ppermute | solution.py:15
  178.4 15.0 %collective-permute-start.38 = (f32[4,64,256]{2,1,0:T(8,128)}, f32[4,64,256]{2,1,0:T(8,128)S(1)}, u32[]{:S(2)}, u32[]{:S(2)}) collective-permute-start(f32[4,64,256]{2,1,0:T(8,128)} %get-tuple-element.50), channel_id=1, source_target_pairs={{0,4},{2,6},{4,0},{6,2},{1,5},{3,7},{5,1},{7,3},{8,12},{10,14},{12... | collective-permute-start | bytes 786440 | tf_op jit(solution)/shard_map/ppermute | solution.py:15
  181.3 12.1 %collective-permute-start.39 = (f32[4,64,256]{2,1,0:T(8,128)}, f32[4,64,256]{2,1,0:T(8,128)S(1)}, u32[]{:S(2)}, u32[]{:S(2)}) collective-permute-start(f32[4,64,256]{2,1,0:T(8,128)} %get-tuple-element.51), channel_id=1, source_target_pairs={{0,6},{2,4},{4,2},{6,0},{1,7},{3,5},{5,3},{7,1},{8,14},{10,12},{12... | collective-permute-start | bytes 786440 | tf_op jit(solution)/shard_map/ppermute | solution.py:15
  188.6 8.3 %collective-permute-start.34 = (f32[64,256]{1,0:T(8,128)S(1)}, f32[64,256]{1,0:T(8,128)S(1)}, u32[]{:S(2)}, u32[]{:S(2)}) collective-permute-start(f32[64,256]{1,0:T(8,128)S(1)} %get-tuple-element.86), channel_id=1, source_target_pairs={{0,2},{2,0},{4,6},{6,4},{1,3},{3,1},{5,7},{7,5},{8,10},{10,8},{12,... | collective-permute-start | bytes 196616 | tf_op jit(solution)/shard_map/ppermute | solution.py:15
  188.9 9.4 %collective-permute-start.35 = (f32[64,256]{1,0:T(8,128)S(1)}, f32[64,256]{1,0:T(8,128)S(1)}, u32[]{:S(2)}, u32[]{:S(2)}) collective-permute-start(f32[64,256]{1,0:T(8,128)S(1)} %get-tuple-element.85), channel_id=1, source_target_pairs={{0,4},{2,6},{4,0},{6,2},{1,5},{3,7},{5,1},{7,3},{8,12},{10,14},{12... | collective-permute-start | bytes 196616 | tf_op jit(solution)/shard_map/ppermute | solution.py:15
  191.6 6.7 %collective-permute-start.36 = (f32[64,256]{1,0:T(8,128)S(1)}, f32[64,256]{1,0:T(8,128)S(1)}, u32[]{:S(2)}, u32[]{:S(2)}) collective-permute-start(f32[64,256]{1,0:T(8,128)S(1)} %get-tuple-element.84), channel_id=1, source_target_pairs={{0,6},{2,4},{4,2},{6,0},{1,7},{3,5},{5,3},{7,1},{8,14},{10,12},{12... | collective-permute-start | bytes 196616 | tf_op jit(solution)/shard_map/ppermute | solution.py:15
  193.6 6.2 %collective-permute-start.41 = (f32[64,256]{1,0:T(8,128)S(1)}, f32[64,256]{1,0:T(8,128)S(1)}, u32[]{:S(2)}, u32[]{:S(2)}) collective-permute-start(f32[64,256]{1,0:T(8,128)S(1)} %get-tuple-element.88), channel_id=1, source_target_pairs={{0,16},{8,24},{16,0},{24,8},{1,17},{9,25},{17,1},{25,9},{2,18},{10... | collective-permute-start | bytes 196616 | tf_op jit(solution)/shard_map/ppermute | solution.py:15
  196.9 5.5 %collective-permute-start.42 = (f32[64,256]{1,0:T(8,128)S(1)}, f32[64,256]{1,0:T(8,128)S(1)}, u32[]{:S(2)}, u32[]{:S(2)}) collective-permute-start(f32[64,256]{1,0:T(8,128)S(1)} %get-tuple-element.87), channel_id=1, source_target_pairs={{0,24},{8,16},{16,8},{24,0},{1,25},{9,17},{17,9},{25,1},{2,26},{10... | collective-permute-start | bytes 196616 | tf_op jit(solution)/shard_map/ppermute | solution.py:15
  202.4 8.4 %collective-permute-start.43 = (f32[2,16,512]{2,1,0:T(8,128)S(1)}, f32[2,16,512]{2,1,0:T(8,128)S(1)}, u32[]{:S(2)}, u32[]{:S(2)}) collective-permute-start(f32[2,16,512]{2,1,0:T(8,128)S(1)} %select_bitcast_fusion), channel_id=1, source_target_pairs={{0,1},{1,0},{2,3},{3,2},{4,5},{5,4},{6,7},{7,6},{8,9},{9,8},{10,11... | collective-permute-start | bytes 196616 | tf_op jit(solution)/shard_map/ppermute | solution.py:15
  (34 other events, 336.0 us)

commit v5 on v4

--- a/solution.py
+++ b/solution.py
@@ -204,7 +204,7 @@
         ),
         in_specs=[pl.BlockSpec(memory_space=pltpu.SMEM)] + [vmem] * 3,
         out_specs=(vmem,) * 3,
-        compiler_params=pltpu.CompilerParams(vmem_limit_bytes=VMEM_BYTES),
+        compiler_params=pltpu.CompilerParams(vmem_limit_bytes=VMEM_BYTES // 4),
         cost_estimate=pl.CostEstimate(
             flops=8 * rows * cols,
             bytes_accessed=12 * rows * cols,

time: 215 us -> 210 us (0.977)
  transfers between devices with their start and end apart: 46 -> 46, of which waited for: 29 -> 29; matrix products, arithmetic and copies ran while one was open for 2% -> 1% of each run, Pallas kernels for 3% -> 3%
where the time goes in v5:
time: 210 us; the launch traced here: 207 us
  waiting for transfers between devices  113 us (54%)
  starting transfers between devices  69.9 us (33%)
  Pallas kernels  13.5 us (6%)
  local copies, waits for them, and re-layouts  5.96 us (3%)
  other arithmetic  3.45 us (2%)
    ppermute x45, waiting for transfers between devices, swap(): return lax.ppermute(value, axis, [(i, i ^ flip) for i in range(AXES[axis])])  113 us
    ppermute x45, starting transfers between devices, swap(): return lax.ppermute(value, axis, [(i, i ^ flip) for i in range(AXES[axis])])  62.6 us
    all_to_all x1, starting transfers between devices, per_device(): lax.all_to_all(jnp.broadcast_to(feats, (16, *feats.shape)), ('x', 'y'), 0...  7.22 us
    pallas_call x1, Pallas kernels, call_logits(): pl.pallas_call(logits_kernel, out_shape=(jax.ShapeDtypeStruct((cols, rows...  6.17 us
    pallas_call x1, Pallas kernels, call_grad(): pl.pallas_call(grad_kernel, out_shape=(out,) * 8, in_specs=[hbm] * 8, out...  6.06 us
  transfers between devices with their start and end apart: 46, of which 29 were waited for; matrix products, arithmetic and copies ran while one was open for 1% of the time, Pallas kernels for 3%

profile of v5, /device:TPU:32, one launch (start us, length us, event | category | flops | bytes accessed | tf_op | source)
XLA Modules:
  0.0 207.1 jit_solution(14734675790385733752)
XLA Ops:
  0.6 6.4 %collective-permute-start = (bf16[128,128]{1,0:T(8,128)(2,1)}, bf16[128,128]{1,0:T(8,128)(2,1)S(1)}, u32[]{:S(2)}, u32[]{:S(2)}) collective-permute-start(bf16[128,128]{1,0:T(8,128)(2,1)} %param.7), channel_id=1, source_target_pairs={{0,1},{1,0},{2,3},{3,2},{4,5},{5,4},{6,7},{7,6},{8,9},{9,8},{10,11... | collective-permute-start | bytes 98312 | tf_op jit(solution)/shard_map/ppermute | solution.py:15
  7.0 2.1 %collective-permute-done = bf16[128,128]{1,0:T(8,128)(2,1)S(1)} collective-permute-done((bf16[128,128]{1,0:T(8,128)(2,1)}, bf16[128,128]{1,0:T(8,128)(2,1)S(1)}, u32[]{:S(2)}, u32[]{:S(2)}) %collective-permute-start) | collective-permute-done | bytes 32800 | tf_op jit(solution)/shard_map/ppermute | solution.py:15
  11.5 2.0 collective-permute-start.10
  14.8 2.9 %collective-permute-done.10 = bf16[128,256]{1,0:T(8,128)(2,1)S(1)} collective-permute-done((bf16[128,256]{1,0:T(8,128)(2,1)S(1)}, bf16[128,256]{1,0:T(8,128)(2,1)S(1)}, u32[]{:S(2)}, u32[]{:S(2)}) %collective-permute-start.10) | collective-permute-done | bytes 65568 | tf_op jit(solution)/shard_map/ppermute | solution.py:15
  18.8 2.5 %broadcast_in_dim.6 = bf16[16,512,256]{2,1,0:T(8,128)(2,1)} broadcast(bf16[512,256]{1,0:T(8,128)(2,1)S(1)} %pad_maximum_fusion.1), dimensions={1,2} | broadcast | bytes 4456448 | tf_op jit(solution)/shard_map/broadcast_in_dim | solution.py:269
  21.3 7.2 %all-to-all-start = ((bf16[16,512,256]{2,1,0:T(8,128)(2,1)}), bf16[16,512,256]{2,1,0:T(8,128)(2,1)}, u32[]{:S(2)}, u32[]{:S(2)}) async-start(bf16[16,512,256]{2,1,0:T(8,128)(2,1)} %broadcast_in_dim.6), calls=%async_computation | async-start | bytes 8388608 | tf_op jit(solution)/shard_map/all_to_all | solution.py:269
  32.5 18.3 %collective-permute-done.2.refs_1_ = bf16[512,512]{1,0:T(8,128)(2,1)S(1)} collective-permute-done((bf16[512,512]{1,0:T(8,128)(2,1)S(1)}, bf16[512,512]{1,0:T(8,128)(2,1)S(1)}, u32[]{:S(2)}, u32[]{:S(2)}) %collective-permute-start.2) | collective-permute-done | bytes 524320 | tf_op jit(solution)/shard_map/ppermute | solution.py:15
  50.8 15.4 %collective-permute-done.4.refs_2_ = bf16[512,512]{1,0:T(8,128)(2,1)S(1)} collective-permute-done((bf16[512,512]{1,0:T(8,128)(2,1)S(1)}, bf16[512,512]{1,0:T(8,128)(2,1)S(1)}, u32[]{:S(2)}, u32[]{:S(2)}) %collective-permute-start.4) | collective-permute-done | bytes 524320 | tf_op jit(solution)/shard_map/ppermute | solution.py:15
  66.2 9.7 %collective-permute-done.5.refs_3_ = bf16[512,512]{1,0:T(8,128)(2,1)S(1)} collective-permute-done((bf16[512,512]{1,0:T(8,128)(2,1)S(1)}, bf16[512,512]{1,0:T(8,128)(2,1)S(1)}, u32[]{:S(2)}, u32[]{:S(2)}) %collective-permute-start.5) | collective-permute-done | bytes 524320 | tf_op jit(solution)/shard_map/ppermute | solution.py:15
  81.1 6.2 %logits_block.1 = (f32[512,512]{1,0:T(8,128)}, f32[2,512]{1,0:T(2,128)}) custom-call(bf16[512,512]{1,0:T(8,128)(2,1)} %copy-done.5, bf16[512,512]{1,0:T(8,128)(2,1)} %copy-done.6, bf16[512,512]{1,0:T(8,128)(2,1)} %copy-done.7, bf16[512,512]{1,0:T(8,128)(2,1)} %copy-done.8, bf16[512,512]{1,0:T(8,128)(2,1)} %copy-done.9, bf16[512,512]{1,0:T(8,128)(2,1)} %copy-done.10, ...), custom_call_target="tpu_custom_call" | custom-call | flops 2147483648 | bytes 8388608 | tf_op jit(solution)/shard_map/logits_block/pallas_call | solution.py:171
  89.2 3.9 %collective-permute-done.14 = bf16[144,512]{1,0:T(8,128)(2,1)S(1)} collective-permute-done((bf16[144,512]{1,0:T(8,128)(2,1)S(1)}, bf16[144,512]{1,0:T(8,128)(2,1)S(1)}, u32[]{:S(2)}, u32[]{:S(2)}) %collective-permute-start.14) | collective-permute-done | bytes 147488 | tf_op jit(solution)/shard_map/ppermute | solution.py:15
  96.8 2.9 %collective-permute-start.16 = (f32[8,512]{1,0:T(8,128)S(1)}, f32[8,512]{1,0:T(8,128)S(1)}, u32[]{:S(2)}, u32[]{:S(2)}) collective-permute-start(f32[8,512]{1,0:T(8,128)S(1)} %get-tuple-element.41), channel_id=1, source_target_pairs={{0,24},{8,16},{16,8},{24,0},{1,25},{9,17},{17,9},{25,1},{2,26},{10... | collective-permute-start | bytes 49160 | tf_op jit(solution)/shard_map/ppermute | solution.py:15
  101.8 3.1 %collective-permute-done.17 = f32[8,512]{1,0:T(8,128)S(1)} collective-permute-done((f32[8,512]{1,0:T(8,128)S(1)}, f32[8,512]{1,0:T(8,128)S(1)}, u32[]{:S(2)}, u32[]{:S(2)}) %collective-permute-start.17) | collective-permute-done | bytes 16416 | tf_op jit(solution)/shard_map/ppermute | solution.py:15
  105.0 2.8 %collective-permute-start.19 = (f32[8,512]{1,0:T(8,128)S(1)}, f32[8,512]{1,0:T(8,128)S(1)}, u32[]{:S(2)}, u32[]{:S(2)}) collective-permute-start(f32[8,512]{1,0:T(8,128)S(1)} %pad_maximum_fusion.5), channel_id=1, source_target_pairs={{0,6},{2,4},{4,2},{6,0},{1,7},{3,5},{5,3},{7,1},{8,14},{10,12},{12... | collective-permute-start | bytes 49160 | tf_op jit(solution)/shard_map/ppermute | solution.py:15
  110.1 3.0 %collective-permute-done.20 = f32[8,512]{1,0:T(8,128)S(1)} collective-permute-done((f32[8,512]{1,0:T(8,128)S(1)}, f32[8,512]{1,0:T(8,128)S(1)}, u32[]{:S(2)}, u32[]{:S(2)}) %collective-permute-start.20) | collective-permute-done | bytes 16416 | tf_op jit(solution)/shard_map/ppermute | solution.py:15
  118.9 4.6 %collective-permute-start.25 = (f32[8,512]{1,0:T(8,128)S(1)}, f32[8,512]{1,0:T(8,128)S(1)}, u32[]{:S(2)}, u32[]{:S(2)}) collective-permute-start(f32[8,512]{1,0:T(8,128)S(1)} %pad_maximum_fusion.7), channel_id=1, source_target_pairs={{0,1},{1,0},{2,3},{3,2},{4,5},{5,4},{6,7},{7,6},{8,9},{9,8},{10,11... | collective-permute-start | bytes 49160 | tf_op jit(solution)/shard_map/ppermute | solution.py:15
  123.4 3.2 %collective-permute-done.25 = f32[8,512]{1,0:T(8,128)S(1)} collective-permute-done((f32[8,512]{1,0:T(8,128)S(1)}, f32[8,512]{1,0:T(8,128)S(1)}, u32[]{:S(2)}, u32[]{:S(2)}) %collective-permute-start.25) | collective-permute-done | bytes 16416 | tf_op jit(solution)/shard_map/ppermute | solution.py:15
  129.9 2.0 collective-permute-start.28
  131.9 16.4 %collective-permute-done.27.refs_4_ = bf16[256,512]{1,0:T(8,128)(2,1)S(1)} collective-permute-done((bf16[256,512]{1,0:T(8,128)(2,1)S(1)}, bf16[256,512]{1,0:T(8,128)(2,1)S(1)}, u32[]{:S(2)}, u32[]{:S(2)}) %collective-permute-start.27) | collective-permute-done | bytes 262176 | tf_op jit(solution)/shard_map/ppermute | solution.py:15
  148.3 5.6 %collective-permute-done.28.refs_5_ = bf16[256,512]{1,0:T(8,128)(2,1)S(1)} collective-permute-done((bf16[256,512]{1,0:T(8,128)(2,1)S(1)}, bf16[256,512]{1,0:T(8,128)(2,1)S(1)}, u32[]{:S(2)}, u32[]{:S(2)}) %collective-permute-start.28) | collective-permute-done | bytes 262176 | tf_op jit(solution)/shard_map/ppermute | solution.py:15
  153.9 4.2 %collective-permute-done.29.refs_6_ = bf16[256,512]{1,0:T(8,128)(2,1)S(1)} collective-permute-done((bf16[256,512]{1,0:T(8,128)(2,1)S(1)}, bf16[256,512]{1,0:T(8,128)(2,1)S(1)}, u32[]{:S(2)}, u32[]{:S(2)}) %collective-permute-start.29) | collective-permute-done | bytes 262176 | tf_op jit(solution)/shard_map/ppermute | solution.py:15
  158.1 2.8 %collective-permute-done.30.refs_7_ = bf16[256,512]{1,0:T(8,128)(2,1)S(1)} collective-permute-done((bf16[256,512]{1,0:T(8,128)(2,1)S(1)}, bf16[256,512]{1,0:T(8,128)(2,1)S(1)}, u32[]{:S(2)}, u32[]{:S(2)}) %collective-permute-start.30) | collective-permute-done | bytes 262176 | tf_op jit(solution)/shard_map/ppermute | solution.py:15
  161.7 6.1 %grad_block.1 = (f32[4,64,256]{2,1,0:T(8,128)}, f32[4,64,256]{2,1,0:T(8,128)}, f32[4,64,256]{2,1,0:T(8,128)}, f32[4,64,256]{2,1,0:T(8,128)}, f32[4,64,256]{2,1,0...) custom-call(bf16[512,2048]{1,0:T(8,128)(2,1)} %refs_0_.1, ...), custom_call_target="tpu_custom_call" | custom-call | flops 2147483648 | bytes 6291456 | tf_op jit(solution)/shard_map/grad_block/pallas_call | solution.py:224
  168.1 2.6 %collective-permute-start.32 = (f32[4,64,256]{2,1,0:T(8,128)}, f32[4,64,256]{2,1,0:T(8,128)S(1)}, u32[]{:S(2)}, u32[]{:S(2)}) collective-permute-start(f32[4,64,256]{2,1,0:T(8,128)} %get-tuple-element.46), channel_id=1, source_target_pairs={{0,16},{8,24},{16,0},{24,8},{1,17},{9,25},{17,1},{25,9},{2,18},{10... | collective-permute-start | bytes 786440 | tf_op jit(solution)/shard_map/ppermute | solution.py:15
  172.8 2.6 %collective-permute-start.38 = (f32[4,64,256]{2,1,0:T(8,128)}, f32[4,64,256]{2,1,0:T(8,128)S(1)}, u32[]{:S(2)}, u32[]{:S(2)}) collective-permute-start(f32[4,64,256]{2,1,0:T(8,128)} %get-tuple-element.50), channel_id=1, source_target_pairs={{0,4},{2,6},{4,0},{6,2},{1,5},{3,7},{5,1},{7,3},{8,12},{10,14},{12... | collective-permute-start | bytes 786440 | tf_op jit(solution)/shard_map/ppermute | solution.py:15
  177.2 2.1 %collective-permute-done.32 = f32[4,64,256]{2,1,0:T(8,128)S(1)} collective-permute-done((f32[4,64,256]{2,1,0:T(8,128)}, f32[4,64,256]{2,1,0:T(8,128)S(1)}, u32[]{:S(2)}, u32[]{:S(2)}) %collective-permute-start.32) | collective-permute-done | bytes 262176 | tf_op jit(solution)/shard_map/ppermute | solution.py:15
  179.3 2.5 %collective-permute-done.33 = f32[4,64,256]{2,1,0:T(8,128)S(1)} collective-permute-done((f32[4,64,256]{2,1,0:T(8,128)}, f32[4,64,256]{2,1,0:T(8,128)S(1)}, u32[]{:S(2)}, u32[]{:S(2)}) %collective-permute-start.33) | collective-permute-done | bytes 262176 | tf_op jit(solution)/shard_map/ppermute | solution.py:15
  183.2 2.6 %collective-permute-start.35 = (f32[64,256]{1,0:T(8,128)S(1)}, f32[64,256]{1,0:T(8,128)S(1)}, u32[]{:S(2)}, u32[]{:S(2)}) collective-permute-start(f32[64,256]{1,0:T(8,128)S(1)} %get-tuple-element.85), channel_id=1, source_target_pairs={{0,4},{2,6},{4,0},{6,2},{1,5},{3,7},{5,1},{7,3},{8,12},{10,14},{12... | collective-permute-start | bytes 196616 | tf_op jit(solution)/shard_map/ppermute | solution.py:15
  187.9 3.3 %collective-permute-start.41 = (f32[64,256]{1,0:T(8,128)S(1)}, f32[64,256]{1,0:T(8,128)S(1)}, u32[]{:S(2)}, u32[]{:S(2)}) collective-permute-start(f32[64,256]{1,0:T(8,128)S(1)} %get-tuple-element.88), channel_id=1, source_target_pairs={{0,16},{8,24},{16,0},{24,8},{1,17},{9,25},{17,1},{25,9},{2,18},{10... | collective-permute-start | bytes 196616 | tf_op jit(solution)/shard_map/ppermute | solution.py:15
  194.1 2.5 %collective-permute-done.42 = f32[64,256]{1,0:T(8,128)S(1)} collective-permute-done((f32[64,256]{1,0:T(8,128)S(1)}, f32[64,256]{1,0:T(8,128)S(1)}, u32[]{:S(2)}, u32[]{:S(2)}) %collective-permute-start.42) | collective-permute-done | bytes 65568 | tf_op jit(solution)/shard_map/ppermute | solution.py:15
  196.7 4.2 %collective-permute-start.43 = (f32[2,16,512]{2,1,0:T(8,128)S(1)}, f32[2,16,512]{2,1,0:T(8,128)S(1)}, u32[]{:S(2)}, u32[]{:S(2)}) collective-permute-start(f32[2,16,512]{2,1,0:T(8,128)S(1)} %select_bitcast_fusion), channel_id=1, source_target_pairs={{0,1},{1,0},{2,3},{3,2},{4,5},{5,4},{6,7},{7,6},{8,9},{9,8},{10,11... | collective-permute-start | bytes 196616 | tf_op jit(solution)/shard_map/ppermute | solution.py:15
  200.9 4.1 %collective-permute-done.43 = f32[2,16,512]{2,1,0:T(8,128)S(1)} collective-permute-done((f32[2,16,512]{2,1,0:T(8,128)S(1)}, f32[2,16,512]{2,1,0:T(8,128)S(1)}, u32[]{:S(2)}, u32[]{:S(2)}) %collective-permute-start.43) | collective-permute-done | bytes 65568 | tf_op jit(solution)/shard_map/ppermute | solution.py:15
  (164 shorter events, 46.3 us)
Async XLA Ops:
  0.6 8.5 %collective-permute-start = (bf16[128,128]{1,0:T(8,128)(2,1)}, bf16[128,128]{1,0:T(8,128)(2,1)S(1)}, u32[]{:S(2)}, u32[]{:S(2)}) collective-permute-start(bf16[128,128]{1,0:T(8,128)(2,1)} %param.7), channel_id=1, source_target_pairs={{0,1},{1,0},{2,3},{3,2},{4,5},{5,4},{6,7},{7,6},{8,9},{9,8},{10,11... | collective-permute-start | bytes 98312 | tf_op jit(solution)/shard_map/ppermute | solution.py:15
  11.5 6.2 %collective-permute-start.10 = (bf16[128,256]{1,0:T(8,128)(2,1)S(1)}, bf16[128,256]{1,0:T(8,128)(2,1)S(1)}, u32[]{:S(2)}, u32[]{:S(2)}) collective-permute-start(bf16[128,256]{1,0:T(8,128)(2,1)S(1)} %pad_maximum_fusion.3), channel_id=1, source_target_pairs={{0,192},{64,128},{128,64},{192,0},{1,193},{65,129},{129,65},{193,1... | collective-permute-start | bytes 196616 | tf_op jit(solution)/shard_map/ppermute | solution.py:15
  13.4 5.3 %collective-permute-start.11 = (bf16[128,256]{1,0:T(8,128)(2,1)S(1)}, bf16[128,256]{1,0:T(8,128)(2,1)S(1)}, u32[]{:S(2)}, u32[]{:S(2)}) collective-permute-start(bf16[128,256]{1,0:T(8,128)(2,1)S(1)} %pad_maximum_fusion.3), channel_id=1, source_target_pairs={{0,128},{64,192},{128,0},{192,64},{1,129},{65,193},{129,1},{193,65... | collective-permute-start | bytes 196616 | tf_op jit(solution)/shard_map/ppermute | solution.py:15
  21.3 59.8 %all-to-all-start = ((bf16[16,512,256]{2,1,0:T(8,128)(2,1)}), bf16[16,512,256]{2,1,0:T(8,128)(2,1)}, u32[]{:S(2)}, u32[]{:S(2)}) async-start(bf16[16,512,256]{2,1,0:T(8,128)(2,1)} %broadcast_in_dim.6), calls=%async_computation | async-start | bytes 8388608 | tf_op jit(solution)/shard_map/all_to_all | solution.py:269
  28.8 22.0 %collective-permute-start.2 = (bf16[512,512]{1,0:T(8,128)(2,1)S(1)}, bf16[512,512]{1,0:T(8,128)(2,1)S(1)}, u32[]{:S(2)}, u32[]{:S(2)}) collective-permute-start(bf16[512,512]{1,0:T(8,128)(2,1)S(1)} %get-tuple-element.27), channel_id=1, source_target_pairs={{0,64},{64,0},{128,192},{192,128},{1,65},{65,1},{129,193},{193,129... | collective-permute-start | bytes 1572872 | tf_op jit(solution)/shard_map/ppermute | solution.py:15
  30.7 35.5 %collective-permute-start.4 = (bf16[512,512]{1,0:T(8,128)(2,1)S(1)}, bf16[512,512]{1,0:T(8,128)(2,1)S(1)}, u32[]{:S(2)}, u32[]{:S(2)}) collective-permute-start(bf16[512,512]{1,0:T(8,128)(2,1)S(1)} %get-tuple-element.29), channel_id=1, source_target_pairs={{0,128},{64,192},{128,0},{192,64},{1,129},{65,193},{129,1},{193,65... | collective-permute-start | bytes 1572872 | tf_op jit(solution)/shard_map/ppermute | solution.py:15
  31.4 44.5 %collective-permute-start.5 = (bf16[512,512]{1,0:T(8,128)(2,1)S(1)}, bf16[512,512]{1,0:T(8,128)(2,1)S(1)}, u32[]{:S(2)}, u32[]{:S(2)}) collective-permute-start(bf16[512,512]{1,0:T(8,128)(2,1)S(1)} %get-tuple-element.30), channel_id=1, source_target_pairs={{0,192},{64,128},{128,64},{192,0},{1,193},{65,129},{129,65},{193,1... | collective-permute-start | bytes 1572872 | tf_op jit(solution)/shard_map/ppermute | solution.py:15
  32.4 44.3 %collective-permute-start.6 = (bf16[512,512]{1,0:T(8,128)(2,1)S(1)}, bf16[512,512]{1,0:T(8,128)(2,1)S(1)}, u32[]{:S(2)}, u32[]{:S(2)}) collective-permute-start(bf16[512,512]{1,0:T(8,128)(2,1)S(1)} %get-tuple-element.76.refs_0_), channel_id=1, source_target_pairs={{0,32},{32,0},{1,33},{33,1},{2,34},{34,2},{3,35},{35,3},{4,36},{36... | collective-permute-start | bytes 1572872 | tf_op jit(solution)/shard_map/ppermute | solution.py:15
  50.8 27.8 %collective-permute-start.7 = (bf16[512,512]{1,0:T(8,128)(2,1)S(1)}, bf16[512,512]{1,0:T(8,128)(2,1)S(1)}, u32[]{:S(2)}, u32[]{:S(2)}) collective-permute-start(bf16[512,512]{1,0:T(8,128)(2,1)S(1)} %collective-permute-done.2.refs_1_), channel_id=1, source_target_pairs={{0,32},{32,0},{1,33},{33,1},{2,34},{34,2},{3,35},{35,3},{4,36},{36... | collective-permute-start | bytes 1572872 | tf_op jit(solution)/shard_map/ppermute | solution.py:15
  66.2 14.0 %collective-permute-start.8 = (bf16[512,512]{1,0:T(8,128)(2,1)S(1)}, bf16[512,512]{1,0:T(8,128)(2,1)S(1)}, u32[]{:S(2)}, u32[]{:S(2)}) collective-permute-start(bf16[512,512]{1,0:T(8,128)(2,1)S(1)} %collective-permute-done.4.refs_2_), channel_id=1, source_target_pairs={{0,32},{32,0},{1,33},{33,1},{2,34},{34,2},{3,35},{35,3},{4,36},{36... | collective-permute-start | bytes 1572872 | tf_op jit(solution)/shard_map/ppermute | solution.py:15
  76.7 10.6 %collective-permute-start.12 = (bf16[144,512]{1,0:T(8,128)(2,1)S(1)}, bf16[144,512]{1,0:T(8,128)(2,1)S(1)}, u32[]{:S(2)}, u32[]{:S(2)}) collective-permute-start(bf16[144,512]{1,0:T(8,128)(2,1)S(1)} %get-tuple-element.33), channel_id=1, source_target_pairs={{0,64},{64,0},{128,192},{192,128},{1,65},{65,1},{129,193},{193,129... | collective-permute-start | bytes 442376 | tf_op jit(solution)/shard_map/ppermute | solution.py:15
  76.7 12.5 %collective-permute-start.13 = (bf16[144,512]{1,0:T(8,128)(2,1)S(1)}, bf16[144,512]{1,0:T(8,128)(2,1)S(1)}, u32[]{:S(2)}, u32[]{:S(2)}) collective-permute-start(bf16[144,512]{1,0:T(8,128)(2,1)S(1)} %get-tuple-element.34), channel_id=1, source_target_pairs={{0,128},{64,192},{128,0},{192,64},{1,129},{65,193},{129,1},{193,65... | collective-permute-start | bytes 442376 | tf_op jit(solution)/shard_map/ppermute | solution.py:15
  78.6 14.4 %collective-permute-start.14 = (bf16[144,512]{1,0:T(8,128)(2,1)S(1)}, bf16[144,512]{1,0:T(8,128)(2,1)S(1)}, u32[]{:S(2)}, u32[]{:S(2)}) collective-permute-start(bf16[144,512]{1,0:T(8,128)(2,1)S(1)} %get-tuple-element.35), channel_id=1, source_target_pairs={{0,192},{64,128},{128,64},{192,0},{1,193},{65,129},{129,65},{193,1... | collective-permute-start | bytes 442376 | tf_op jit(solution)/shard_map/ppermute | solution.py:15
  116.7 37.2 %collective-permute-start.3 = (bf16[512,2048]{1,0:T(8,128)(2,1)}, bf16[512,2048]{1,0:T(8,128)(2,1)S(1)}, u32[]{:S(2)}, u32[]{:S(2)}) collective-permute-start(bf16[512,2048]{1,0:T(8,128)(2,1)} %refs_0_.1), channel_id=1, source_target_pairs={{0,32},{32,0},{1,33},{33,1},{2,34},{34,2},{3,35},{35,3},{4,36},{36... | collective-permute-start | bytes 6291464 | tf_op jit(solution)/shard_map/ppermute | solution.py:15
  118.9 7.7 %collective-permute-start.25 = (f32[8,512]{1,0:T(8,128)S(1)}, f32[8,512]{1,0:T(8,128)S(1)}, u32[]{:S(2)}, u32[]{:S(2)}) collective-permute-start(f32[8,512]{1,0:T(8,128)S(1)} %pad_maximum_fusion.7), channel_id=1, source_target_pairs={{0,1},{1,0},{2,3},{3,2},{4,5},{5,4},{6,7},{7,6},{8,9},{9,8},{10,11... | collective-permute-start | bytes 49160 | tf_op jit(solution)/shard_map/ppermute | solution.py:15
  127.1 26.8 %collective-permute-start.26 = (bf16[512,512]{1,0:T(8,128)(2,1)S(1)}, bf16[512,512]{1,0:T(8,128)(2,1)S(1)}, u32[]{:S(2)}, u32[]{:S(2)}) collective-permute-start(bf16[512,512]{1,0:T(8,128)(2,1)S(1)} %subtract_convert_fusion.refs_2_), channel_id=1, source_target_pairs={{0,64},{64,0},{128,192},{192,128},{1,65},{65,1},{129,193},{193,129... | collective-permute-start | bytes 1572872 | tf_op jit(solution)/shard_map/ppermute | solution.py:15
  128.9 19.4 %collective-permute-start.27 = (bf16[256,512]{1,0:T(8,128)(2,1)S(1)}, bf16[256,512]{1,0:T(8,128)(2,1)S(1)}, u32[]{:S(2)}, u32[]{:S(2)}) collective-permute-start(bf16[256,512]{1,0:T(8,128)(2,1)S(1)} %get-tuple-element.83), channel_id=1, source_target_pairs={{0,128},{64,192},{128,0},{192,64},{1,129},{65,193},{129,1},{193,65... | collective-permute-start | bytes 786440 | tf_op jit(solution)/shard_map/ppermute | solution.py:15
  129.9 24.0 %collective-permute-start.28 = (bf16[256,512]{1,0:T(8,128)(2,1)S(1)}, bf16[256,512]{1,0:T(8,128)(2,1)S(1)}, u32[]{:S(2)}, u32[]{:S(2)}) collective-permute-start(bf16[256,512]{1,0:T(8,128)(2,1)S(1)} %get-tuple-element.82), channel_id=1, source_target_pairs={{0,128},{64,192},{128,0},{192,64},{1,129},{65,193},{129,1},{193,65... | collective-permute-start | bytes 786440 | tf_op jit(solution)/shard_map/ppermute | solution.py:15
  148.3 9.8 %collective-permute-start.29 = (bf16[256,512]{1,0:T(8,128)(2,1)S(1)}, bf16[256,512]{1,0:T(8,128)(2,1)S(1)}, u32[]{:S(2)}, u32[]{:S(2)}) collective-permute-start(bf16[256,512]{1,0:T(8,128)(2,1)S(1)} %collective-permute-done.27.refs_4_), channel_id=1, source_target_pairs={{0,64},{64,0},{128,192},{192,128},{1,65},{65,1},{129,193},{193,129... | collective-permute-start | bytes 786440 | tf_op jit(solution)/shard_map/ppermute | solution.py:15
  153.9 7.0 %collective-permute-start.30 = (bf16[256,512]{1,0:T(8,128)(2,1)S(1)}, bf16[256,512]{1,0:T(8,128)(2,1)S(1)}, u32[]{:S(2)}, u32[]{:S(2)}) collective-permute-start(bf16[256,512]{1,0:T(8,128)(2,1)S(1)} %collective-permute-done.28.refs_5_), channel_id=1, source_target_pairs={{0,64},{64,0},{128,192},{192,128},{1,65},{65,1},{129,193},{193,129... | collective-permute-start | bytes 786440 | tf_op jit(solution)/shard_map/ppermute | solution.py:15
  167.7 7.8 %collective-permute-start.31 = (f32[4,64,256]{2,1,0:T(8,128)}, f32[4,64,256]{2,1,0:T(8,128)S(1)}, u32[]{:S(2)}, u32[]{:S(2)}) collective-permute-start(f32[4,64,256]{2,1,0:T(8,128)} %get-tuple-element.45), channel_id=1, source_target_pairs={{0,8},{8,0},{16,24},{24,16},{1,9},{9,1},{17,25},{25,17},{2,10},{10... | collective-permute-start | bytes 786440 | tf_op jit(solution)/shard_map/ppermute | solution.py:15
  168.1 11.2 %collective-permute-start.32 = (f32[4,64,256]{2,1,0:T(8,128)}, f32[4,64,256]{2,1,0:T(8,128)S(1)}, u32[]{:S(2)}, u32[]{:S(2)}) collective-permute-start(f32[4,64,256]{2,1,0:T(8,128)} %get-tuple-element.46), channel_id=1, source_target_pairs={{0,16},{8,24},{16,0},{24,8},{1,17},{9,25},{17,1},{25,9},{2,18},{10... | collective-permute-start | bytes 786440 | tf_op jit(solution)/shard_map/ppermute | solution.py:15
  170.7 11.2 %collective-permute-start.33 = (f32[4,64,256]{2,1,0:T(8,128)}, f32[4,64,256]{2,1,0:T(8,128)S(1)}, u32[]{:S(2)}, u32[]{:S(2)}) collective-permute-start(f32[4,64,256]{2,1,0:T(8,128)} %get-tuple-element.47), channel_id=1, source_target_pairs={{0,24},{8,16},{16,8},{24,0},{1,25},{9,17},{17,9},{25,1},{2,26},{10... | collective-permute-start | bytes 786440 | tf_op jit(solution)/shard_map/ppermute | solution.py:15
  172.5 13.3 %collective-permute-start.37 = (f32[4,64,256]{2,1,0:T(8,128)}, f32[4,64,256]{2,1,0:T(8,128)S(1)}, u32[]{:S(2)}, u32[]{:S(2)}) collective-permute-start(f32[4,64,256]{2,1,0:T(8,128)} %get-tuple-element.49), channel_id=1, source_target_pairs={{0,2},{2,0},{4,6},{6,4},{1,3},{3,1},{5,7},{7,5},{8,10},{10,8},{12,... | collective-permute-start | bytes 786440 | tf_op jit(solution)/shard_map/ppermute | solution.py:15
  172.8 14.9 %collective-permute-start.38 = (f32[4,64,256]{2,1,0:T(8,128)}, f32[4,64,256]{2,1,0:T(8,128)S(1)}, u32[]{:S(2)}, u32[]{:S(2)}) collective-permute-start(f32[4,64,256]{2,1,0:T(8,128)} %get-tuple-element.50), channel_id=1, source_target_pairs={{0,4},{2,6},{4,0},{6,2},{1,5},{3,7},{5,1},{7,3},{8,12},{10,14},{12... | collective-permute-start | bytes 786440 | tf_op jit(solution)/shard_map/ppermute | solution.py:15
  175.6 12.1 %collective-permute-start.39 = (f32[4,64,256]{2,1,0:T(8,128)}, f32[4,64,256]{2,1,0:T(8,128)S(1)}, u32[]{:S(2)}, u32[]{:S(2)}) collective-permute-start(f32[4,64,256]{2,1,0:T(8,128)} %get-tuple-element.51), channel_id=1, source_target_pairs={{0,6},{2,4},{4,2},{6,0},{1,7},{3,5},{5,3},{7,1},{8,14},{10,12},{12... | collective-permute-start | bytes 786440 | tf_op jit(solution)/shard_map/ppermute | solution.py:15
  182.9 8.3 %collective-permute-start.34 = (f32[64,256]{1,0:T(8,128)S(1)}, f32[64,256]{1,0:T(8,128)S(1)}, u32[]{:S(2)}, u32[]{:S(2)}) collective-permute-start(f32[64,256]{1,0:T(8,128)S(1)} %get-tuple-element.86), channel_id=1, source_target_pairs={{0,2},{2,0},{4,6},{6,4},{1,3},{3,1},{5,7},{7,5},{8,10},{10,8},{12,... | collective-permute-start | bytes 196616 | tf_op jit(solution)/shard_map/ppermute | solution.py:15
  183.2 9.4 %collective-permute-start.35 = (f32[64,256]{1,0:T(8,128)S(1)}, f32[64,256]{1,0:T(8,128)S(1)}, u32[]{:S(2)}, u32[]{:S(2)}) collective-permute-start(f32[64,256]{1,0:T(8,128)S(1)} %get-tuple-element.85), channel_id=1, source_target_pairs={{0,4},{2,6},{4,0},{6,2},{1,5},{3,7},{5,1},{7,3},{8,12},{10,14},{12... | collective-permute-start | bytes 196616 | tf_op jit(solution)/shard_map/ppermute | solution.py:15
  185.9 6.7 %collective-permute-start.36 = (f32[64,256]{1,0:T(8,128)S(1)}, f32[64,256]{1,0:T(8,128)S(1)}, u32[]{:S(2)}, u32[]{:S(2)}) collective-permute-start(f32[64,256]{1,0:T(8,128)S(1)} %get-tuple-element.84), channel_id=1, source_target_pairs={{0,6},{2,4},{4,2},{6,0},{1,7},{3,5},{5,3},{7,1},{8,14},{10,12},{12... | collective-permute-start | bytes 196616 | tf_op jit(solution)/shard_map/ppermute | solution.py:15
  187.9 6.2 %collective-permute-start.41 = (f32[64,256]{1,0:T(8,128)S(1)}, f32[64,256]{1,0:T(8,128)S(1)}, u32[]{:S(2)}, u32[]{:S(2)}) collective-permute-start(f32[64,256]{1,0:T(8,128)S(1)} %get-tuple-element.88), channel_id=1, source_target_pairs={{0,16},{8,24},{16,0},{24,8},{1,17},{9,25},{17,1},{25,9},{2,18},{10... | collective-permute-start | bytes 196616 | tf_op jit(solution)/shard_map/ppermute | solution.py:15
  191.2 5.5 %collective-permute-start.42 = (f32[64,256]{1,0:T(8,128)S(1)}, f32[64,256]{1,0:T(8,128)S(1)}, u32[]{:S(2)}, u32[]{:S(2)}) collective-permute-start(f32[64,256]{1,0:T(8,128)S(1)} %get-tuple-element.87), channel_id=1, source_target_pairs={{0,24},{8,16},{16,8},{24,0},{1,25},{9,17},{17,9},{25,1},{2,26},{10... | collective-permute-start | bytes 196616 | tf_op jit(solution)/shard_map/ppermute | solution.py:15
  196.7 8.3 %collective-permute-start.43 = (f32[2,16,512]{2,1,0:T(8,128)S(1)}, f32[2,16,512]{2,1,0:T(8,128)S(1)}, u32[]{:S(2)}, u32[]{:S(2)}) collective-permute-start(f32[2,16,512]{2,1,0:T(8,128)S(1)} %select_bitcast_fusion), channel_id=1, source_target_pairs={{0,1},{1,0},{2,3},{3,2},{4,5},{5,4},{6,7},{7,6},{8,9},{9,8},{10,11... | collective-permute-start | bytes 196616 | tf_op jit(solution)/shard_map/ppermute | solution.py:15
  (35 other events, 305.5 us)
